TPU v7x, 128 devices: a whole 4x4x4 slice. The times are simulated.
128 devices in a mesh: fsdp: 8 (over y, x_lo), tensor: 16 (over x_hi, z, core).
Axes of the slice: x: 4 (x_hi: 2, x_lo: 2; x = x_hi * 2 + x_lo), y: 4, z: 4, core: 2. Of those that a mesh axis runs over, the one named last changes fastest.
Arguments:
- prompt: bfloat16 [1024, 16384], P('tensor', 'fsdp'), may hold values from -6 to 6
- decode_in: bfloat16 [128, 16384], P('tensor', 'fsdp'), may hold values from -6 to 6
- gate_weight: bfloat16 [16384, 26624], P(('fsdp', 'tensor')), may hold values from -0.046875 to 0.046875
- up_weight: bfloat16 [16384, 26624], P(('fsdp', 'tensor')), may hold values from -0.046875 to 0.046875
- down_weight: bfloat16 [26624, 16384], P(None, ('fsdp', 'tensor')), may hold values from -0.0390625 to 0.0390625
Outputs:
- prompt_out: bfloat16 [1024, 16384], P('tensor', 'fsdp')
- decoded: bfloat16 [128, 16384], P('tensor', 'fsdp')
All inputs are finite; a program needn't handle non-finite values.
Results may differ from a plain program's by a relative error of at most 0.019.
Values may be sent and summed in bfloat16 or wider, within the bound.
No kernel may reach another device: no remote copies, remote signals or barrier semaphores. Data moves between devices by JAX's collectives and lax.ppermute only.
A program may use at most 192 MiB of HBM per device.

v0:
```python
import jax
import jax.numpy as jnp
from jax import lax
from jax.sharding import PartitionSpec as P

STEPS = 2


def down_term(hidden, down_slice):
    return jnp.dot(hidden, down_slice, preferred_element_type=jnp.float32)


def gated(gate_sum, up_sum):
    return (jax.nn.silu(gate_sum) * up_sum).astype(jnp.bfloat16)


def shards(prompt, decode_in, gate_weight, up_weight, down_weight):
    parts = lax.axis_size("tensor")
    width = gate_weight.shape[1]
    per_device = width // parts
    groups = per_device // 128
    local_rows = gate_weight.shape[0]
    gate_grouped = gate_weight.reshape(local_rows, groups, width // groups)
    up_grouped = up_weight.reshape(local_rows, groups, width // groups)
    gathered = lax.all_gather(prompt, "tensor", axis=0, tiled=True)
    gate_slice, up_slice = (
        lax.all_to_all(gate_grouped, "tensor", split_axis=2, concat_axis=0, tiled=True),
        lax.all_to_all(up_grouped, "tensor", split_axis=2, concat_axis=0, tiled=True),
    )
    gate_slice = gate_slice.reshape(gate_slice.shape[0], -1)
    up_slice = up_slice.reshape(up_slice.shape[0], -1)
    gate_part = jnp.dot(gathered, gate_slice, preferred_element_type=jnp.float32)
    up_part = jnp.dot(gathered, up_slice, preferred_element_type=jnp.float32)
    down_grouped = down_weight.reshape(groups, width // groups, down_weight.shape[1])
    down_slice = lax.all_to_all(down_grouped, "tensor", split_axis=1, concat_axis=2, tiled=True)
    down_slice = down_slice.reshape(-1, down_slice.shape[2])
    gate_share, up_share = (
        lax.psum_scatter(gate_part, "fsdp", scatter_dimension=0, tiled=True),
        lax.psum_scatter(up_part, "fsdp", scatter_dimension=0, tiled=True),
    )
    hidden = lax.all_gather(gated(gate_share, up_share), "fsdp", axis=0, tiled=True)
    prompt_out = lax.psum_scatter(
        down_term(hidden, down_slice).astype(jnp.bfloat16),
        "tensor",
        scatter_dimension=0,
        tiled=True,
    )
    state = decode_in
    for turn in range(STEPS):
        rows_all = lax.all_gather(state, "tensor", axis=0, tiled=True)
        gate_step = jnp.dot(rows_all, gate_slice, preferred_element_type=jnp.float32)
        up_step = jnp.dot(rows_all, up_slice, preferred_element_type=jnp.float32)
        gate_full, up_full = lax.psum((gate_step, up_step), "fsdp")
        hidden_step = gated(gate_full, up_full)
        update = lax.psum_scatter(
            down_term(hidden_step, down_slice), "tensor", scatter_dimension=0, tiled=True
        )
        state = (state.astype(jnp.float32) + update).astype(jnp.bfloat16)
    return (prompt_out, state)


def solution(mesh):
    return jax.shard_map(
        shards,
        mesh=mesh,
        in_specs=(
            P("tensor", "fsdp"),
            P("tensor", "fsdp"),
            P(("fsdp", "tensor"), None),
            P(("fsdp", "tensor"), None),
            P(None, ("fsdp", "tensor")),
        ),
        out_specs=(P("tensor", "fsdp"), P("tensor", "fsdp")),
        check_vma=False,
    )
```

profile of v0, /device:TPU:1, one launch (start us, length us, event | category | flops | bytes accessed | tf_op | source)
XLA Modules:
  0.0 1120.3 jit_solution(3397916809330797872)
XLA Ops:
  8.0 9.9 copy.26
  17.9 9.5 copy.27
  27.4 9.3 all-to-all-start
  36.6 9.7 copy.30
  46.3 9.4 copy.31
  55.7 0.0 copy-start.2
  55.7 100.3 %all-to-all-done = bf16[128,13,2048]{0,1,2:T(8,128)(2,1)} async-done(((bf16[128,13,2048]{0,1,2:T(8,128)(2,1)}), bf16[128,13,2048]{0,1,2:T(8,128)(2,1)}, u32[]{:S(2)}, u32[]{:S(2)}) %all-to-all-start) | async-done | bytes 6815776 | tf_op jit(solution)/shard_map/all_to_all | solution.py:27
  156.1 14.9 %all-to-all-start.1 = ((bf16[128,13,2048]{0,1,2:T(8,128)(2,1)}), bf16[128,13,2048]{0,1,2:T(8,128)(2,1)}, u32[]{:S(2)}, u32[]{:S(2)}) async-start(bf16[128,13,2048]{0,1,2:T(8,128)(2,1)} %copy.31), calls=%async_computation.2 | async-start | bytes 16777216 | tf_op jit(solution)/shard_map/all_to_all | solution.py:28
  171.0 0.0 all-reduce.7.cloned.1.call-start
  171.0 0.0 copy-done.2
  171.0 142.5 %all_gather.14 = bf16[128,2048]{1,0:T(8,128)(2,1)S(1)} all-gather(bf16[8,2048]{1,0:T(8,128)(2,1)S(1)} %copy-done.2), channel_id=1, replica_groups=mesh['fsdp'=8,'tensor'=16] {'tensor'}, dimensions={0}, use_global_device_ids=true | all-gather | bytes 557056 | tf_op jit(solution)/shard_map/all_gather | solution.py:50
  313.5 10.9 copy.29
  324.4 0.0 all-to-all-done.1
  324.4 0.0 copy-start
  324.4 11.1 copy.33
  335.5 0.0 copy-start.1
  335.5 0.0 copy-done
  335.5 3.3 fusion.14
  338.8 0.0 copy-done.1
  338.8 3.5 fusion.8
  342.2 0.0 all-reduce.7.cloned.1.call-update
  342.3 0.0 all-gather.3.cloned.1.call-start
  342.3 0.5 all-gather.3.cloned.1.call-update
  342.8 0.0 reduce-scatter.12.cloned.1.call-start
  342.9 7.3 copy.34
  350.2 171.5 %all_to_all.45 = bf16[13,2048,128]{2,0,1:T(8,128)(2,1)S(1)} all-to-all(bf16[13,2048,128]{2,0,1:T(8,128)(2,1)S(1)} %copy.34), channel_id=1, replica_groups=mesh['fsdp'=8,'tensor'=16] {'tensor'}, dimensions={1} | all-to-all | bytes 13631488 | tf_op jit(solution)/shard_map/all_to_all | solution.py:35
  521.6 7.5 copy.36
  529.1 0.0 all-reduce.7.cloned.1.call-done
  529.1 5.8 fusion.2
  534.9 0.0 reduce-scatter.12.cloned.1.call-update
  535.0 0.3 reduce-scatter.6.cloned.1.call-start
  535.2 0.0 all-gather.3.cloned.1.call-done
  535.3 13.3 %fusion.16 = f32[1024,1664]{1,0:T(8,128)} fusion(bf16[1024,2048]{1,0:T(8,128)(2,1)} %all-gather.3.cloned.1.call-done, bf16[208,8,16,128]{3,2,1,0:T(8,128)(2,1)} %bitcast.59), kind=kOutput, calls=%fused_computation.16 | convolution fusion | flops 6979321856 | bytes 17825792 | tf_op jit(solution)/shard_map/dot_general | solution.py:32
  548.6 0.0 reduce-scatter.6.cloned.1.call-update
  548.6 0.0 reduce-scatter.8.cloned.1.call-start
  548.7 13.5 %fusion.10 = f32[1024,1664]{1,0:T(8,128)} fusion(bf16[1024,2048]{1,0:T(8,128)(2,1)} %all-gather.3.cloned.1.call-done, bf16[208,8,16,128]{3,2,1,0:T(8,128)(2,1)} %bitcast.62), kind=kOutput, calls=%fused_computation.10 | convolution fusion | flops 6979321856 | bytes 17825792 | tf_op jit(solution)/shard_map/dot_general | solution.py:33
  562.2 0.0 slice-start
  562.2 0.0 reduce-scatter.8.cloned.1.call-update
  562.2 0.0 all-reduce.5.cloned.1.call-start
  562.3 35.2 %reduce-scatter.12.cloned.1.call-done = f32[8,2048]{1,0:T(8,128)} async-done(((f32[128,2048]{1,0:T(8,128)}), f32[8,2048]{1,0:T(8,128)}) %reduce-scatter.12.cloned.1.call-update) | async-done | bytes 65552 | tf_op jit(solution)/shard_map/reduce_scatter | solution.py:55
  597.5 0.8 add_convert_fusion.1
  598.4 26.6 %all_gather.15 = bf16[128,2048]{1,0:T(8,128)(2,1)S(1)} all-gather(bf16[8,2048]{1,0:T(8,128)(2,1)S(1)} %add_convert_fusion.1), channel_id=1, replica_groups=mesh['fsdp'=8,'tensor'=16] {'tensor'}, dimensions={0}, use_global_device_ids=true | all-gather | bytes 557056 | tf_op jit(solution)/shard_map/all_gather | solution.py:50
  625.0 0.0 slice-start.1
  625.0 6.4 fusion.12
  631.4 0.0 slice-done
  631.4 0.0 slice-done.1
  631.4 3.3 fusion.6
  634.7 0.0 all-reduce.5.cloned.1.call-update
  634.7 0.0 all-gather.5.cloned.1.call-start
  634.8 129.3 %reduce-scatter.6.cloned.1.call-done = f32[128,1664]{1,0:T(8,128)} async-done(((f32[1024,1664]{1,0:T(8,128)}), f32[128,1664]{1,0:T(8,128)}) %reduce-scatter.6.cloned.1.call-update) | async-done | bytes 851984 | tf_op jit(solution)/shard_map/reduce_scatter | solution.py:38
  764.1 171.5 %reduce-scatter.8.cloned.1.call-done = f32[128,1664]{1,0:T(8,128)} async-done(((f32[1024,1664]{1,0:T(8,128)}), f32[128,1664]{1,0:T(8,128)}) %reduce-scatter.8.cloned.1.call-update) | async-done | bytes 851984 | tf_op jit(solution)/shard_map/reduce_scatter | solution.py:39
  935.6 2.4 multiply_convert_fusion.2
  938.0 0.0 all-gather.5.cloned.1.call-update
  938.0 0.3 reduce-scatter.14.cloned.1.call-start
  938.3 1.8 all-reduce.5.cloned.1.call-done
  940.2 5.8 fusion
  946.0 0.0 reduce-scatter.14.cloned.1.call-update
  946.1 0.0 reduce-scatter.10.cloned.1.call-start
  946.1 75.1 %all-gather.5.cloned.1.call-done = bf16[1024,1664]{1,0:T(8,128)(2,1)} async-done(((bf16[128,1664]{1,0:T(8,128)(2,1)}), bf16[1024,1664]{1,0:T(8,128)(2,1)}) %all-gather.5.cloned.1.call-update) | async-done | bytes 3407888 | tf_op jit(solution)/shard_map/all_gather | solution.py:41
  1021.2 12.5 %fusion.27 = bf16[1024,2048]{1,0:T(8,128)(2,1)} fusion(bf16[1024,1664]{1,0:T(8,128)(2,1)} %all-gather.5.cloned.1.call-done, bf16[208,8,16,128]{3,2,1,0:T(8,128)(2,1)} %bitcast.58), kind=kOutput, calls=%fused_computation.27 | convolution fusion | flops 6981419008 | bytes 14417920 | tf_op jit(solution)/shard_map/dot_general | solution.py:10
  1033.7 0.0 reduce-scatter.10.cloned.1.call-update
  1033.7 0.0 reduce-scatter.14.cloned.1.call-done
  1033.7 1.5 add_convert_fusion
  1035.2 77.7 %reduce-scatter.10.cloned.1.call-done = bf16[64,2048]{1,0:T(8,128)(2,1)} async-done(((bf16[1024,2048]{1,0:T(8,128)(2,1)}), bf16[64,2048]{1,0:T(8,128)(2,1)}) %reduce-scatter.10.cloned.1.call-update) | async-done | bytes 262160 | tf_op jit(solution)/shard_map/reduce_scatter | solution.py:42
  (1 shorter events, 0.0 us)
Async XLA Ops:
  27.4 128.7 %all-to-all-start = ((bf16[128,13,2048]{0,1,2:T(8,128)(2,1)}), bf16[128,13,2048]{0,1,2:T(8,128)(2,1)}, u32[]{:S(2)}, u32[]{:S(2)}) async-start(bf16[128,13,2048]{0,1,2:T(8,128)(2,1)} %copy.27), calls=%async_computation | async-start | bytes 16777216 | tf_op jit(solution)/shard_map/all_to_all | solution.py:27
  55.7 115.3 %copy-start.2 = (bf16[8,2048]{1,0:T(8,128)(2,1)S(1)}, bf16[8,2048]{1,0:T(8,128)(2,1)}, u32[]{:S(2)}) copy-start(bf16[8,2048]{1,0:T(8,128)(2,1)} %param.6) | copy-start | bytes 98308
  156.1 168.4 %all-to-all-start.1 = ((bf16[128,13,2048]{0,1,2:T(8,128)(2,1)}), bf16[128,13,2048]{0,1,2:T(8,128)(2,1)}, u32[]{:S(2)}, u32[]{:S(2)}) async-start(bf16[128,13,2048]{0,1,2:T(8,128)(2,1)} %copy.31), calls=%async_computation.2 | async-start | bytes 16777216 | tf_op jit(solution)/shard_map/all_to_all | solution.py:28
  171.0 358.2 %all-reduce.7.cloned.1.call-start = ((), (), s32[]{:S(2)}) async-start(), calls=%async_computation.16 | async-start | bytes 3407872 | tf_op jit(solution)/shard_map/psum | solution.py:53
  324.4 11.1 copy-start
  335.5 3.3 copy-start.1
  342.3 193.0 %all-gather.3.cloned.1.call-start = ((), (), s32[]{:S(2)}) async-start(), calls=%async_computation.8 | async-start | bytes 4456448 | tf_op jit(solution)/shard_map/all_gather | solution.py:25
  342.8 254.7 %reduce-scatter.12.cloned.1.call-start = ((), (), s32[]{:S(2)}) async-start(), calls=%async_computation.13 | async-start | bytes 1114112 | tf_op jit(solution)/shard_map/reduce_scatter | solution.py:55
  535.0 229.1 %reduce-scatter.6.cloned.1.call-start = ((), (), s32[]{:S(2)}) async-start(), calls=%async_computation.9 | async-start | bytes 7667712 | tf_op jit(solution)/shard_map/reduce_scatter | solution.py:38
  548.6 387.0 %reduce-scatter.8.cloned.1.call-start = ((), (), s32[]{:S(2)}) async-start(), calls=%async_computation.10 | async-start | bytes 7667712 | tf_op jit(solution)/shard_map/reduce_scatter | solution.py:39
  562.2 69.2 %slice-start = ((s8[6815744]{0:T(1024)(128)(4,1)}), s8[2621440]{0:T(1024)(128)(4,1)S(1)}, s32[]{:S(2)}) async-start(s8[6815744]{0:T(1024)(128)(4,1)} %bitcast.64), calls=%async_computation.17 | async-start | bytes 5242880
  562.2 378.0 %all-reduce.5.cloned.1.call-start = ((), (), s32[]{:S(2)}) async-start(), calls=%async_computation.15 | async-start | bytes 3407872 | tf_op jit(solution)/shard_map/psum | solution.py:53
  625.0 6.4 slice-start.1
  634.7 386.5 %all-gather.5.cloned.1.call-start = ((), (), s32[]{:S(2)}) async-start(), calls=%async_computation.11 | async-start | bytes 3833856 | tf_op jit(solution)/shard_map/all_gather | solution.py:41
  938.0 95.7 %reduce-scatter.14.cloned.1.call-start = ((), (), s32[]{:S(2)}) async-start(), calls=%async_computation.14 | async-start | bytes 1114112 | tf_op jit(solution)/shard_map/reduce_scatter | solution.py:55
  946.1 166.8 %reduce-scatter.10.cloned.1.call-start = ((), (), s32[]{:S(2)}) async-start(), calls=%async_computation.12 | async-start | bytes 4456448 | tf_op jit(solution)/shard_map/reduce_scatter | solution.py:42
Sparse Core Ops, SparseCore 0:
  342.4 173.0 all-reduce.6
  634.9 305.2 all-reduce.4
  941.8 79.3 all-gather.4
Sparse Core Ops, SparseCore 1:
  345.2 87.5 all-gather.2
  535.0 62.4 reduce-scatter.11
  599.8 164.2 reduce-scatter.5
  766.5 169.0 reduce-scatter.7
  946.1 75.6 reduce-scatter.13
  1033.8 79.0 reduce-scatter.9
where the time goes:
time: 1130 us; the launch traced here: 1120 us
  waiting for transfers between devices  592 us (52%)
  blocking collectives  341 us (30%)
  local copies, waits for them, and re-layouts  75.2 us (7%)
  matrix products  67.4 us (6%)
  starting transfers between devices  25 us (2%)
  between operations  15.6 us (1%)
    reduce_scatter x1, waiting for transfers between devices, shards(): lax.psum_scatter(up_part, 'fsdp', scatter_dimension=0, tiled=True)  172 us
    all_to_all x1, blocking collectives, shards(): lax.all_to_all(down_grouped, 'tensor', split_axis=1, concat_axis=2, tiled...  171 us
    all_gather x2, blocking collectives, shards(): rows_all = lax.all_gather(state, 'tensor', axis=0, tiled=True)  169 us
    reduce_scatter x1, waiting for transfers between devices, shards(): lax.psum_scatter(gate_part, 'fsdp', scatter_dimension=0, tiled=True)  129 us
    all_to_all x1, waiting for transfers between devices, shards(): lax.all_to_all(gate_grouped, 'tensor', split_axis=2, concat_axis=0, tiled...  100 us
    reduce_scatter x1, waiting for transfers between devices, shards(): lax.psum_scatter(down_term(hidden, down_slice).astype(jnp.bfloat16), 'ten...  77.7 us
    all_gather x1, waiting for transfers between devices, shards(): lax.all_gather(gated(gate_share, up_share), 'fsdp', axis=0, tiled=True)  75.1 us
    reduce_scatter x2, waiting for transfers between devices, shards(): lax.psum_scatter(down_term(hidden_step, down_slice), 'tensor', scatter_di...  35.3 us
  transfers between devices with their start and end apart: 11, of which 7 were waited for; matrix products, arithmetic and copies ran while one was open for 10% of the time, Pallas kernels for 0%

commit v1 on v0

v1 whole, which is shorter than its diff:
```python
import jax
import jax.numpy as jnp
from jax import lax
from jax.experimental import pallas as pl
from jax.experimental.pallas import tpu as pltpu
from jax.sharding import Mesh, PartitionSpec as P

STEPS = 2
SHIFTS = (0, 1, -1, 2)
FLIP = (0, 2, 1, 3)
LANES = 128
VMEM_LIMIT = 60 * 1024 * 1024
PLAN = (("z", "x", "y"), ("x", "y", "z"), ("y", "z", "x"))
RINGS = {"x": ("xl", "xh"), "y": ("y",), "z": ("z",)}


def ring_index(ring, place, core):
    if ring == "x":
        place = (place % 2) * 2 + place // 2
    return place * 2 + core


def ring_permute(value, ring, slot):
    pairs = []
    for core, sign in ((0, 1), (1, -1)):
        for place in range(4):
            target = (place + sign * SHIFTS[slot]) % 4
            pairs.append((ring_index(ring, place, core), ring_index(ring, target, core)))
    return lax.ppermute(value, RINGS[ring] + ("c",), pairs)


def core_swap(value):
    return lax.ppermute(value, "c", [(0, 1), (1, 0)])


def params():
    return pltpu.CompilerParams(vmem_limit_bytes=VMEM_LIMIT)


def smem():
    return pl.BlockSpec(memory_space=pltpu.SMEM)


def vmem():
    return pl.BlockSpec(memory_space=pltpu.VMEM)


def copy_cost(nbytes):
    return pl.CostEstimate(flops=0, bytes_accessed=int(2 * nbytes), transcendentals=0)


def pack_gate_up(where, gate, up, begin, width):
    rows = gate.shape[0]
    base = begin // (2 * width)
    step = rows // 4

    def body(where_ref, *rest):
        ins, outs = rest[:8], rest[8:]
        core = where_ref[0]
        for slot in range(4):
            for at in range(2):
                source = ins[4 * at + slot]
                outs[slot][0, at] = source[:, pl.ds(pl.multiple_of(core * width, LANES), width)]
                outs[slot][1, at] = source[:, pl.ds(pl.multiple_of((1 - core) * width, LANES), width)]

    def columns(slot):
        return lambda at, where_ref: (at, base + where_ref[1 + slot])

    return pl.pallas_call(
        body,
        out_shape=[jax.ShapeDtypeStruct((2, 2, rows, width), gate.dtype)] * 4,
        grid_spec=pltpu.PrefetchScalarGridSpec(
            num_scalar_prefetch=1,
            grid=(rows // step,),
            in_specs=[pl.BlockSpec((step, 2 * width), columns(slot)) for slot in range(4)] * 2,
            out_specs=[pl.BlockSpec((2, 2, step, width), lambda at, where_ref: (0, 0, at, 0))] * 4,
        ),
        compiler_params=params(),
        cost_estimate=copy_cost(16 * rows * width * 2),
        name="pack_gate_up",
    )(where, *([gate] * 4), *([up] * 4))


def pack_down(where, down, begin, width):
    columns = down.shape[1]
    base = begin // width
    tile = tile_of(width)
    tiles = width // tile

    def body(where_ref, *rest):
        ins, outs = rest[:8], rest[8:]
        for slot in range(4):
            outs[slot][0] = ins[2 * slot][...]
            outs[slot][1] = ins[2 * slot + 1][...]

    def half(slot, other):
        def block(at, where_ref):
            core = 1 - where_ref[0] if other else where_ref[0]
            return ((base + 2 * where_ref[1 + slot] + core) * tiles + at, 0)

        return block

    return pl.pallas_call(
        body,
        out_shape=[jax.ShapeDtypeStruct((2, width, columns), down.dtype)] * 4,
        grid_spec=pltpu.PrefetchScalarGridSpec(
            num_scalar_prefetch=1,
            grid=(tiles,),
            in_specs=[
                pl.BlockSpec((tile, columns), half(slot, other)) for slot in range(4) for other in (False, True)
            ],
            out_specs=[pl.BlockSpec((2, tile, columns), lambda at, where_ref: (0, at, 0))] * 4,
        ),
        compiler_params=params(),
        cost_estimate=copy_cost(8 * width * columns * 2),
        name="pack_down",
    )(where, *([down] * 8))


def tile_of(width):
    return width // 3 if width % 384 == 0 else width // 2


def gate_up_products(part, where, mine, others, weights):
    own_weights, other_weights = weights
    rows, own = mine[0].shape
    width = other_weights.shape[3]
    quarter = rows // 4
    depth = 8 * own
    tile = tile_of(width)

    def body(where_ref, *rest):
        mine_refs, others_ref, weight_refs, other_ref = rest[:4], rest[4], rest[5:9], rest[9]
        outs, joined, sums = rest[10:14], rest[14], rest[15]

        @pl.when((pl.program_id(0) == 0) & (pl.program_id(1) == 0))
        def _():
            for slot in range(4):
                joined[:, own * slot : own * (slot + 1)] = mine_refs[slot][...]
                joined[:, own * (4 + slot) : own * (5 + slot)] = others_ref[slot]

        weight = jnp.concatenate([ref[0, 0] for ref in weight_refs] + [other_ref[slot, 0] for slot in range(4)], axis=0)
        product = jnp.dot(joined[...], weight, preferred_element_type=jnp.float32)
        sums[...] = product.reshape(4, quarter, tile)
        for slot in range(4):
            outs[slot][0] = sums[where_ref[5 + slot]].astype(jnp.bfloat16)

    return pl.pallas_call(
        body,
        grid=(2, width // tile),
        out_shape=[jax.ShapeDtypeStruct((2, quarter, width), jnp.bfloat16)] * 4,
        in_specs=[smem()]
        + [pl.BlockSpec((rows, own), lambda g, j: (0, 0))] * 4
        + [pl.BlockSpec((4, rows, own), lambda g, j: (part, 0, 0))]
        + [pl.BlockSpec((1, 1, own, tile), lambda g, j: (0, g, 0, j))] * 4
        + [pl.BlockSpec((4, 1, own, tile), lambda g, j: (0, g, 0, j))],
        out_specs=[pl.BlockSpec((1, quarter, tile), lambda g, j: (g, 0, j))] * 4,
        scratch_shapes=[
            pltpu.VMEM((rows, depth), jnp.bfloat16),
            pltpu.VMEM((4, quarter, tile), jnp.float32),
        ],
        compiler_params=params(),
        cost_estimate=pl.CostEstimate(
            flops=4 * rows * depth * width,
            bytes_accessed=2 * (rows * depth + 2 * depth * width + 2 * rows * width),
            transcendentals=0,
        ),
        name="gate_up_products",
    )(where, *mine, others, *own_weights, other_weights)


def first_sums(where, terms, kept):
    _, quarter, width = terms[0].shape
    block = quarter // 4
    tile = tile_of(width)

    def body(where_ref, *rest):
        ins, outs, sums = rest[:4], rest[4:8], rest[8]
        total = ins[0][0].astype(jnp.float32)
        for ref in ins[1:]:
            total = total + ref[0].astype(jnp.float32)
        sums[...] = total.reshape(4, block, tile)
        for slot in range(4):
            outs[slot][0] = sums[where_ref[9 + slot]].astype(kept)

    return pl.pallas_call(
        body,
        grid=(2, width // tile),
        out_shape=[jax.ShapeDtypeStruct((2, block, width), kept)] * 4,
        in_specs=[smem()] + [pl.BlockSpec((1, quarter, tile), lambda g, j: (g, 0, j))] * 4,
        out_specs=[pl.BlockSpec((1, block, tile), lambda g, j: (g, 0, j))] * 4,
        scratch_shapes=[pltpu.VMEM((4, block, tile), jnp.float32)],
        compiler_params=params(),
        cost_estimate=pl.CostEstimate(
            flops=8 * quarter * width, bytes_accessed=20 * quarter * width, transcendentals=0
        ),
        name="first_sums",
    )(where, *terms)


def down_products(where, hidden, weights):
    _, block, width = hidden[0].shape
    rows = 16 * block
    own_weights, other_weights = weights
    own = other_weights.shape[2]
    blocks = 16 if rows <= 256 else 4
    chunk = blocks * block
    held = jnp.bfloat16 if block % 16 == 0 else jnp.float32

    def body(where_ref, *rest):
        hidden_refs, weight_refs, theirs_ref = rest[:4], rest[4:8], rest[8]
        outs, other_ref, joined = rest[9:13], rest[13], rest[14]
        for first in range(4):
            for second in range(4):
                row = where_ref[13 + first] * 4 + where_ref[17 + second]
                joined[row] = hidden_refs[first][second].astype(held)

        def step(at, carry):
            value = joined[pl.ds(at * blocks, blocks)].reshape(chunk, width).astype(jnp.bfloat16)
            span = pl.ds(pl.multiple_of(at * chunk, chunk), chunk)
            for slot in range(4):
                weight = jnp.concatenate([weight_refs[slot][0], theirs_ref[slot]], axis=1)
                product = jnp.dot(value, weight, preferred_element_type=jnp.float32)
                product = product.astype(jnp.bfloat16)
                outs[FLIP[slot]][span, :] = product[:, :own]
                other_ref[FLIP[slot], span, :] = product[:, own:]
            return carry

        lax.fori_loop(0, rows // chunk, step, 0)

    result = pl.pallas_call(
        body,
        grid=(1,),
        out_shape=[jax.ShapeDtypeStruct((rows, own), jnp.bfloat16)] * 4
        + [jax.ShapeDtypeStruct((4, rows, own), jnp.bfloat16)],
        in_specs=[smem()]
        + [vmem()] * 4
        + [pl.BlockSpec((1, width, own), lambda at: (0, 0, 0))] * 4
        + [vmem()],
        out_specs=[vmem()] * 5,
        scratch_shapes=[pltpu.VMEM((16, block, width), held)],
        compiler_params=params(),
        cost_estimate=pl.CostEstimate(
            flops=16 * rows * width * own,
            bytes_accessed=2 * (rows * width + 8 * width * own + 8 * rows * own),
            transcendentals=0,
        ),
        name="down_products",
    )(where, *hidden, *own_weights, other_weights)
    return result[:4], result[4]


def exchange(values, ring):
    return [values[0]] + [ring_permute(values[slot], ring, slot) for slot in (1, 2, 3)]


def gated(gate_sum, up_sum):
    return (jax.nn.silu(gate_sum) * up_sum).astype(jnp.bfloat16)


def gather_rows(rows):
    mine = [[rows, None, None, None] for _ in PLAN]
    for slot in (1, 2, 3):
        for at, (cross, _, _) in enumerate(PLAN):
            mine[at][slot] = ring_permute(rows, cross, slot)
    return mine


def exchange_all(values, rings):
    result = [[value[0], None, None, None] for value in values]
    first = [ring_permute(value[1], ring, 1) for value, ring in zip(values, rings)]
    later = lax.optimization_barrier([value[1:] for value in values])
    second = [ring_permute(value[1], ring, 2) for value, ring in zip(later, rings)]
    third, first = lax.optimization_barrier(([value[2] for value in later], first))
    third = [ring_permute(value, ring, 3) for value, ring in zip(third, rings)]
    return [[value[0], *slots] for value, *slots in zip(values, first, second, third)]


def share_cores(received):
    return received, core_swap(jnp.stack([value[1] for value in received]))


def block_update(mine, others, wheres, gate_up, down):
    rows = mine[0][0].shape[0]
    kept = jnp.bfloat16 if rows >= 256 else jnp.float32
    cross, first, second = zip(*PLAN)
    parts = [
        gate_up_products(at, where, mine[at], others, weights)
        for at, (where, weights) in enumerate(zip(wheres, gate_up))
    ]
    parts = exchange_all(parts, first)
    sums = [first_sums(where, terms, kept) for where, terms in zip(wheres, parts)]
    sums = exchange_all(sums, second)
    hidden = []
    for terms in sums:
        both = sum(term.astype(jnp.float32) for term in terms)
        hidden.append(gated(both[0], both[1]))
    hidden = exchange_all([[value] * 4 for value in hidden], second)
    hidden = exchange_all([[jnp.stack(value)] * 4 for value in hidden], first)
    terms, sent = [], []
    for where, value, weights in zip(wheres, hidden, down):
        products, other = down_products(where, value, weights)
        other = core_swap(other)
        pairs = [
            product.astype(jnp.float32) + other[slot].astype(jnp.float32) for slot, product in enumerate(products)
        ]
        terms.append(pairs[0])
        sent.append([pairs[0]] + [pair.astype(jnp.bfloat16) for pair in pairs[1:]])
    for received in exchange_all(sent, cross):
        terms += [term.astype(jnp.float32) for term in received[1:]]
    return sum(terms[1:], terms[0])


def shards(prompt, decode_in, gate_weight, up_weight, down_weight):
    core = lax.axis_index("c")
    sign = 1 - 2 * core
    place = {
        "x": lax.axis_index("xh") * 2 + lax.axis_index("xl"),
        "y": lax.axis_index("y"),
        "z": lax.axis_index("z"),
    }
    tensor = ("xh", "z", "c")
    own = down_weight.shape[1]

    units = gate_weight.shape[1] // (8 * LANES)
    widths = [(units // 3 + (1 if at < units % 3 else 0)) * LANES for at in range(3)]
    begins = [8 * sum(widths[:at]) for at in range(3)]

    wheres = []
    for cross, first, second in PLAN:
        to = lambda ring: [(place[ring] + sign * shift) % 4 for shift in SHIFTS]
        back = lambda ring: [(place[ring] - sign * shift) % 4 for shift in SHIFTS]
        where = [core] + to(cross) + to(first) + to(second) + back(first) + back(second)
        wheres.append(jnp.stack([jnp.asarray(entry, jnp.int32) for entry in where]))

    cross = [rings[0] for rings in PLAN]
    packing = list(zip(wheres, begins, widths))
    packed = [pack_gate_up(where, gate_weight, up_weight, *at) for where, *at in packing]
    received = exchange_all(packed, cross)

    count, decode_count = prompt.shape[0], decode_in.shape[0]
    block = count + decode_count
    both = jnp.concatenate([prompt, decode_in], axis=0)
    both = both.reshape(block, 16, own).swapaxes(0, 1)
    both = lax.all_to_all(both, tensor, split_axis=0, concat_axis=0, tiled=True)
    prompt_rows, state = both[:, :count], both[:, count:]

    packed = [pack_down(where, down_weight, *at) for where, *at in packing]
    gate_up = [share_cores(values) for values in received]
    received, packed = lax.optimization_barrier((received, packed))
    down = [share_cores(values) for values in exchange_all(packed, cross)]

    span = count // STEPS
    outs = []
    for turn in range(STEPS):
        rows = jnp.concatenate([prompt_rows[:, turn * span : (turn + 1) * span], state], axis=1)
        mine = gather_rows(rows.reshape(-1, own))
        others = core_swap(jnp.stack([value for part in mine for value in part]))
        update = block_update(mine, others, wheres, gate_up, down).reshape(rows.shape)
        outs.append(update[:, :span].astype(jnp.bfloat16))
        state = (state.astype(jnp.float32) + update[:, span:]).astype(jnp.bfloat16)

    both = jnp.concatenate(outs + [state], axis=1)
    both = lax.all_to_all(both, tensor, split_axis=0, concat_axis=0, tiled=True)
    both = both.swapaxes(0, 1).reshape(block, 16 * own)
    return both[:count], both[count:]


def solution(mesh):
    fine = Mesh(mesh.devices.reshape(4, 2, 2, 4, 2), ("y", "xl", "xh", "z", "c"))
    fsdp, tensor = ("y", "xl"), ("xh", "z", "c")
    return jax.shard_map(
        shards,
        mesh=fine,
        in_specs=(
            P(tensor, fsdp),
            P(tensor, fsdp),
            P(fsdp + tensor, None),
            P(fsdp + tensor, None),
            P(None, fsdp + tensor),
        ),
        out_specs=(P(tensor, fsdp), P(tensor, fsdp)),
        check_vma=False,
    )
```

time: 1130 us -> 602 us (0.53)
  waiting for transfers between devices: 592 us -> 170 us
  blocking collectives: 341 us -> 17.3 us
  starting transfers between devices: 25 us -> 217 us
  Pallas kernels: 0 us -> 143 us
  matrix products: 67.4 us -> 0 us
  local copies, waits for them, and re-layouts: 75.2 us -> 26.7 us
  between operations: 15.6 us -> 2.92 us
    reduce_scatter x5 -> x0, waiting for transfers between devices: 414 us -> none  [the longest x1 172 us: shards(): lax.psum_scatter(up_part, 'fsdp', scatter_dimension=0, tiled=True)]
    ppermute x0 -> x140, starting transfers between devices: none -> 208 us  [the longest x126 166 us: ring_permute(): return lax.ppermute(value, RINGS[ring] + ('c',), pairs)]
    ppermute x0 -> x140, waiting for transfers between devices: none -> 170 us  [the longest x126 166 us: ring_permute(): return lax.ppermute(value, RINGS[ring] + ('c',), pairs)]
    all_gather x2 -> x0, blocking collectives: 169 us -> none  [shards(): rows_all = lax.all_gather(state, 'tensor', axis=0, tiled=True)]
    all_to_all x1, blocking collectives: 171 us -> 17.3 us  [shards(): both = lax.all_to_all(both, tensor, split_axis=0, concat_axis=0, tiled=True)]
    pallas_call x0 -> x24, Pallas kernels: none -> 143 us  [the longest x6 51.5 us: gate_up_products(): pl.pallas_call(body, grid=(2, width // tile), out_shape=[jax.ShapeDtypeSt...]
    all_to_all x2 -> x1, waiting for transfers between devices: 100 us -> 0.01 us  [shards(): both = lax.all_to_all(both, tensor, split_axis=0, concat_axis=0, tiled=True)]
    all_gather x2 -> x0, waiting for transfers between devices: 75.1 us -> none  [the longest x1 75.1 us: shards(): lax.all_gather(gated(gate_share, up_share), 'fsdp', axis=0, tiled=True)]
  transfers between devices with their start and end apart: 11 -> 141, of which waited for: 7 -> 50; matrix products, arithmetic and copies ran while one was open for 10% -> 5% of each run, Pallas kernels for 0% -> 23%
where the time goes in v1:
time: 602 us; the launch traced here: 591 us
  starting transfers between devices  217 us (36%)
  waiting for transfers between devices  170 us (28%)
  Pallas kernels  143 us (24%)
  local copies, waits for them, and re-layouts  26.7 us (4%)
  blocking collectives  17.3 us (3%)
  other arithmetic  14.1 us (2%)
    ppermute x126, waiting for transfers between devices, ring_permute(): return lax.ppermute(value, RINGS[ring] + ('c',), pairs)  166 us
    ppermute x126, starting transfers between devices, ring_permute(): return lax.ppermute(value, RINGS[ring] + ('c',), pairs)  166 us
    pallas_call x6, Pallas kernels, gate_up_products(): pl.pallas_call(body, grid=(2, width // tile), out_shape=[jax.ShapeDtypeSt...  51.5 us
    ppermute x14, starting transfers between devices, core_swap(): return lax.ppermute(value, 'c', [(0, 1), (1, 0)])  42 us
    pallas_call x6, Pallas kernels, down_products(): pl.pallas_call(body, grid=(1,), out_shape=[jax.ShapeDtypeStruct((rows, ow...  33.4 us
    pallas_call x6, Pallas kernels, first_sums(): pl.pallas_call(body, grid=(2, width // tile), out_shape=[jax.ShapeDtypeSt...  27.7 us
    all_to_all x1, blocking collectives, shards(): both = lax.all_to_all(both, tensor, split_axis=0, concat_axis=0, tiled=True)  17.3 us
    pallas_call x3, Pallas kernels, pack_gate_up(): pl.pallas_call(body, out_shape=[jax.ShapeDtypeStruct((2, 2, rows, width),...  17.2 us
  transfers between devices with their start and end apart: 141, of which 50 were waited for; matrix products, arithmetic and copies ran while one was open for 5% of the time, Pallas kernels for 23%

profile of v1, /device:TPU:1, one launch (start us, length us, event | category | flops | bytes accessed | tf_op | source)
XLA Modules:
  0.0 590.9 jit_solution(1778061296072743354)
XLA Ops:
  2.4 9.3 %all-to-all-start = ((bf16[16,72,128]{2,1,0:T(8,128)(2,1)}), bf16[16,72,128]{2,1,0:T(8,128)(2,1)}, u32[]{:S(2)}, u32[]{:S(2)}) async-start(bf16[16,72,128]{2,1,0:T(8,128)(2,1)} %bitcast_bitcast_fusion), calls=%async_computation | async-start | bytes 589824 | tf_op jit(solution)/shard_map/all_to_all | solution.py:345
  12.4 5.9 pack_gate_up.3
  21.6 5.9 pack_gate_up.4
  30.6 5.5 pack_gate_up.5
  46.8 4.9 collective-permute-done.1.rest_2_
  52.5 5.3 collective-permute-done.2.rest_3_
  62.2 4.0 collective-permute-start.5
  84.7 13.8 %collective-permute-start.9 = (bf16[12,640,128]{2,1,0:T(8,128)(2,1)}, bf16[12,640,128]{2,1,0:T(8,128)(2,1)}, u32[]{:S(2)}, u32[]{:S(2)}) collective-permute-start(bf16[12,640,128]{2,1,0:T(8,128)(2,1)} %bitcast_dynamic-update-slice_fusion.12), channel_id=1, source_target_pairs={{0,1},{1,0},{2,3},{3,2},{4,5},{5,4},{6,7},{7,6},{8,9},{9,8},{10,11... | collective-permute-start | bytes 5898248 | tf_op jit(solution)/shard_map/ppermute | solution.py:33
  98.6 14.2 %collective-permute-done.16.rest_7_ = bf16[2,2,128,1152]{3,2,1,0:T(8,128)(2,1)S(1)} collective-permute-done((bf16[2,2,128,1152]{3,2,1,0:T(8,128)(2,1)S(1)}, bf16[2,2,128,1152]{3,2,1,0:T(8,128)(2,1)S(1)}, u32[]{:S(2)}, u32[]{:S(2)}) %collective-permute-start.16) | collective-permute-done | bytes 1179680 | tf_op jit(solution)/shard_map/ppermute | solution.py:29
  121.9 4.7 pack_down.3
  126.6 4.8 pack_down.4
  131.4 3.4 pack_down.5
  136.9 7.3 %gate_up_products.8 = (bf16[2,160,1024]{2,1,0:T(8,128)(2,1)}, bf16[2,160,1024]{2,1,0:T(8,128)(2,1)}, bf16[2,160,1024]{2,1,0:T(8,128)(2,1)}, bf16[2,160,1024]{2,1,0:T(8,128)(2,1)}) custom-call(s32[21]{0:T(128)} %stack.306.where_ref, bf16[640,128]{1,0:T(8,128)(2,1)} %bitcast.343, bf16[640,128]{1,0:T(8,128)(2,1)} %copy-done.48, bf16[640,128]{1,0:T(8,128)(2,1)} %copy-done.49, ...), custom_call_target="tpu_custom_call" | custom-call | flops 2684354560 | bytes 8126464 | tf_op jit(solution)/shard_map/gate_up_products/pallas_call | solution.py:148
  144.4 9.2 %gate_up_products.6 = (bf16[2,160,1152]{2,1,0:T(8,128)(2,1)}, bf16[2,160,1152]{2,1,0:T(8,128)(2,1)}, bf16[2,160,1152]{2,1,0:T(8,128)(2,1)}, bf16[2,160,1152]{2,1,0:T(8,128)(2,1)}) custom-call(s32[21]{0:T(128)} %stack.291.where_ref, bf16[640,128]{1,0:T(8,128)(2,1)} %bitcast.344, bf16[640,128]{1,0:T(8,128)(2,1)} %copy-done.42, bf16[640,128]{1,0:T(8,128)(2,1)} %copy-done.43, ...), custom_call_target="tpu_custom_call" | custom-call | flops 3019898880 | bytes 8978432 | tf_op jit(solution)/shard_map/gate_up_products/pallas_call | solution.py:148
  153.6 3.5 collective-permute-start.22
  157.0 9.2 %gate_up_products.7 = (bf16[2,160,1152]{2,1,0:T(8,128)(2,1)}, bf16[2,160,1152]{2,1,0:T(8,128)(2,1)}, bf16[2,160,1152]{2,1,0:T(8,128)(2,1)}, bf16[2,160,1152]{2,1,0:T(8,128)(2,1)}) custom-call(s32[21]{0:T(128)} %stack.305.where_ref, bf16[640,128]{1,0:T(8,128)(2,1)} %bitcast.345, bf16[640,128]{1,0:T(8,128)(2,1)} %copy-done.44, bf16[640,128]{1,0:T(8,128)(2,1)} %copy-done.46, ...), custom_call_target="tpu_custom_call" | custom-call | flops 3019898880 | bytes 8978432 | tf_op jit(solution)/shard_map/gate_up_products/pallas_call | solution.py:148
  172.6 5.0 collective-permute-done.23.rest_1_
  182.1 12.8 %collective-permute-done.63.rest_6_ = bf16[2,1152,128]{2,1,0:T(8,128)(2,1)S(1)} collective-permute-done((bf16[2,1152,128]{2,1,0:T(8,128)(2,1)}, bf16[2,1152,128]{2,1,0:T(8,128)(2,1)S(1)}, u32[]{:S(2)}, u32[]{:S(2)}) %collective-permute-start.63) | collective-permute-done | bytes 589856 | tf_op jit(solution)/shard_map/ppermute | solution.py:29
  197.6 15.5 %collective-permute-start.70 = (bf16[2,1024,128]{2,1,0:T(8,128)(2,1)}, bf16[2,1024,128]{2,1,0:T(8,128)(2,1)}, u32[]{:S(2)}, u32[]{:S(2)}) collective-permute-start(bf16[2,1024,128]{2,1,0:T(8,128)(2,1)} %get-tuple-element.395), channel_id=1, source_target_pairs={{0,64},{32,96},{64,0},{96,32},{1,65},{33,97},{65,1},{97,33},{2,66}... | collective-permute-start | bytes 1572872 | tf_op jit(solution)/shard_map/ppermute | solution.py:29
  215.1 5.0 first_sums.6
  220.1 4.9 first_sums.7
  225.1 7.5 %collective-permute-done.29.rest_2_ = bf16[2,160,1024]{2,1,0:T(8,128)(2,1)} collective-permute-done((bf16[2,160,1024]{2,1,0:T(8,128)(2,1)}, bf16[2,160,1024]{2,1,0:T(8,128)(2,1)}, u32[]{:S(2)}, u32[]{:S(2)}) %collective-permute-start.29) | collective-permute-done | bytes 655392 | tf_op jit(solution)/shard_map/ppermute | solution.py:29
  232.6 3.9 first_sums.8
  236.5 4.5 collective-permute-start.33
  246.9 7.2 %collective-permute-done.33 = bf16[2,40,1024]{2,1,0:T(8,128)(2,1)S(1)} collective-permute-done((bf16[2,40,1024]{2,1,0:T(8,128)(2,1)}, bf16[2,40,1024]{2,1,0:T(8,128)(2,1)S(1)}, u32[]{:S(2)}, u32[]{:S(2)}) %collective-permute-start.33) | collective-permute-done | bytes 163872 | tf_op jit(solution)/shard_map/ppermute | solution.py:29
  254.2 3.1 collective-permute-start.38
  257.3 2.9 collective-permute-start.39
  266.5 4.6 collective-permute-done.35
  277.3 3.2 collective-permute-start.48
  293.7 2.9 collective-permute-done.51.rest_1_
  296.6 7.2 %collective-permute-start.65 = (bf16[4,1152,128]{2,1,0:T(8,128)(2,1)S(1)}, bf16[4,1152,128]{2,1,0:T(8,128)(2,1)}, u32[]{:S(2)}, u32[]{:S(2)}) collective-permute-start(bf16[4,1152,128]{2,1,0:T(8,128)(2,1)S(1)} %pad_maximum_fusion.4), channel_id=1, source_target_pairs={{0,1},{1,0},{2,3},{3,2},{4,5},{5,4},{6,7},{7,6},{8,9},{9,8},{10,11... | collective-permute-start | bytes 3538952 | tf_op jit(solution)/shard_map/ppermute | solution.py:33
  307.7 10.7 %collective-permute-done.67.rest_2_ = bf16[4,40,1024]{2,1,0:T(8,128)(2,1)S(1)} collective-permute-done((bf16[4,40,1024]{2,1,0:T(8,128)(2,1)S(1)}, bf16[4,40,1024]{2,1,0:T(8,128)(2,1)S(1)}, u32[]{:S(2)}, u32[]{:S(2)}) %collective-permute-start.67) | collective-permute-done | bytes 327712 | tf_op jit(solution)/shard_map/ppermute | solution.py:29
  319.2 3.0 collective-permute-start.62
  322.3 5.2 down_products.8
  328.2 5.7 down_products.6
  335.0 5.7 down_products.7
  355.8 3.0 collective-permute-done.81
  368.8 3.8 collective-permute-done.83.rest_2_
  372.7 4.2 collective-permute-start.89
  379.8 4.2 collective-permute-done.90.rest_3_
  384.0 5.0 collective-permute-start.91
  389.0 3.7 collective-permute-done.91.rest_4_
  392.7 9.2 %gate_up_products.9 = (bf16[2,160,1152]{2,1,0:T(8,128)(2,1)}, bf16[2,160,1152]{2,1,0:T(8,128)(2,1)}, bf16[2,160,1152]{2,1,0:T(8,128)(2,1)}, bf16[2,160,1152]{2,1,0:T(8,128)(2,1)}) custom-call(s32[21]{0:T(128)} %stack.291.where_ref, bf16[640,128]{1,0:T(8,128)(2,1)} %bitcast.358, bf16[640,128]{1,0:T(8,128)(2,1)} %copy-done.54, bf16[640,128]{1,0:T(8,128)(2,1)} %copy-done.55, ...), custom_call_target="tpu_custom_call" | custom-call | flops 3019898880 | bytes 8978432 | tf_op jit(solution)/shard_map/gate_up_products/pallas_call | solution.py:148
  403.1 9.2 %gate_up_products.10 = (bf16[2,160,1152]{2,1,0:T(8,128)(2,1)}, bf16[2,160,1152]{2,1,0:T(8,128)(2,1)}, bf16[2,160,1152]{2,1,0:T(8,128)(2,1)}, bf16[2,160,1152]{2,1,0:T(8,128)(2,1)}) custom-call(s32[21]{0:T(128)} %stack.305.where_ref, bf16[640,128]{1,0:T(8,128)(2,1)} %bitcast.359, bf16[640,128]{1,0:T(8,128)(2,1)} %copy-done.51, bf16[640,128]{1,0:T(8,128)(2,1)} %copy-done.52, ...), custom_call_target="tpu_custom_call" | custom-call | flops 3019898880 | bytes 8978432 | tf_op jit(solution)/shard_map/gate_up_products/pallas_call | solution.py:148
  413.5 7.3 %gate_up_products.11 = (bf16[2,160,1024]{2,1,0:T(8,128)(2,1)}, bf16[2,160,1024]{2,1,0:T(8,128)(2,1)}, bf16[2,160,1024]{2,1,0:T(8,128)(2,1)}, bf16[2,160,1024]{2,1,0:T(8,128)(2,1)}) custom-call(s32[21]{0:T(128)} %stack.306.where_ref, bf16[640,128]{1,0:T(8,128)(2,1)} %bitcast.360, bf16[640,128]{1,0:T(8,128)(2,1)} %copy-done.53, bf16[640,128]{1,0:T(8,128)(2,1)} %copy-done.58, ...), custom_call_target="tpu_custom_call" | custom-call | flops 2684354560 | bytes 8126464 | tf_op jit(solution)/shard_map/gate_up_products/pallas_call | solution.py:148
  421.8 9.2 %collective-permute-done.94.rest_1_ = bf16[2,160,1024]{2,1,0:T(8,128)(2,1)S(1)} collective-permute-done((bf16[2,160,1024]{2,1,0:T(8,128)(2,1)}, bf16[2,160,1024]{2,1,0:T(8,128)(2,1)S(1)}, u32[]{:S(2)}, u32[]{:S(2)}) %collective-permute-start.94) | collective-permute-done | bytes 655392 | tf_op jit(solution)/shard_map/ppermute | solution.py:29
  435.4 15.3 %collective-permute-done.96.rest_3_ = bf16[2,160,1152]{2,1,0:T(8,128)(2,1)} collective-permute-done((bf16[2,160,1152]{2,1,0:T(8,128)(2,1)}, bf16[2,160,1152]{2,1,0:T(8,128)(2,1)}, u32[]{:S(2)}, u32[]{:S(2)}) %collective-permute-start.96) | collective-permute-done | bytes 737312 | tf_op jit(solution)/shard_map/ppermute | solution.py:29
  450.6 5.0 first_sums.9
  455.7 3.1 collective-permute-done.97.rest_2_
  459.6 4.9 first_sums.10
  466.8 4.0 first_sums.11
  482.7 3.6 collective-permute-start.112
  486.8 3.4 collective-permute-start.110
  497.1 3.0 collective-permute-start.116
  506.5 5.7 collective-permute-done.121.rest_1_
  512.9 3.1 collective-permute-start.123
  518.5 3.6 collective-permute-done.129.rest_3_
  522.1 5.2 down_products.11
  527.3 11.5 %collective-permute-start.130 = (bf16[4,640,128]{2,1,0:T(8,128)(2,1)}, bf16[4,640,128]{2,1,0:T(8,128)(2,1)S(1)}, u32[]{:S(2)}, u32[]{:S(2)}) collective-permute-start(bf16[4,640,128]{2,1,0:T(8,128)(2,1)} %get-tuple-element.496), channel_id=1, source_target_pairs={{0,1},{1,0},{2,3},{3,2},{4,5},{5,4},{6,7},{7,6},{8,9},{9,8},{10,11... | collective-permute-start | bytes 1966088 | tf_op jit(solution)/shard_map/ppermute | solution.py:33
  540.2 5.7 down_products.9
  546.1 5.9 %down_products.10 = (bf16[640,128]{1,0:T(8,128)(2,1)}, bf16[640,128]{1,0:T(8,128)(2,1)}, bf16[640,128]{1,0:T(8,128)(2,1)}, bf16[640,128]{1,0:T(8,128)(2,1)}, bf16[4,640,128]{2,1,0:T(8,128)(2,1)}) custom-call(s32[21]{0:T(128)} %stack.305.where_ref, bf16[4,40,1152]{2,1,0:T(8,128)(2,1)} %copy-done.26, bf16[4,40,1152]{2,1,0:T(8,128)(2,1)} %copy-done.89, ...), custom_call_target="tpu_custom_call" | custom-call | flops 1509949440 | bytes 5144576 | tf_op jit(solution)/shard_map/down_products/pallas_call | solution.py:231
  553.9 3.4 collective-permute-start.131
  562.5 3.2 collective-permute-start.137
  571.8 17.3 %all_to_all.10 = bf16[16,72,128]{2,1,0:T(8,128)(2,1)S(1)} all-to-all(bf16[16,72,128]{2,1,0:T(8,128)(2,1)S(1)} %pad_maximum_fusion.12), channel_id=1, replica_groups=mesh['y'=4,'xl'=2,'xh'=2,'z'=4,'c'=2] {'xh','z','c'}, dimensions={0} | all-to-all | bytes 589824 | tf_op jit(solution)/shard_map/all_to_all | solution.py:364
  (580 shorter events, 190.7 us)
Async XLA Ops:
  2.4 36.5 %all-to-all-start = ((bf16[16,72,128]{2,1,0:T(8,128)(2,1)}), bf16[16,72,128]{2,1,0:T(8,128)(2,1)}, u32[]{:S(2)}, u32[]{:S(2)}) async-start(bf16[16,72,128]{2,1,0:T(8,128)(2,1)} %bitcast_bitcast_fusion), calls=%async_computation | async-start | bytes 589824 | tf_op jit(solution)/shard_map/all_to_all | solution.py:345
  18.2 48.0 %collective-permute-start.10 = (bf16[2,2,128,1152]{3,2,1,0:T(8,128)(2,1)}, bf16[2,2,128,1152]{3,2,1,0:T(8,128)(2,1)S(1)}, u32[]{:S(2)}, u32[]{:S(2)}) collective-permute-start(bf16[2,2,128,1152]{3,2,1,0:T(8,128)(2,1)} %get-tuple-element.261), channel_id=1, source_target_pairs={{0,2},{2,4},{4,6},{6,0},{1,7},{3,1},{5,3},{7,5},{8,10},{10,12},{12... | collective-permute-start | bytes 3538952 | tf_op jit(solution)/shard_map/ppermute | solution.py:29
  27.4 39.1 %collective-permute-start.11 = (bf16[2,2,128,1152]{3,2,1,0:T(8,128)(2,1)}, bf16[2,2,128,1152]{3,2,1,0:T(8,128)(2,1)S(1)}, u32[]{:S(2)}, u32[]{:S(2)}) collective-permute-start(bf16[2,2,128,1152]{3,2,1,0:T(8,128)(2,1)} %get-tuple-element.264), channel_id=1, source_target_pairs={{0,16},{16,8},{8,24},{24,0},{1,25},{17,1},{9,17},{25,9},{2,18},{18... | collective-permute-start | bytes 3538952 | tf_op jit(solution)/shard_map/ppermute | solution.py:29
  36.1 26.1 %collective-permute-start.12 = (bf16[2,2,128,1024]{3,2,1,0:T(8,128)(2,1)}, bf16[2,2,128,1024]{3,2,1,0:T(8,128)(2,1)S(1)}, u32[]{:S(2)}, u32[]{:S(2)}) collective-permute-start(bf16[2,2,128,1024]{3,2,1,0:T(8,128)(2,1)} %get-tuple-element.267), channel_id=1, source_target_pairs={{0,32},{32,64},{64,96},{96,0},{1,97},{33,1},{65,33},{97,65},{2,34}... | collective-permute-start | bytes 3145736 | tf_op jit(solution)/shard_map/ppermute | solution.py:29
  42.1 37.4 %collective-permute-start.19 = (bf16[2,2,128,1024]{3,2,1,0:T(8,128)(2,1)}, bf16[2,2,128,1024]{3,2,1,0:T(8,128)(2,1)S(1)}, u32[]{:S(2)}, u32[]{:S(2)}) collective-permute-start(bf16[2,2,128,1024]{3,2,1,0:T(8,128)(2,1)} %get-tuple-element.289), channel_id=1, source_target_pairs={{0,96},{32,0},{64,32},{96,64},{1,33},{33,65},{65,97},{97,1},{2,98}... | collective-permute-start | bytes 3145736 | tf_op jit(solution)/shard_map/ppermute | solution.py:29
  68.4 16.3 %collective-permute-start.13 = (bf16[2,2,128,1152]{3,2,1,0:T(8,128)(2,1)S(1)}, bf16[2,2,128,1152]{3,2,1,0:T(8,128)(2,1)S(1)}, u32[]{:S(2)}, u32[]{:S(2)}) collective-permute-start(bf16[2,2,128,1152]{3,2,1,0:T(8,128)(2,1)S(1)} %copy-done.85), channel_id=1, source_target_pairs={{0,6},{2,0},{4,2},{6,4},{1,3},{3,5},{5,7},{7,1},{8,14},{10,8},{12,... | collective-permute-start | bytes 3538952 | tf_op jit(solution)/shard_map/ppermute | solution.py:29
  71.2 41.6 %collective-permute-start.16 = (bf16[2,2,128,1152]{3,2,1,0:T(8,128)(2,1)S(1)}, bf16[2,2,128,1152]{3,2,1,0:T(8,128)(2,1)S(1)}, u32[]{:S(2)}, u32[]{:S(2)}) collective-permute-start(bf16[2,2,128,1152]{3,2,1,0:T(8,128)(2,1)S(1)} %copy-done.87), channel_id=1, source_target_pairs={{0,24},{16,0},{8,16},{24,8},{1,17},{17,9},{9,25},{25,1},{2,26},{18... | collective-permute-start | bytes 3538952 | tf_op jit(solution)/shard_map/ppermute | solution.py:29
  73.5 39.2 %collective-permute-start.20 = (bf16[2,2,128,1024]{3,2,1,0:T(8,128)(2,1)}, bf16[2,2,128,1024]{3,2,1,0:T(8,128)(2,1)S(1)}, u32[]{:S(2)}, u32[]{:S(2)}) collective-permute-start(bf16[2,2,128,1024]{3,2,1,0:T(8,128)(2,1)} %get-tuple-element.290), channel_id=1, source_target_pairs={{0,64},{32,96},{64,0},{96,32},{1,65},{33,97},{65,1},{97,33},{2,66}... | collective-permute-start | bytes 3145736 | tf_op jit(solution)/shard_map/ppermute | solution.py:29
  77.0 40.4 %collective-permute-start.14 = (bf16[2,2,128,1152]{3,2,1,0:T(8,128)(2,1)S(1)}, bf16[2,2,128,1152]{3,2,1,0:T(8,128)(2,1)S(1)}, u32[]{:S(2)}, u32[]{:S(2)}) collective-permute-start(bf16[2,2,128,1152]{3,2,1,0:T(8,128)(2,1)S(1)} %copy-done.84), channel_id=1, source_target_pairs={{0,4},{2,6},{4,0},{6,2},{1,5},{3,7},{5,1},{7,3},{8,12},{10,14},{12... | collective-permute-start | bytes 3538952 | tf_op jit(solution)/shard_map/ppermute | solution.py:29
  79.6 39.8 %collective-permute-start.17 = (bf16[2,2,128,1152]{3,2,1,0:T(8,128)(2,1)S(1)}, bf16[2,2,128,1152]{3,2,1,0:T(8,128)(2,1)S(1)}, u32[]{:S(2)}, u32[]{:S(2)}) collective-permute-start(bf16[2,2,128,1152]{3,2,1,0:T(8,128)(2,1)S(1)} %copy-done.86), channel_id=1, source_target_pairs={{0,8},{16,24},{8,0},{24,16},{1,9},{17,25},{9,1},{25,17},{2,10},{18... | collective-permute-start | bytes 3538952 | tf_op jit(solution)/shard_map/ppermute | solution.py:29
  84.7 50.7 %collective-permute-start.9 = (bf16[12,640,128]{2,1,0:T(8,128)(2,1)}, bf16[12,640,128]{2,1,0:T(8,128)(2,1)}, u32[]{:S(2)}, u32[]{:S(2)}) collective-permute-start(bf16[12,640,128]{2,1,0:T(8,128)(2,1)} %bitcast_dynamic-update-slice_fusion.12), channel_id=1, source_target_pairs={{0,1},{1,0},{2,3},{3,2},{4,5},{5,4},{6,7},{7,6},{8,9},{9,8},{10,11... | collective-permute-start | bytes 5898248 | tf_op jit(solution)/shard_map/ppermute | solution.py:33
  115.5 21.2 %collective-permute-start.21 = (bf16[4,2,128,1024]{3,2,1,0:T(8,128)(2,1)}, bf16[4,2,128,1024]{3,2,1,0:T(8,128)(2,1)}, u32[]{:S(2)}, u32[]{:S(2)}) collective-permute-start(bf16[4,2,128,1024]{3,2,1,0:T(8,128)(2,1)} %pad_maximum_fusion.2), channel_id=1, source_target_pairs={{0,1},{1,0},{2,3},{3,2},{4,5},{5,4},{6,7},{7,6},{8,9},{9,8},{10,11... | collective-permute-start | bytes 6291464 | tf_op jit(solution)/shard_map/ppermute | solution.py:33
  119.3 24.9 %collective-permute-start.15 = (bf16[4,2,128,1152]{3,2,1,0:T(8,128)(2,1)}, bf16[4,2,128,1152]{3,2,1,0:T(8,128)(2,1)}, u32[]{:S(2)}, u32[]{:S(2)}) collective-permute-start(bf16[4,2,128,1152]{3,2,1,0:T(8,128)(2,1)} %pad_maximum_fusion), channel_id=1, source_target_pairs={{0,1},{1,0},{2,3},{3,2},{4,5},{5,4},{6,7},{7,6},{8,9},{9,8},{10,11... | collective-permute-start | bytes 7077896 | tf_op jit(solution)/shard_map/ppermute | solution.py:33
  121.3 32.2 %collective-permute-start.18 = (bf16[4,2,128,1152]{3,2,1,0:T(8,128)(2,1)}, bf16[4,2,128,1152]{3,2,1,0:T(8,128)(2,1)}, u32[]{:S(2)}, u32[]{:S(2)}) collective-permute-start(bf16[4,2,128,1152]{3,2,1,0:T(8,128)(2,1)} %pad_maximum_fusion.1), channel_id=1, source_target_pairs={{0,1},{1,0},{2,3},{3,2},{4,5},{5,4},{6,7},{7,6},{8,9},{9,8},{10,11... | collective-permute-start | bytes 7077896 | tf_op jit(solution)/shard_map/ppermute | solution.py:33
  134.8 34.0 %collective-permute-start.54 = (bf16[2,1152,128]{2,1,0:T(8,128)(2,1)}, bf16[2,1152,128]{2,1,0:T(8,128)(2,1)S(1)}, u32[]{:S(2)}, u32[]{:S(2)}) collective-permute-start(bf16[2,1152,128]{2,1,0:T(8,128)(2,1)} %get-tuple-element.363), channel_id=1, source_target_pairs={{0,2},{2,4},{4,6},{6,0},{1,7},{3,1},{5,3},{7,5},{8,10},{10,12},{12... | collective-permute-start | bytes 1769480 | tf_op jit(solution)/shard_map/ppermute | solution.py:29
  135.4 30.8 %collective-permute-start.56 = (bf16[2,1024,128]{2,1,0:T(8,128)(2,1)}, bf16[2,1024,128]{2,1,0:T(8,128)(2,1)S(1)}, u32[]{:S(2)}, u32[]{:S(2)}) collective-permute-start(bf16[2,1024,128]{2,1,0:T(8,128)(2,1)} %get-tuple-element.369), channel_id=1, source_target_pairs={{0,32},{32,64},{64,96},{96,0},{1,97},{33,1},{65,33},{97,65},{2,34}... | collective-permute-start | bytes 1572872 | tf_op jit(solution)/shard_map/ppermute | solution.py:29
  136.7 32.1 %collective-permute-start.69 = (bf16[2,1024,128]{2,1,0:T(8,128)(2,1)}, bf16[2,1024,128]{2,1,0:T(8,128)(2,1)S(1)}, u32[]{:S(2)}, u32[]{:S(2)}) collective-permute-start(bf16[2,1024,128]{2,1,0:T(8,128)(2,1)} %get-tuple-element.394), channel_id=1, source_target_pairs={{0,96},{32,0},{64,32},{96,64},{1,33},{33,65},{65,97},{97,1},{2,98}... | collective-permute-start | bytes 1572872 | tf_op jit(solution)/shard_map/ppermute | solution.py:29
  144.2 26.1 %collective-permute-start.24 = (bf16[2,160,1024]{2,1,0:T(8,128)(2,1)}, bf16[2,160,1024]{2,1,0:T(8,128)(2,1)S(1)}, u32[]{:S(2)}, u32[]{:S(2)}) collective-permute-start(bf16[2,160,1024]{2,1,0:T(8,128)(2,1)} %get-tuple-element.291), channel_id=1, source_target_pairs={{0,2},{2,4},{4,6},{6,0},{1,7},{3,1},{5,3},{7,5},{8,10},{10,12},{12... | collective-permute-start | bytes 1966088 | tf_op jit(solution)/shard_map/ppermute | solution.py:29
  153.6 18.1 %collective-permute-start.22 = (bf16[2,160,1152]{2,1,0:T(8,128)(2,1)}, bf16[2,160,1152]{2,1,0:T(8,128)(2,1)}, u32[]{:S(2)}, u32[]{:S(2)}) collective-permute-start(bf16[2,160,1152]{2,1,0:T(8,128)(2,1)} %get-tuple-element.277), channel_id=1, source_target_pairs={{0,16},{16,8},{8,24},{24,0},{1,25},{17,1},{9,17},{25,9},{2,18},{18... | collective-permute-start | bytes 2211848 | tf_op jit(solution)/shard_map/ppermute | solution.py:29
  166.3 11.3 %collective-permute-start.23 = (bf16[2,160,1152]{2,1,0:T(8,128)(2,1)}, bf16[2,160,1152]{2,1,0:T(8,128)(2,1)S(1)}, u32[]{:S(2)}, u32[]{:S(2)}) collective-permute-start(bf16[2,160,1152]{2,1,0:T(8,128)(2,1)} %get-tuple-element.284), channel_id=1, source_target_pairs={{0,32},{32,64},{64,96},{96,0},{1,97},{33,1},{65,33},{97,65},{2,34}... | collective-permute-start | bytes 2211848 | tf_op jit(solution)/shard_map/ppermute | solution.py:29
  170.3 27.3 %collective-permute-start.25 = (bf16[2,160,1152]{2,1,0:T(8,128)(2,1)}, bf16[2,160,1152]{2,1,0:T(8,128)(2,1)S(1)}, u32[]{:S(2)}, u32[]{:S(2)}) collective-permute-start(bf16[2,160,1152]{2,1,0:T(8,128)(2,1)} %get-tuple-element.298), channel_id=1, source_target_pairs={{0,24},{16,0},{8,16},{24,8},{1,17},{17,9},{9,25},{25,1},{2,26},{18... | collective-permute-start | bytes 2211848 | tf_op jit(solution)/shard_map/ppermute | solution.py:29
  171.7 23.2 %collective-permute-start.63 = (bf16[2,1152,128]{2,1,0:T(8,128)(2,1)}, bf16[2,1152,128]{2,1,0:T(8,128)(2,1)S(1)}, u32[]{:S(2)}, u32[]{:S(2)}) collective-permute-start(bf16[2,1152,128]{2,1,0:T(8,128)(2,1)} %get-tuple-element.385), channel_id=1, source_target_pairs={{0,24},{16,0},{8,16},{24,8},{1,17},{17,9},{9,25},{25,1},{2,26},{18... | collective-permute-start | bytes 1769480 | tf_op jit(solution)/shard_map/ppermute | solution.py:29
  177.5 20.1 %collective-permute-start.27 = (bf16[2,160,1152]{2,1,0:T(8,128)(2,1)}, bf16[2,160,1152]{2,1,0:T(8,128)(2,1)S(1)}, u32[]{:S(2)}, u32[]{:S(2)}) collective-permute-start(bf16[2,160,1152]{2,1,0:T(8,128)(2,1)} %get-tuple-element.306), channel_id=1, source_target_pairs={{0,96},{32,0},{64,32},{96,64},{1,33},{33,65},{65,97},{97,1},{2,98}... | collective-permute-start | bytes 2211848 | tf_op jit(solution)/shard_map/ppermute | solution.py:29
  179.9 33.2 %collective-permute-start.26 = (bf16[2,160,1152]{2,1,0:T(8,128)(2,1)}, bf16[2,160,1152]{2,1,0:T(8,128)(2,1)S(1)}, u32[]{:S(2)}, u32[]{:S(2)}) collective-permute-start(bf16[2,160,1152]{2,1,0:T(8,128)(2,1)} %get-tuple-element.299), channel_id=1, source_target_pairs={{0,8},{16,24},{8,0},{24,16},{1,9},{17,25},{9,1},{25,17},{2,10},{18... | collective-permute-start | bytes 2211848 | tf_op jit(solution)/shard_map/ppermute | solution.py:29
  179.9 33.3 %collective-permute-start.28 = (bf16[2,160,1152]{2,1,0:T(8,128)(2,1)}, bf16[2,160,1152]{2,1,0:T(8,128)(2,1)S(1)}, u32[]{:S(2)}, u32[]{:S(2)}) collective-permute-start(bf16[2,160,1152]{2,1,0:T(8,128)(2,1)} %get-tuple-element.307), channel_id=1, source_target_pairs={{0,64},{32,96},{64,0},{96,32},{1,65},{33,97},{65,1},{97,33},{2,66}... | collective-permute-start | bytes 2211848 | tf_op jit(solution)/shard_map/ppermute | solution.py:29
  195.0 37.6 %collective-permute-start.29 = (bf16[2,160,1024]{2,1,0:T(8,128)(2,1)}, bf16[2,160,1024]{2,1,0:T(8,128)(2,1)}, u32[]{:S(2)}, u32[]{:S(2)}) collective-permute-start(bf16[2,160,1024]{2,1,0:T(8,128)(2,1)} %get-tuple-element.313), channel_id=1, source_target_pairs={{0,6},{2,0},{4,2},{6,4},{1,3},{3,5},{5,7},{7,1},{8,14},{10,8},{12,... | collective-permute-start | bytes 1966088 | tf_op jit(solution)/shard_map/ppermute | solution.py:29
  197.6 35.0 %collective-permute-start.30 = (bf16[2,160,1024]{2,1,0:T(8,128)(2,1)}, bf16[2,160,1024]{2,1,0:T(8,128)(2,1)}, u32[]{:S(2)}, u32[]{:S(2)}) collective-permute-start(bf16[2,160,1024]{2,1,0:T(8,128)(2,1)} %get-tuple-element.314), channel_id=1, source_target_pairs={{0,4},{2,6},{4,0},{6,2},{1,5},{3,7},{5,1},{7,3},{8,12},{10,14},{12... | collective-permute-start | bytes 1966088 | tf_op jit(solution)/shard_map/ppermute | solution.py:29
  197.6 38.9 %collective-permute-start.70 = (bf16[2,1024,128]{2,1,0:T(8,128)(2,1)}, bf16[2,1024,128]{2,1,0:T(8,128)(2,1)}, u32[]{:S(2)}, u32[]{:S(2)}) collective-permute-start(bf16[2,1024,128]{2,1,0:T(8,128)(2,1)} %get-tuple-element.395), channel_id=1, source_target_pairs={{0,64},{32,96},{64,0},{96,32},{1,65},{33,97},{65,1},{97,33},{2,66}... | collective-permute-start | bytes 1572872 | tf_op jit(solution)/shard_map/ppermute | solution.py:29
  213.1 32.2 %collective-permute-start.58 = (bf16[2,1152,128]{2,1,0:T(8,128)(2,1)}, bf16[2,1152,128]{2,1,0:T(8,128)(2,1)}, u32[]{:S(2)}, u32[]{:S(2)}) collective-permute-start(bf16[2,1152,128]{2,1,0:T(8,128)(2,1)} %get-tuple-element.377), channel_id=1, source_target_pairs={{0,4},{2,6},{4,0},{6,2},{1,5},{3,7},{5,1},{7,3},{8,12},{10,14},{12... | collective-permute-start | bytes 1769480 | tf_op jit(solution)/shard_map/ppermute | solution.py:29
  213.2 47.2 %collective-permute-start.64 = (bf16[2,1152,128]{2,1,0:T(8,128)(2,1)}, bf16[2,1152,128]{2,1,0:T(8,128)(2,1)S(1)}, u32[]{:S(2)}, u32[]{:S(2)}) collective-permute-start(bf16[2,1152,128]{2,1,0:T(8,128)(2,1)} %get-tuple-element.386), channel_id=1, source_target_pairs={{0,8},{16,24},{8,0},{24,16},{1,9},{17,25},{9,1},{25,17},{2,10},{18... | collective-permute-start | bytes 1769480 | tf_op jit(solution)/shard_map/ppermute | solution.py:29
  232.6 24.7 %collective-permute-start.31 = (bf16[2,40,1152]{2,1,0:T(8,128)(2,1)}, bf16[2,40,1152]{2,1,0:T(8,128)(2,1)}, u32[]{:S(2)}, u32[]{:S(2)}) collective-permute-start(bf16[2,40,1152]{2,1,0:T(8,128)(2,1)} %get-tuple-element.301), channel_id=1, source_target_pairs={{0,32},{32,64},{64,96},{96,0},{1,97},{33,1},{65,33},{97,65},{2,34}... | collective-permute-start | bytes 552968 | tf_op jit(solution)/shard_map/ppermute | solution.py:29
  232.6 24.7 %collective-permute-start.32 = (bf16[2,40,1152]{2,1,0:T(8,128)(2,1)}, bf16[2,40,1152]{2,1,0:T(8,128)(2,1)S(1)}, u32[]{:S(2)}, u32[]{:S(2)}) collective-permute-start(bf16[2,40,1152]{2,1,0:T(8,128)(2,1)} %get-tuple-element.308), channel_id=1, source_target_pairs={{0,2},{2,4},{4,6},{6,0},{1,7},{3,1},{5,3},{7,5},{8,10},{10,12},{12... | collective-permute-start | bytes 552968 | tf_op jit(solution)/shard_map/ppermute | solution.py:29
  236.5 17.7 %collective-permute-start.33 = (bf16[2,40,1024]{2,1,0:T(8,128)(2,1)}, bf16[2,40,1024]{2,1,0:T(8,128)(2,1)S(1)}, u32[]{:S(2)}, u32[]{:S(2)}) collective-permute-start(bf16[2,40,1024]{2,1,0:T(8,128)(2,1)} %get-tuple-element.315), channel_id=1, source_target_pairs={{0,16},{16,8},{8,24},{24,0},{1,25},{17,1},{9,17},{25,9},{2,18},{18... | collective-permute-start | bytes 491528 | tf_op jit(solution)/shard_map/ppermute | solution.py:29
  245.4 60.4 %collective-permute-start.71 = (bf16[4,1024,128]{2,1,0:T(8,128)(2,1)S(1)}, bf16[4,1024,128]{2,1,0:T(8,128)(2,1)S(1)}, u32[]{:S(2)}, u32[]{:S(2)}) collective-permute-start(bf16[4,1024,128]{2,1,0:T(8,128)(2,1)S(1)} %pad_maximum_fusion.5), channel_id=1, source_target_pairs={{0,1},{1,0},{2,3},{3,2},{4,5},{5,4},{6,7},{7,6},{8,9},{9,8},{10,11... | collective-permute-start | bytes 3145736 | tf_op jit(solution)/shard_map/ppermute | solution.py:33
  260.4 45.4 %collective-permute-start.59 = (bf16[4,1152,128]{2,1,0:T(8,128)(2,1)S(1)}, bf16[4,1152,128]{2,1,0:T(8,128)(2,1)S(1)}, u32[]{:S(2)}, u32[]{:S(2)}) collective-permute-start(bf16[4,1152,128]{2,1,0:T(8,128)(2,1)S(1)} %pad_maximum_fusion.3), channel_id=1, source_target_pairs={{0,1},{1,0},{2,3},{3,2},{4,5},{5,4},{6,7},{7,6},{8,9},{9,8},{10,11... | collective-permute-start | bytes 3538952 | tf_op jit(solution)/shard_map/ppermute | solution.py:33
  290.2 13.7 %collective-permute-start.49 = (bf16[4,40,1152]{2,1,0:T(8,128)(2,1)S(1)}, bf16[4,40,1152]{2,1,0:T(8,128)(2,1)S(1)}, u32[]{:S(2)}, u32[]{:S(2)}) collective-permute-start(bf16[4,40,1152]{2,1,0:T(8,128)(2,1)S(1)} %pad_maximum_fusion.6.rest_0_), channel_id=1, source_target_pairs={{0,16},{16,8},{8,24},{24,0},{1,25},{17,1},{9,17},{25,9},{2,18},{18... | collective-permute-start | bytes 1105928 | tf_op jit(solution)/shard_map/ppermute | solution.py:29
  292.6 11.2 %collective-permute-start.50 = (bf16[4,40,1152]{2,1,0:T(8,128)(2,1)S(1)}, bf16[4,40,1152]{2,1,0:T(8,128)(2,1)S(1)}, u32[]{:S(2)}, u32[]{:S(2)}) collective-permute-start(bf16[4,40,1152]{2,1,0:T(8,128)(2,1)S(1)} %pad_maximum_fusion.7.rest_0_), channel_id=1, source_target_pairs={{0,32},{32,64},{64,96},{96,0},{1,97},{33,1},{65,33},{97,65},{2,34}... | collective-permute-start | bytes 1105928 | tf_op jit(solution)/shard_map/ppermute | solution.py:29
  296.6 37.6 %collective-permute-start.65 = (bf16[4,1152,128]{2,1,0:T(8,128)(2,1)S(1)}, bf16[4,1152,128]{2,1,0:T(8,128)(2,1)}, u32[]{:S(2)}, u32[]{:S(2)}) collective-permute-start(bf16[4,1152,128]{2,1,0:T(8,128)(2,1)S(1)} %pad_maximum_fusion.4), channel_id=1, source_target_pairs={{0,1},{1,0},{2,3},{3,2},{4,5},{5,4},{6,7},{7,6},{8,9},{9,8},{10,11... | collective-permute-start | bytes 3538952 | tf_op jit(solution)/shard_map/ppermute | solution.py:33
  303.8 14.6 %collective-permute-start.67 = (bf16[4,40,1024]{2,1,0:T(8,128)(2,1)S(1)}, bf16[4,40,1024]{2,1,0:T(8,128)(2,1)S(1)}, u32[]{:S(2)}, u32[]{:S(2)}) collective-permute-start(bf16[4,40,1024]{2,1,0:T(8,128)(2,1)S(1)} %pad_maximum_fusion.10.rest_0_), channel_id=1, source_target_pairs={{0,6},{2,0},{4,2},{6,4},{1,3},{3,5},{5,7},{7,1},{8,14},{10,8},{12,... | collective-permute-start | bytes 983048 | tf_op jit(solution)/shard_map/ppermute | solution.py:29
  303.8 14.6 %collective-permute-start.68 = (bf16[4,40,1024]{2,1,0:T(8,128)(2,1)S(1)}, bf16[4,40,1024]{2,1,0:T(8,128)(2,1)S(1)}, u32[]{:S(2)}, u32[]{:S(2)}) collective-permute-start(bf16[4,40,1024]{2,1,0:T(8,128)(2,1)S(1)} %pad_maximum_fusion.10.rest_0_), channel_id=1, source_target_pairs={{0,4},{2,6},{4,0},{6,2},{1,5},{3,7},{5,1},{7,3},{8,12},{10,14},{12... | collective-permute-start | bytes 983048 | tf_op jit(solution)/shard_map/ppermute | solution.py:29
  305.8 21.7 %collective-permute-start.52 = (bf16[4,40,1152]{2,1,0:T(8,128)(2,1)S(1)}, bf16[4,40,1152]{2,1,0:T(8,128)(2,1)S(1)}, u32[]{:S(2)}, u32[]{:S(2)}) collective-permute-start(bf16[4,40,1152]{2,1,0:T(8,128)(2,1)S(1)} %pad_maximum_fusion.6.rest_0_), channel_id=1, source_target_pairs={{0,24},{16,0},{8,16},{24,8},{1,17},{17,9},{9,25},{25,1},{2,26},{18... | collective-permute-start | bytes 1105928 | tf_op jit(solution)/shard_map/ppermute | solution.py:29
  305.8 21.8 %collective-permute-start.53 = (bf16[4,40,1152]{2,1,0:T(8,128)(2,1)S(1)}, bf16[4,40,1152]{2,1,0:T(8,128)(2,1)}, u32[]{:S(2)}, u32[]{:S(2)}) collective-permute-start(bf16[4,40,1152]{2,1,0:T(8,128)(2,1)S(1)} %pad_maximum_fusion.6.rest_0_), channel_id=1, source_target_pairs={{0,8},{16,24},{8,0},{24,16},{1,9},{17,25},{9,1},{25,17},{2,10},{18... | collective-permute-start | bytes 1105928 | tf_op jit(solution)/shard_map/ppermute | solution.py:29
  318.4 15.9 %collective-permute-start.61 = (bf16[4,40,1152]{2,1,0:T(8,128)(2,1)S(1)}, bf16[4,40,1152]{2,1,0:T(8,128)(2,1)S(1)}, u32[]{:S(2)}, u32[]{:S(2)}) collective-permute-start(bf16[4,40,1152]{2,1,0:T(8,128)(2,1)S(1)} %pad_maximum_fusion.7.rest_0_), channel_id=1, source_target_pairs={{0,96},{32,0},{64,32},{96,64},{1,33},{33,65},{65,97},{97,1},{2,98}... | collective-permute-start | bytes 1105928 | tf_op jit(solution)/shard_map/ppermute | solution.py:29
  319.2 15.3 %collective-permute-start.62 = (bf16[4,40,1152]{2,1,0:T(8,128)(2,1)S(1)}, bf16[4,40,1152]{2,1,0:T(8,128)(2,1)}, u32[]{:S(2)}, u32[]{:S(2)}) collective-permute-start(bf16[4,40,1152]{2,1,0:T(8,128)(2,1)S(1)} %pad_maximum_fusion.7.rest_0_), channel_id=1, source_target_pairs={{0,64},{32,96},{64,0},{96,32},{1,65},{33,97},{65,1},{97,33},{2,66}... | collective-permute-start | bytes 1105928 | tf_op jit(solution)/shard_map/ppermute | solution.py:29
  327.5 13.8 %collective-permute-start.72 = (bf16[4,640,128]{2,1,0:T(8,128)(2,1)}, bf16[4,640,128]{2,1,0:T(8,128)(2,1)S(1)}, u32[]{:S(2)}, u32[]{:S(2)}) collective-permute-start(bf16[4,640,128]{2,1,0:T(8,128)(2,1)} %get-tuple-element.397), channel_id=1, source_target_pairs={{0,1},{1,0},{2,3},{3,2},{4,5},{5,4},{6,7},{7,6},{8,9},{9,8},{10,11... | collective-permute-start | bytes 1966088 | tf_op jit(solution)/shard_map/ppermute | solution.py:33
  365.3 11.7 %collective-permute-start.85 = (bf16[640,128]{1,0:T(8,128)(2,1)S(1)}, bf16[640,128]{1,0:T(8,128)(2,1)S(1)}, u32[]{:S(2)}, u32[]{:S(2)}) collective-permute-start(bf16[640,128]{1,0:T(8,128)(2,1)S(1)} %bitcast.349), channel_id=1, source_target_pairs={{0,16},{16,8},{8,24},{24,0},{1,25},{17,1},{9,17},{25,9},{2,18},{18... | collective-permute-start | bytes 491528 | tf_op jit(solution)/shard_map/ppermute | solution.py:29
  365.9 12.9 %collective-permute-start.86 = (bf16[640,128]{1,0:T(8,128)(2,1)S(1)}, bf16[640,128]{1,0:T(8,128)(2,1)S(1)}, u32[]{:S(2)}, u32[]{:S(2)}) collective-permute-start(bf16[640,128]{1,0:T(8,128)(2,1)S(1)} %bitcast.350), channel_id=1, source_target_pairs={{0,24},{16,0},{8,16},{24,8},{1,17},{17,9},{9,25},{25,1},{2,26},{18... | collective-permute-start | bytes 491528 | tf_op jit(solution)/shard_map/ppermute | solution.py:29
  366.9 12.0 %collective-permute-start.87 = (bf16[640,128]{1,0:T(8,128)(2,1)S(1)}, bf16[640,128]{1,0:T(8,128)(2,1)S(1)}, u32[]{:S(2)}, u32[]{:S(2)}) collective-permute-start(bf16[640,128]{1,0:T(8,128)(2,1)S(1)} %bitcast.352), channel_id=1, source_target_pairs={{0,8},{16,24},{8,0},{24,16},{1,9},{17,25},{9,1},{25,17},{2,10},{18... | collective-permute-start | bytes 491528 | tf_op jit(solution)/shard_map/ppermute | solution.py:29
  402.0 29.0 %collective-permute-start.92 = (bf16[2,160,1152]{2,1,0:T(8,128)(2,1)}, bf16[2,160,1152]{2,1,0:T(8,128)(2,1)S(1)}, u32[]{:S(2)}, u32[]{:S(2)}) collective-permute-start(bf16[2,160,1152]{2,1,0:T(8,128)(2,1)} %get-tuple-element.420), channel_id=1, source_target_pairs={{0,16},{16,8},{8,24},{24,0},{1,25},{17,1},{9,17},{25,9},{2,18},{18... | collective-permute-start | bytes 2211848 | tf_op jit(solution)/shard_map/ppermute | solution.py:29
  412.4 18.7 %collective-permute-start.93 = (bf16[2,160,1152]{2,1,0:T(8,128)(2,1)}, bf16[2,160,1152]{2,1,0:T(8,128)(2,1)S(1)}, u32[]{:S(2)}, u32[]{:S(2)}) collective-permute-start(bf16[2,160,1152]{2,1,0:T(8,128)(2,1)} %get-tuple-element.423), channel_id=1, source_target_pairs={{0,32},{32,64},{64,96},{96,0},{1,97},{33,1},{65,33},{97,65},{2,34}... | collective-permute-start | bytes 2211848 | tf_op jit(solution)/shard_map/ppermute | solution.py:29
  421.1 12.4 %collective-permute-start.95 = (bf16[2,160,1152]{2,1,0:T(8,128)(2,1)}, bf16[2,160,1152]{2,1,0:T(8,128)(2,1)S(1)}, u32[]{:S(2)}, u32[]{:S(2)}) collective-permute-start(bf16[2,160,1152]{2,1,0:T(8,128)(2,1)} %get-tuple-element.433), channel_id=1, source_target_pairs={{0,24},{16,0},{8,16},{24,8},{1,17},{17,9},{9,25},{25,1},{2,26},{18... | collective-permute-start | bytes 2211848 | tf_op jit(solution)/shard_map/ppermute | solution.py:29
  431.1 19.6 %collective-permute-start.96 = (bf16[2,160,1152]{2,1,0:T(8,128)(2,1)}, bf16[2,160,1152]{2,1,0:T(8,128)(2,1)}, u32[]{:S(2)}, u32[]{:S(2)}) collective-permute-start(bf16[2,160,1152]{2,1,0:T(8,128)(2,1)} %get-tuple-element.434), channel_id=1, source_target_pairs={{0,8},{16,24},{8,0},{24,16},{1,9},{17,25},{9,1},{25,17},{2,10},{18... | collective-permute-start | bytes 2211848 | tf_op jit(solution)/shard_map/ppermute | solution.py:29
  431.3 27.5 %collective-permute-start.97 = (bf16[2,160,1152]{2,1,0:T(8,128)(2,1)}, bf16[2,160,1152]{2,1,0:T(8,128)(2,1)S(1)}, u32[]{:S(2)}, u32[]{:S(2)}) collective-permute-start(bf16[2,160,1152]{2,1,0:T(8,128)(2,1)} %get-tuple-element.441), channel_id=1, source_target_pairs={{0,96},{32,0},{64,32},{96,64},{1,33},{33,65},{65,97},{97,1},{2,98}... | collective-permute-start | bytes 2211848 | tf_op jit(solution)/shard_map/ppermute | solution.py:29
  431.4 27.4 %collective-permute-start.98 = (bf16[2,160,1152]{2,1,0:T(8,128)(2,1)}, bf16[2,160,1152]{2,1,0:T(8,128)(2,1)}, u32[]{:S(2)}, u32[]{:S(2)}) collective-permute-start(bf16[2,160,1152]{2,1,0:T(8,128)(2,1)} %get-tuple-element.442), channel_id=1, source_target_pairs={{0,64},{32,96},{64,0},{96,32},{1,65},{33,97},{65,1},{97,33},{2,66}... | collective-permute-start | bytes 2211848 | tf_op jit(solution)/shard_map/ppermute | solution.py:29
  432.5 34.3 %collective-permute-start.99 = (bf16[2,160,1024]{2,1,0:T(8,128)(2,1)}, bf16[2,160,1024]{2,1,0:T(8,128)(2,1)}, u32[]{:S(2)}, u32[]{:S(2)}) collective-permute-start(bf16[2,160,1024]{2,1,0:T(8,128)(2,1)} %get-tuple-element.448), channel_id=1, source_target_pairs={{0,6},{2,0},{4,2},{6,4},{1,3},{3,5},{5,7},{7,1},{8,14},{10,8},{12,... | collective-permute-start | bytes 1966088 | tf_op jit(solution)/shard_map/ppermute | solution.py:29
  433.5 33.3 %collective-permute-start.100 = (bf16[2,160,1024]{2,1,0:T(8,128)(2,1)}, bf16[2,160,1024]{2,1,0:T(8,128)(2,1)}, u32[]{:S(2)}, u32[]{:S(2)}) collective-permute-start(bf16[2,160,1024]{2,1,0:T(8,128)(2,1)} %get-tuple-element.449), channel_id=1, source_target_pairs={{0,4},{2,6},{4,0},{6,2},{1,5},{3,7},{5,1},{7,3},{8,12},{10,14},{12... | collective-permute-start | bytes 1966088 | tf_op jit(solution)/shard_map/ppermute | solution.py:29
  455.6 20.1 %collective-permute-start.101 = (bf16[2,40,1152]{2,1,0:T(8,128)(2,1)}, bf16[2,40,1152]{2,1,0:T(8,128)(2,1)S(1)}, u32[]{:S(2)}, u32[]{:S(2)}) collective-permute-start(bf16[2,40,1152]{2,1,0:T(8,128)(2,1)} %get-tuple-element.436), channel_id=1, source_target_pairs={{0,32},{32,64},{64,96},{96,0},{1,97},{33,1},{65,33},{97,65},{2,34}... | collective-permute-start | bytes 552968 | tf_op jit(solution)/shard_map/ppermute | solution.py:29
  464.6 11.1 %collective-permute-start.102 = (bf16[2,40,1152]{2,1,0:T(8,128)(2,1)}, bf16[2,40,1152]{2,1,0:T(8,128)(2,1)S(1)}, u32[]{:S(2)}, u32[]{:S(2)}) collective-permute-start(bf16[2,40,1152]{2,1,0:T(8,128)(2,1)} %get-tuple-element.443), channel_id=1, source_target_pairs={{0,2},{2,4},{4,6},{6,0},{1,7},{3,1},{5,3},{7,5},{8,10},{10,12},{12... | collective-permute-start | bytes 552968 | tf_op jit(solution)/shard_map/ppermute | solution.py:29
  505.1 12.9 %collective-permute-start.128 = (bf16[4,40,1024]{2,1,0:T(8,128)(2,1)S(1)}, bf16[4,40,1024]{2,1,0:T(8,128)(2,1)S(1)}, u32[]{:S(2)}, u32[]{:S(2)}) collective-permute-start(bf16[4,40,1024]{2,1,0:T(8,128)(2,1)S(1)} %pad_maximum_fusion.11.rest_0_), channel_id=1, source_target_pairs={{0,6},{2,0},{4,2},{6,4},{1,3},{3,5},{5,7},{7,1},{8,14},{10,8},{12,... | collective-permute-start | bytes 983048 | tf_op jit(solution)/shard_map/ppermute | solution.py:29
  512.9 25.9 %collective-permute-start.122 = (bf16[4,40,1152]{2,1,0:T(8,128)(2,1)S(1)}, bf16[4,40,1152]{2,1,0:T(8,128)(2,1)S(1)}, u32[]{:S(2)}, u32[]{:S(2)}) collective-permute-start(bf16[4,40,1152]{2,1,0:T(8,128)(2,1)S(1)} %pad_maximum_fusion.8.rest_0_), channel_id=1, source_target_pairs={{0,24},{16,0},{8,16},{24,8},{1,17},{17,9},{9,25},{25,1},{2,26},{18... | collective-permute-start | bytes 1105928 | tf_op jit(solution)/shard_map/ppermute | solution.py:29
  512.9 25.9 %collective-permute-start.123 = (bf16[4,40,1152]{2,1,0:T(8,128)(2,1)S(1)}, bf16[4,40,1152]{2,1,0:T(8,128)(2,1)S(1)}, u32[]{:S(2)}, u32[]{:S(2)}) collective-permute-start(bf16[4,40,1152]{2,1,0:T(8,128)(2,1)S(1)} %pad_maximum_fusion.8.rest_0_), channel_id=1, source_target_pairs={{0,8},{16,24},{8,0},{24,16},{1,9},{17,25},{9,1},{25,17},{2,10},{18... | collective-permute-start | bytes 1105928 | tf_op jit(solution)/shard_map/ppermute | solution.py:29
  516.1 30.1 %collective-permute-start.125 = (bf16[4,40,1152]{2,1,0:T(8,128)(2,1)S(1)}, bf16[4,40,1152]{2,1,0:T(8,128)(2,1)}, u32[]{:S(2)}, u32[]{:S(2)}) collective-permute-start(bf16[4,40,1152]{2,1,0:T(8,128)(2,1)S(1)} %pad_maximum_fusion.9.rest_0_), channel_id=1, source_target_pairs={{0,96},{32,0},{64,32},{96,64},{1,33},{33,65},{65,97},{97,1},{2,98}... | collective-permute-start | bytes 1105928 | tf_op jit(solution)/shard_map/ppermute | solution.py:29
  517.9 28.2 %collective-permute-start.126 = (bf16[4,40,1152]{2,1,0:T(8,128)(2,1)S(1)}, bf16[4,40,1152]{2,1,0:T(8,128)(2,1)}, u32[]{:S(2)}, u32[]{:S(2)}) collective-permute-start(bf16[4,40,1152]{2,1,0:T(8,128)(2,1)S(1)} %pad_maximum_fusion.9.rest_0_), channel_id=1, source_target_pairs={{0,64},{32,96},{64,0},{96,32},{1,65},{33,97},{65,1},{97,33},{2,66}... | collective-permute-start | bytes 1105928 | tf_op jit(solution)/shard_map/ppermute | solution.py:29
  527.3 25.2 %collective-permute-start.130 = (bf16[4,640,128]{2,1,0:T(8,128)(2,1)}, bf16[4,640,128]{2,1,0:T(8,128)(2,1)S(1)}, u32[]{:S(2)}, u32[]{:S(2)}) collective-permute-start(bf16[4,640,128]{2,1,0:T(8,128)(2,1)} %get-tuple-element.496), channel_id=1, source_target_pairs={{0,1},{1,0},{2,3},{3,2},{4,5},{5,4},{6,7},{7,6},{8,9},{9,8},{10,11... | collective-permute-start | bytes 1966088 | tf_op jit(solution)/shard_map/ppermute | solution.py:33
  (201 other events, 2637.4 us)

commit v2 on v1

--- a/solution.py
+++ b/solution.py
@@ -84,8 +84,8 @@
 def pack_down(where, down, begin, width):
     columns = down.shape[1]
     base = begin // width
-    tile = tile_of(width)
-    tiles = width // tile
+    tiles = 2
+    tile = width // tiles
 
     def body(where_ref, *rest):
         ins, outs = rest[:8], rest[8:]
@@ -118,26 +118,26 @@
 
 
 def tile_of(width):
-    return width // 3 if width % 384 == 0 else width // 2
-
-
-def gate_up_products(part, where, mine, others, weights):
+    return width
+
+
+def gate_up_products(where, mine, weights):
     own_weights, other_weights = weights
-    rows, own = mine[0].shape
+    _, rows, own = mine[0].shape
     width = other_weights.shape[3]
     quarter = rows // 4
     depth = 8 * own
     tile = tile_of(width)
 
     def body(where_ref, *rest):
-        mine_refs, others_ref, weight_refs, other_ref = rest[:4], rest[4], rest[5:9], rest[9]
-        outs, joined, sums = rest[10:14], rest[14], rest[15]
+        mine_refs, weight_refs, other_ref = rest[:4], rest[4:8], rest[8]
+        outs, joined, sums = rest[9:13], rest[13], rest[14]
 
         @pl.when((pl.program_id(0) == 0) & (pl.program_id(1) == 0))
         def _():
             for slot in range(4):
-                joined[:, own * slot : own * (slot + 1)] = mine_refs[slot][...]
-                joined[:, own * (4 + slot) : own * (5 + slot)] = others_ref[slot]
+                joined[:, own * slot : own * (slot + 1)] = mine_refs[slot][0]
+                joined[:, own * (4 + slot) : own * (5 + slot)] = mine_refs[FLIP[slot]][1]
 
         weight = jnp.concatenate([ref[0, 0] for ref in weight_refs] + [other_ref[slot, 0] for slot in range(4)], axis=0)
         product = jnp.dot(joined[...], weight, preferred_element_type=jnp.float32)
@@ -150,8 +150,7 @@
         grid=(2, width // tile),
         out_shape=[jax.ShapeDtypeStruct((2, quarter, width), jnp.bfloat16)] * 4,
         in_specs=[smem()]
-        + [pl.BlockSpec((rows, own), lambda g, j: (0, 0))] * 4
-        + [pl.BlockSpec((4, rows, own), lambda g, j: (part, 0, 0))]
+        + [pl.BlockSpec((2, rows, own), lambda g, j: (0, 0, 0))] * 4
         + [pl.BlockSpec((1, 1, own, tile), lambda g, j: (0, g, 0, j))] * 4
         + [pl.BlockSpec((4, 1, own, tile), lambda g, j: (0, g, 0, j))],
         out_specs=[pl.BlockSpec((1, quarter, tile), lambda g, j: (g, 0, j))] * 4,
@@ -166,7 +165,7 @@
             transcendentals=0,
         ),
         name="gate_up_products",
-    )(where, *mine, others, *own_weights, other_weights)
+    )(where, *mine, *own_weights, other_weights)
 
 
 def first_sums(where, terms, kept):
@@ -258,16 +257,20 @@
     return (jax.nn.silu(gate_sum) * up_sum).astype(jnp.bfloat16)
 
 
+def core_pair(rows):
+    return jnp.stack([rows, core_swap(rows)])
+
+
 def gather_rows(rows):
-    mine = [[rows, None, None, None] for _ in PLAN]
+    pair = core_pair(rows)
+    mine = [[pair, None, None, None] for _ in PLAN]
     for slot in (1, 2, 3):
         for at, (cross, _, _) in enumerate(PLAN):
-            mine[at][slot] = ring_permute(rows, cross, slot)
+            mine[at][slot] = ring_permute(pair, cross, slot)
     return mine
 
 
 def exchange_all(values, rings):
-    result = [[value[0], None, None, None] for value in values]
     first = [ring_permute(value[1], ring, 1) for value, ring in zip(values, rings)]
     later = lax.optimization_barrier([value[1:] for value in values])
     second = [ring_permute(value[1], ring, 2) for value, ring in zip(later, rings)]
@@ -276,17 +279,25 @@
     return [[value[0], *slots] for value, *slots in zip(values, first, second, third)]
 
 
+def in_turn(steps, ring, flying=2):
+    results = []
+    for value, slot in steps:
+        if len(results) >= flying:
+            value, results[-flying] = lax.optimization_barrier((value, results[-flying]))
+        results.append(ring_permute(value, ring, slot))
+    return results
+
+
 def share_cores(received):
     return received, core_swap(jnp.stack([value[1] for value in received]))
 
 
-def block_update(mine, others, wheres, gate_up, down):
-    rows = mine[0][0].shape[0]
+def block_update(mine, wheres, gate_up, down):
+    rows = mine[0][0].shape[1]
     kept = jnp.bfloat16 if rows >= 256 else jnp.float32
     cross, first, second = zip(*PLAN)
     parts = [
-        gate_up_products(at, where, mine[at], others, weights)
-        for at, (where, weights) in enumerate(zip(wheres, gate_up))
+        gate_up_products(where, values, weights) for where, values, weights in zip(wheres, mine, gate_up)
     ]
     parts = exchange_all(parts, first)
     sums = [first_sums(where, terms, kept) for where, terms in zip(wheres, parts)]
@@ -322,9 +333,9 @@
     tensor = ("xh", "z", "c")
     own = down_weight.shape[1]
 
-    units = gate_weight.shape[1] // (8 * LANES)
-    widths = [(units // 3 + (1 if at < units % 3 else 0)) * LANES for at in range(3)]
-    begins = [8 * sum(widths[:at]) for at in range(3)]
+    units, parts = gate_weight.shape[1] // (8 * LANES), len(PLAN)
+    widths = [(units // parts + (1 if at < units % parts else 0)) * LANES for at in range(parts)]
+    begins = [8 * sum(widths[:at]) for at in range(parts)]
 
     wheres = []
     for cross, first, second in PLAN:
@@ -336,27 +347,35 @@
     cross = [rings[0] for rings in PLAN]
     packing = list(zip(wheres, begins, widths))
     packed = [pack_gate_up(where, gate_weight, up_weight, *at) for where, *at in packing]
-    received = exchange_all(packed, cross)
-
+    packed_down = [pack_down(where, down_weight, *at) for where, *at in packing]
+    weights = [
+        in_turn([(gates[slot], slot) for slot in (1, 2, 3)] + [(downs[slot], slot) for slot in (1, 2, 3)], ring)
+        for ring, gates, downs in zip(cross, packed, packed_down)
+    ]
+
+    prompt, decode_in, weights[0][0] = lax.optimization_barrier((prompt, decode_in, weights[0][0]))
     count, decode_count = prompt.shape[0], decode_in.shape[0]
-    block = count + decode_count
+    block, span = count + decode_count, count // STEPS
     both = jnp.concatenate([prompt, decode_in], axis=0)
     both = both.reshape(block, 16, own).swapaxes(0, 1)
     both = lax.all_to_all(both, tensor, split_axis=0, concat_axis=0, tiled=True)
     prompt_rows, state = both[:, :count], both[:, count:]
 
-    packed = [pack_down(where, down_weight, *at) for where, *at in packing]
-    gate_up = [share_cores(values) for values in received]
-    received, packed = lax.optimization_barrier((received, packed))
-    down = [share_cores(values) for values in exchange_all(packed, cross)]
-
-    span = count // STEPS
+    def turn_rows(turn):
+        return jnp.concatenate([prompt_rows[:, turn * span : (turn + 1) * span], state], axis=1)
+
+    rows = turn_rows(0)
+    pair = core_pair(rows.reshape(-1, own))
+    mine = [[pair, *in_turn([(pair, slot) for slot in (1, 2, 3)], ring, 1)] for ring in cross]
+    gate_up = [share_cores([gates[0], *results[:3]]) for gates, results in zip(packed, weights)]
+    down = [share_cores([downs[0], *results[3:]]) for downs, results in zip(packed_down, weights)]
+
     outs = []
     for turn in range(STEPS):
-        rows = jnp.concatenate([prompt_rows[:, turn * span : (turn + 1) * span], state], axis=1)
-        mine = gather_rows(rows.reshape(-1, own))
-        others = core_swap(jnp.stack([value for part in mine for value in part]))
-        update = block_update(mine, others, wheres, gate_up, down).reshape(rows.shape)
+        if turn > 0:
+            rows = turn_rows(turn)
+            mine = gather_rows(rows.reshape(-1, own))
+        update = block_update(mine, wheres, gate_up, down).reshape(rows.shape)
         outs.append(update[:, :span].astype(jnp.bfloat16))
         state = (state.astype(jnp.float32) + update[:, span:]).astype(jnp.bfloat16)
 

time: 602 us -> 579 us (0.962)
  Pallas kernels: 143 us -> 121 us
  starting transfers between devices: 217 us -> 208 us
    ppermute x14, starting transfers between devices: 42 us -> 24.9 us  [core_swap(): return lax.ppermute(value, 'c', [(0, 1), (1, 0)])]
    ppermute x126, starting transfers between devices: 166 us -> 179 us  [ring_permute(): return lax.ppermute(value, RINGS[ring] + ('c',), pairs)]
    pallas_call x6, Pallas kernels: 27.7 us -> 16.7 us  [first_sums(): pl.pallas_call(body, grid=(2, width // tile), out_shape=[jax.ShapeDtypeSt...]
    pallas_call x6, Pallas kernels: 51.5 us -> 43.4 us  [gate_up_products(): pl.pallas_call(body, grid=(2, width // tile), out_shape=[jax.ShapeDtypeSt...]
    ppermute x126, waiting for transfers between devices: 166 us -> 173 us  [ring_permute(): return lax.ppermute(value, RINGS[ring] + ('c',), pairs)]
    slice x36 -> x35, local copies, waits for them, and re-layouts: 6.58 us -> 12.6 us  [share_cores(): return (received, core_swap(jnp.stack([value[1] for value in received])))]
    unnamed x246 -> x224, local copies, waits for them, and re-layouts: 13.4 us -> 11.1 us
  transfers between devices with their start and end apart: 141 -> 141, of which waited for: 50 -> 44; matrix products, arithmetic and copies ran while one was open for 5% -> 5% of each run, Pallas kernels for 23% -> 20%
where the time goes in v2:
time: 579 us; the launch traced here: 569 us
  starting transfers between devices  208 us (36%)
  waiting for transfers between devices  176 us (30%)
  Pallas kernels  121 us (21%)
  local copies, waits for them, and re-layouts  28.7 us (5%)
  blocking collectives  18.4 us (3%)
  other arithmetic  13 us (2%)
    ppermute x126, starting transfers between devices, ring_permute(): return lax.ppermute(value, RINGS[ring] + ('c',), pairs)  179 us
    ppermute x126, waiting for transfers between devices, ring_permute(): return lax.ppermute(value, RINGS[ring] + ('c',), pairs)  173 us
    pallas_call x6, Pallas kernels, gate_up_products(): pl.pallas_call(body, grid=(2, width // tile), out_shape=[jax.ShapeDtypeSt...  43.4 us
    pallas_call x6, Pallas kernels, down_products(): pl.pallas_call(body, grid=(1,), out_shape=[jax.ShapeDtypeStruct((rows, ow...  33.3 us
    ppermute x14, starting transfers between devices, core_swap(): return lax.ppermute(value, 'c', [(0, 1), (1, 0)])  24.9 us
    all_to_all x1, blocking collectives, shards(): both = lax.all_to_all(both, tensor, split_axis=0, concat_axis=0, tiled=True)  18.4 us
    pallas_call x3, Pallas kernels, pack_gate_up(): pl.pallas_call(body, out_shape=[jax.ShapeDtypeStruct((2, 2, rows, width),...  17.1 us
    pallas_call x6, Pallas kernels, first_sums(): pl.pallas_call(body, grid=(2, width // tile), out_shape=[jax.ShapeDtypeSt...  16.7 us
  transfers between devices with their start and end apart: 141, of which 44 were waited for; matrix products, arithmetic and copies ran while one was open for 5% of the time, Pallas kernels for 20%

profile of v2, /device:TPU:1, one launch (start us, length us, event | category | flops | bytes accessed | tf_op | source)
XLA Modules:
  0.0 568.9 jit_solution(13858980057932572252)
XLA Ops:
  1.6 5.5 pack_gate_up.5
  7.0 3.6 collective-permute-start.18
  11.4 5.8 %pack_gate_up.3 = (bf16[2,2,128,1152]{3,2,1,0:T(8,128)(2,1)}, bf16[2,2,128,1152]{3,2,1,0:T(8,128)(2,1)}, bf16[2,2,128,1152]{3,2,1,0:T(8,128)(2,1)}, bf16[2,2,128,1152]{3,2,1,0:T(8,128)(2,1)}) custom-call(s32[21]{0:T(128)} %stack.243.where_ref, bf16[128,26624]{1,0:T(8,128)(2,1)} %rest_3_.10, bf16[128,26624]{1,0:T(8,128)(2,1)} %rest_3_.10, ...), custom_call_target="tpu_custom_call" | custom-call | bytes 9437184 | tf_op jit(solution)/shard_map/pack_gate_up/pallas_call | solution.py:69
  17.2 3.8 collective-permute-start
  21.6 5.8 %pack_gate_up.4 = (bf16[2,2,128,1152]{3,2,1,0:T(8,128)(2,1)}, bf16[2,2,128,1152]{3,2,1,0:T(8,128)(2,1)}, bf16[2,2,128,1152]{3,2,1,0:T(8,128)(2,1)}, bf16[2,2,128,1152]{3,2,1,0:T(8,128)(2,1)}) custom-call(s32[21]{0:T(128)} %stack.250.where_ref, bf16[128,26624]{1,0:T(8,128)(2,1)} %rest_3_.10, bf16[128,26624]{1,0:T(8,128)(2,1)} %rest_3_.10, ...), custom_call_target="tpu_custom_call" | custom-call | bytes 9437184 | tf_op jit(solution)/shard_map/pack_gate_up/pallas_call | solution.py:69
  31.0 6.4 %collective-permute-done.rest_5_ = bf16[2,2,128,1152]{3,2,1,0:T(8,128)(2,1)S(1)} collective-permute-done((bf16[2,2,128,1152]{3,2,1,0:T(8,128)(2,1)}, bf16[2,2,128,1152]{3,2,1,0:T(8,128)(2,1)S(1)}, u32[]{:S(2)}, u32[]{:S(2)}) %collective-permute-start) | collective-permute-done | bytes 1179680 | tf_op jit(solution)/shard_map/ppermute | solution.py:29
  37.4 15.2 %collective-permute-done.11.rest_5_ = bf16[2,2,128,1152]{3,2,1,0:T(8,128)(2,1)S(1)} collective-permute-done((bf16[2,2,128,1152]{3,2,1,0:T(8,128)(2,1)}, bf16[2,2,128,1152]{3,2,1,0:T(8,128)(2,1)S(1)}, u32[]{:S(2)}, u32[]{:S(2)}) %collective-permute-start.11) | collective-permute-done | bytes 1179680 | tf_op jit(solution)/shard_map/ppermute | solution.py:29
  52.6 15.3 %collective-permute-done.19.rest_6_ = bf16[2,2,128,1024]{3,2,1,0:T(8,128)(2,1)} collective-permute-done((bf16[2,2,128,1024]{3,2,1,0:T(8,128)(2,1)}, bf16[2,2,128,1024]{3,2,1,0:T(8,128)(2,1)}, u32[]{:S(2)}, u32[]{:S(2)}) %collective-permute-start.19) | collective-permute-done | bytes 1048608 | tf_op jit(solution)/shard_map/ppermute | solution.py:29
  68.4 3.6 pack_down.3
  72.1 3.7 pack_down.4
  75.8 3.5 pack_down.5
  84.6 4.1 all-to-all-start
  107.0 2.8 collective-permute-start.2
  111.1 3.6 collective-permute-start.8
  114.7 4.0 collective-permute-done.8.rest_1_
  122.6 3.3 collective-permute-done.3.rest_2_
  133.3 5.5 collective-permute-start.68
  138.8 3.0 collective-permute-start.10
  141.9 6.7 %gate_up_products.8 = (bf16[2,160,1024]{2,1,0:T(8,128)(2,1)}, bf16[2,160,1024]{2,1,0:T(8,128)(2,1)}, bf16[2,160,1024]{2,1,0:T(8,128)(2,1)}, bf16[2,160,1024]{2,1,0:T(8,128)(2,1)}) custom-call(s32[21]{0:T(128)} %stack.252.where_ref, bf16[2,640,128]{2,1,0:T(8,128)(2,1)} %copy-done.29, bf16[2,640,128]{2,1,0:T(8,128)(2,1)} %copy-done.88, ...), custom_call_target="tpu_custom_call" | custom-call | flops 2684354560 | bytes 8126464 | tf_op jit(solution)/shard_map/gate_up_products/pallas_call | solution.py:148
  151.3 7.5 %gate_up_products.6 = (bf16[2,160,1152]{2,1,0:T(8,128)(2,1)}, bf16[2,160,1152]{2,1,0:T(8,128)(2,1)}, bf16[2,160,1152]{2,1,0:T(8,128)(2,1)}, bf16[2,160,1152]{2,1,0:T(8,128)(2,1)}) custom-call(s32[21]{0:T(128)} %stack.243.where_ref, bf16[2,640,128]{2,1,0:T(8,128)(2,1)} %copy-done.29, bf16[2,640,128]{2,1,0:T(8,128)(2,1)} %copy-done.84, ...), custom_call_target="tpu_custom_call" | custom-call | flops 3019898880 | bytes 8978432 | tf_op jit(solution)/shard_map/gate_up_products/pallas_call | solution.py:148
  159.3 7.6 %gate_up_products.7 = (bf16[2,160,1152]{2,1,0:T(8,128)(2,1)}, bf16[2,160,1152]{2,1,0:T(8,128)(2,1)}, bf16[2,160,1152]{2,1,0:T(8,128)(2,1)}, bf16[2,160,1152]{2,1,0:T(8,128)(2,1)}) custom-call(s32[21]{0:T(128)} %stack.250.where_ref, bf16[2,640,128]{2,1,0:T(8,128)(2,1)} %copy-done.29, bf16[2,640,128]{2,1,0:T(8,128)(2,1)} %copy-done.82, ...), custom_call_target="tpu_custom_call" | custom-call | flops 3019898880 | bytes 8978432 | tf_op jit(solution)/shard_map/gate_up_products/pallas_call | solution.py:148
  167.7 2.8 collective-permute-start.56
  174.3 8.4 %collective-permute-done.23.rest_1_ = bf16[2,160,1152]{2,1,0:T(8,128)(2,1)S(1)} collective-permute-done((bf16[2,160,1152]{2,1,0:T(8,128)(2,1)}, bf16[2,160,1152]{2,1,0:T(8,128)(2,1)S(1)}, u32[]{:S(2)}, u32[]{:S(2)}) %collective-permute-start.23) | collective-permute-done | bytes 737312 | tf_op jit(solution)/shard_map/ppermute | solution.py:29
  187.4 8.6 %collective-permute-done.63.rest_7_ = bf16[2,1152,128]{2,1,0:T(8,128)(2,1)S(1)} collective-permute-done((bf16[2,1152,128]{2,1,0:T(8,128)(2,1)}, bf16[2,1152,128]{2,1,0:T(8,128)(2,1)S(1)}, u32[]{:S(2)}, u32[]{:S(2)}) %collective-permute-start.63) | collective-permute-done | bytes 589856 | tf_op jit(solution)/shard_map/ppermute | solution.py:29
  198.7 14.4 %collective-permute-start.69 = (bf16[2,1024,128]{2,1,0:T(8,128)(2,1)}, bf16[2,1024,128]{2,1,0:T(8,128)(2,1)}, u32[]{:S(2)}, u32[]{:S(2)}) collective-permute-start(bf16[2,1024,128]{2,1,0:T(8,128)(2,1)} %get-tuple-element.400), channel_id=1, source_target_pairs={{0,96},{32,0},{64,32},{96,64},{1,33},{33,65},{65,97},{97,1},{2,98}... | collective-permute-start | bytes 1572872 | tf_op jit(solution)/shard_map/ppermute | solution.py:29
  216.1 2.8 first_sums.6
  218.9 2.8 first_sums.7
  232.6 4.9 collective-permute-start.71
  238.7 4.2 collective-permute-start.39
  261.7 3.4 collective-permute-start.47
  265.2 2.9 collective-permute-start.48
  281.1 3.0 collective-permute-done.51.rest_1_
  284.1 6.4 %collective-permute-start.64 = (bf16[4,1152,128]{2,1,0:T(8,128)(2,1)S(1)}, bf16[4,1152,128]{2,1,0:T(8,128)(2,1)}, u32[]{:S(2)}, u32[]{:S(2)}) collective-permute-start(bf16[4,1152,128]{2,1,0:T(8,128)(2,1)S(1)} %pad_maximum_fusion.4), channel_id=1, source_target_pairs={{0,1},{1,0},{2,3},{3,2},{4,5},{5,4},{6,7},{7,6},{8,9},{9,8},{10,11... | collective-permute-start | bytes 3538952 | tf_op jit(solution)/shard_map/ppermute | solution.py:33
  294.4 10.7 %collective-permute-done.66.rest_2_ = bf16[4,40,1024]{2,1,0:T(8,128)(2,1)S(1)} collective-permute-done((bf16[4,40,1024]{2,1,0:T(8,128)(2,1)S(1)}, bf16[4,40,1024]{2,1,0:T(8,128)(2,1)S(1)}, u32[]{:S(2)}, u32[]{:S(2)}) %collective-permute-start.66) | collective-permute-done | bytes 327712 | tf_op jit(solution)/shard_map/ppermute | solution.py:29
  308.0 5.2 down_products.8
  314.7 5.7 down_products.6
  321.4 5.7 %down_products.7 = (bf16[640,128]{1,0:T(8,128)(2,1)}, bf16[640,128]{1,0:T(8,128)(2,1)}, bf16[640,128]{1,0:T(8,128)(2,1)}, bf16[640,128]{1,0:T(8,128)(2,1)}, bf16[4,640,128]{2,1,0:T(8,128)(2,1)}) custom-call(s32[21]{0:T(128)} %stack.250.where_ref, bf16[4,40,1152]{2,1,0:T(8,128)(2,1)} %copy-done.27, bf16[4,40,1152]{2,1,0:T(8,128)(2,1)} %copy-done.76, ...), custom_call_target="tpu_custom_call" | custom-call | flops 1509949440 | bytes 5144576 | tf_op jit(solution)/shard_map/down_products/pallas_call | solution.py:230
  327.7 2.8 collective-permute-start.75
  344.1 3.5 collective-permute-done.79
  356.8 4.8 collective-permute-done.83.rest_1_
  362.5 8.9 %collective-permute-done.84.rest_2_ = bf16[2,640,128]{2,1,0:T(8,128)(2,1)S(1)} collective-permute-done((bf16[2,640,128]{2,1,0:T(8,128)(2,1)S(1)}, bf16[2,640,128]{2,1,0:T(8,128)(2,1)S(1)}, u32[]{:S(2)}, u32[]{:S(2)}) %collective-permute-start.84) | collective-permute-done | bytes 327712 | tf_op jit(solution)/shard_map/ppermute | solution.py:29
  374.8 7.5 %gate_up_products.9 = (bf16[2,160,1152]{2,1,0:T(8,128)(2,1)}, bf16[2,160,1152]{2,1,0:T(8,128)(2,1)}, bf16[2,160,1152]{2,1,0:T(8,128)(2,1)}, bf16[2,160,1152]{2,1,0:T(8,128)(2,1)}) custom-call(s32[21]{0:T(128)} %stack.243.where_ref, bf16[2,640,128]{2,1,0:T(8,128)(2,1)} %copy-done.30, bf16[2,640,128]{2,1,0:T(8,128)(2,1)} %copy-done.94, ...), custom_call_target="tpu_custom_call" | custom-call | flops 3019898880 | bytes 8978432 | tf_op jit(solution)/shard_map/gate_up_products/pallas_call | solution.py:148
  383.8 7.5 %gate_up_products.10 = (bf16[2,160,1152]{2,1,0:T(8,128)(2,1)}, bf16[2,160,1152]{2,1,0:T(8,128)(2,1)}, bf16[2,160,1152]{2,1,0:T(8,128)(2,1)}, bf16[2,160,1152]{2,1,0:T(8,128)(2,1)}) custom-call(s32[21]{0:T(128)} %stack.250.where_ref, bf16[2,640,128]{2,1,0:T(8,128)(2,1)} %copy-done.30, bf16[2,640,128]{2,1,0:T(8,128)(2,1)} %copy-done.90, ...), custom_call_target="tpu_custom_call" | custom-call | flops 3019898880 | bytes 8978432 | tf_op jit(solution)/shard_map/gate_up_products/pallas_call | solution.py:148
  394.0 6.6 %gate_up_products.11 = (bf16[2,160,1024]{2,1,0:T(8,128)(2,1)}, bf16[2,160,1024]{2,1,0:T(8,128)(2,1)}, bf16[2,160,1024]{2,1,0:T(8,128)(2,1)}, bf16[2,160,1024]{2,1,0:T(8,128)(2,1)}) custom-call(s32[21]{0:T(128)} %stack.252.where_ref, bf16[2,640,128]{2,1,0:T(8,128)(2,1)} %copy-done.30, bf16[2,640,128]{2,1,0:T(8,128)(2,1)} %copy-done.86, ...), custom_call_target="tpu_custom_call" | custom-call | flops 2684354560 | bytes 8126464 | tf_op jit(solution)/shard_map/gate_up_products/pallas_call | solution.py:148
  401.6 9.0 %collective-permute-done.94.rest_1_ = bf16[2,160,1024]{2,1,0:T(8,128)(2,1)S(1)} collective-permute-done((bf16[2,160,1024]{2,1,0:T(8,128)(2,1)}, bf16[2,160,1024]{2,1,0:T(8,128)(2,1)S(1)}, u32[]{:S(2)}, u32[]{:S(2)}) %collective-permute-start.94) | collective-permute-done | bytes 655392 | tf_op jit(solution)/shard_map/ppermute | solution.py:29
  416.9 10.6 %collective-permute-done.96.rest_3_ = bf16[2,160,1152]{2,1,0:T(8,128)(2,1)} collective-permute-done((bf16[2,160,1152]{2,1,0:T(8,128)(2,1)}, bf16[2,160,1152]{2,1,0:T(8,128)(2,1)}, u32[]{:S(2)}, u32[]{:S(2)}) %collective-permute-start.96) | collective-permute-done | bytes 737312 | tf_op jit(solution)/shard_map/ppermute | solution.py:29
  427.5 2.8 first_sums.9
  430.5 10.6 %collective-permute-done.97.rest_2_ = bf16[2,160,1152]{2,1,0:T(8,128)(2,1)S(1)} collective-permute-done((bf16[2,160,1152]{2,1,0:T(8,128)(2,1)}, bf16[2,160,1152]{2,1,0:T(8,128)(2,1)S(1)}, u32[]{:S(2)}, u32[]{:S(2)}) %collective-permute-start.97) | collective-permute-done | bytes 737312 | tf_op jit(solution)/shard_map/ppermute | solution.py:29
  442.2 2.8 first_sums.10
  445.6 2.8 first_sums.11
  450.4 4.1 collective-permute-done.103
  454.6 2.8 collective-permute-start.109
  458.0 4.4 collective-permute-done.109
  465.4 2.8 collective-permute-start.110
  468.2 3.3 collective-permute-start.111
  475.6 4.0 collective-permute-start.116
  486.2 4.8 collective-permute-done.121.rest_1_
  498.3 3.6 collective-permute-done.129.rest_3_
  501.9 5.2 down_products.11
  507.1 9.0 %collective-permute-start.130 = (bf16[4,640,128]{2,1,0:T(8,128)(2,1)}, bf16[4,640,128]{2,1,0:T(8,128)(2,1)S(1)}, u32[]{:S(2)}, u32[]{:S(2)}) collective-permute-start(bf16[4,640,128]{2,1,0:T(8,128)(2,1)} %get-tuple-element.502), channel_id=1, source_target_pairs={{0,1},{1,0},{2,3},{3,2},{4,5},{5,4},{6,7},{7,6},{8,9},{9,8},{10,11... | collective-permute-start | bytes 1966088 | tf_op jit(solution)/shard_map/ppermute | solution.py:33
  516.9 5.8 %down_products.9 = (bf16[640,128]{1,0:T(8,128)(2,1)}, bf16[640,128]{1,0:T(8,128)(2,1)}, bf16[640,128]{1,0:T(8,128)(2,1)}, bf16[640,128]{1,0:T(8,128)(2,1)}, bf16[4,640,128]{2,1,0:T(8,128)(2,1)}) custom-call(s32[21]{0:T(128)} %stack.243.where_ref, bf16[4,40,1152]{2,1,0:T(8,128)(2,1)} %copy-done.26, bf16[4,40,1152]{2,1,0:T(8,128)(2,1)} %copy-done.75, ...), custom_call_target="tpu_custom_call" | custom-call | flops 1509949440 | bytes 5144576 | tf_op jit(solution)/shard_map/down_products/pallas_call | solution.py:230
  524.3 5.7 %down_products.10 = (bf16[640,128]{1,0:T(8,128)(2,1)}, bf16[640,128]{1,0:T(8,128)(2,1)}, bf16[640,128]{1,0:T(8,128)(2,1)}, bf16[640,128]{1,0:T(8,128)(2,1)}, bf16[4,640,128]{2,1,0:T(8,128)(2,1)}) custom-call(s32[21]{0:T(128)} %stack.250.where_ref, bf16[4,40,1152]{2,1,0:T(8,128)(2,1)} %copy-done.25, bf16[4,40,1152]{2,1,0:T(8,128)(2,1)} %copy-done.74, ...), custom_call_target="tpu_custom_call" | custom-call | flops 1509949440 | bytes 5144576 | tf_op jit(solution)/shard_map/down_products/pallas_call | solution.py:230
  545.1 2.8 collective-permute-done.135
  548.7 18.4 %all_to_all.10 = bf16[16,72,128]{2,1,0:T(8,128)(2,1)S(1)} all-to-all(bf16[16,72,128]{2,1,0:T(8,128)(2,1)S(1)} %pad_maximum_fusion.14), channel_id=1, replica_groups=mesh['y'=4,'xl'=2,'xh'=2,'z'=4,'c'=2] {'xh','z','c'}, dimensions={0} | all-to-all | bytes 589824 | tf_op jit(solution)/shard_map/all_to_all | solution.py:383
  (557 shorter events, 196.4 us)
Async XLA Ops:
  7.0 22.9 %collective-permute-start.18 = (bf16[2,2,128,1024]{3,2,1,0:T(8,128)(2,1)}, bf16[2,2,128,1024]{3,2,1,0:T(8,128)(2,1)S(1)}, u32[]{:S(2)}, u32[]{:S(2)}) collective-permute-start(bf16[2,2,128,1024]{3,2,1,0:T(8,128)(2,1)} %get-tuple-element.307), channel_id=1, source_target_pairs={{0,32},{32,64},{64,96},{96,0},{1,97},{33,1},{65,33},{97,65},{2,34}... | collective-permute-start | bytes 3145736 | tf_op jit(solution)/shard_map/ppermute | solution.py:29
  17.2 20.2 %collective-permute-start = (bf16[2,2,128,1152]{3,2,1,0:T(8,128)(2,1)}, bf16[2,2,128,1152]{3,2,1,0:T(8,128)(2,1)S(1)}, u32[]{:S(2)}, u32[]{:S(2)}) collective-permute-start(bf16[2,2,128,1152]{3,2,1,0:T(8,128)(2,1)} %get-tuple-element.264), channel_id=1, source_target_pairs={{0,2},{2,4},{4,6},{6,0},{1,7},{3,1},{5,3},{7,5},{8,10},{10,12},{12... | collective-permute-start | bytes 3538952 | tf_op jit(solution)/shard_map/ppermute | solution.py:29
  27.4 25.2 %collective-permute-start.11 = (bf16[2,2,128,1152]{3,2,1,0:T(8,128)(2,1)}, bf16[2,2,128,1152]{3,2,1,0:T(8,128)(2,1)S(1)}, u32[]{:S(2)}, u32[]{:S(2)}) collective-permute-start(bf16[2,2,128,1152]{3,2,1,0:T(8,128)(2,1)} %get-tuple-element.290), channel_id=1, source_target_pairs={{0,16},{16,8},{8,24},{24,0},{1,25},{17,1},{9,17},{25,9},{2,18},{18... | collective-permute-start | bytes 3538952 | tf_op jit(solution)/shard_map/ppermute | solution.py:29
  30.0 37.9 %collective-permute-start.19 = (bf16[2,2,128,1024]{3,2,1,0:T(8,128)(2,1)}, bf16[2,2,128,1024]{3,2,1,0:T(8,128)(2,1)}, u32[]{:S(2)}, u32[]{:S(2)}) collective-permute-start(bf16[2,2,128,1024]{3,2,1,0:T(8,128)(2,1)} %get-tuple-element.310), channel_id=1, source_target_pairs={{0,96},{32,0},{64,32},{96,64},{1,33},{33,65},{65,97},{97,1},{2,98}... | collective-permute-start | bytes 3145736 | tf_op jit(solution)/shard_map/ppermute | solution.py:29
  30.0 58.7 %collective-permute-start.5 = (bf16[2,2,128,1152]{3,2,1,0:T(8,128)(2,1)}, bf16[2,2,128,1152]{3,2,1,0:T(8,128)(2,1)}, u32[]{:S(2)}, u32[]{:S(2)}) collective-permute-start(bf16[2,2,128,1152]{3,2,1,0:T(8,128)(2,1)} %get-tuple-element.275), channel_id=1, source_target_pairs={{0,6},{2,0},{4,2},{6,4},{1,3},{3,5},{5,7},{7,1},{8,14},{10,8},{12,... | collective-permute-start | bytes 3538952 | tf_op jit(solution)/shard_map/ppermute | solution.py:29
  31.0 58.9 %collective-permute-start.12 = (bf16[2,2,128,1152]{3,2,1,0:T(8,128)(2,1)}, bf16[2,2,128,1152]{3,2,1,0:T(8,128)(2,1)S(1)}, u32[]{:S(2)}, u32[]{:S(2)}) collective-permute-start(bf16[2,2,128,1152]{3,2,1,0:T(8,128)(2,1)} %get-tuple-element.293), channel_id=1, source_target_pairs={{0,24},{16,0},{8,16},{24,8},{1,17},{17,9},{9,25},{25,1},{2,26},{18... | collective-permute-start | bytes 3538952 | tf_op jit(solution)/shard_map/ppermute | solution.py:29
  37.4 53.5 %collective-permute-start.20 = (bf16[2,2,128,1024]{3,2,1,0:T(8,128)(2,1)}, bf16[2,2,128,1024]{3,2,1,0:T(8,128)(2,1)}, u32[]{:S(2)}, u32[]{:S(2)}) collective-permute-start(bf16[2,2,128,1024]{3,2,1,0:T(8,128)(2,1)} %get-tuple-element.313), channel_id=1, source_target_pairs={{0,64},{32,96},{64,0},{96,32},{1,65},{33,97},{65,1},{97,33},{2,66}... | collective-permute-start | bytes 3145736 | tf_op jit(solution)/shard_map/ppermute | solution.py:29
  52.6 41.1 %collective-permute-start.6 = (bf16[2,2,128,1152]{3,2,1,0:T(8,128)(2,1)}, bf16[2,2,128,1152]{3,2,1,0:T(8,128)(2,1)}, u32[]{:S(2)}, u32[]{:S(2)}) collective-permute-start(bf16[2,2,128,1152]{3,2,1,0:T(8,128)(2,1)} %get-tuple-element.278), channel_id=1, source_target_pairs={{0,4},{2,6},{4,0},{6,2},{1,5},{3,7},{5,1},{7,3},{8,12},{10,14},{12... | collective-permute-start | bytes 3538952 | tf_op jit(solution)/shard_map/ppermute | solution.py:29
  67.9 29.0 %collective-permute-start.13 = (bf16[2,2,128,1152]{3,2,1,0:T(8,128)(2,1)}, bf16[2,2,128,1152]{3,2,1,0:T(8,128)(2,1)}, u32[]{:S(2)}, u32[]{:S(2)}) collective-permute-start(bf16[2,2,128,1152]{3,2,1,0:T(8,128)(2,1)} %get-tuple-element.296), channel_id=1, source_target_pairs={{0,8},{16,24},{8,0},{24,16},{1,9},{17,25},{9,1},{25,17},{2,10},{18... | collective-permute-start | bytes 3538952 | tf_op jit(solution)/shard_map/ppermute | solution.py:29
  84.6 15.5 %all-to-all-start = ((bf16[16,72,128]{2,1,0:T(8,128)(2,1)}), bf16[16,72,128]{2,1,0:T(8,128)(2,1)}, u32[]{:S(2)}, u32[]{:S(2)}) async-start(bf16[16,72,128]{2,1,0:T(8,128)(2,1)} %bitcast_bitcast_fusion), calls=%async_computation | async-start | bytes 589824 | tf_op jit(solution)/shard_map/all_to_all | solution.py:361
  93.5 45.3 %collective-permute-start.21 = (bf16[4,2,128,1024]{3,2,1,0:T(8,128)(2,1)}, bf16[4,2,128,1024]{3,2,1,0:T(8,128)(2,1)}, u32[]{:S(2)}, u32[]{:S(2)}) collective-permute-start(bf16[4,2,128,1024]{3,2,1,0:T(8,128)(2,1)} %pad_maximum_fusion.2), channel_id=1, source_target_pairs={{0,1},{1,0},{2,3},{3,2},{4,5},{5,4},{6,7},{7,6},{8,9},{9,8},{10,11... | collective-permute-start | bytes 6291464 | tf_op jit(solution)/shard_map/ppermute | solution.py:33
  96.6 52.1 %collective-permute-start.7 = (bf16[4,2,128,1152]{3,2,1,0:T(8,128)(2,1)}, bf16[4,2,128,1152]{3,2,1,0:T(8,128)(2,1)}, u32[]{:S(2)}, u32[]{:S(2)}) collective-permute-start(bf16[4,2,128,1152]{3,2,1,0:T(8,128)(2,1)} %pad_maximum_fusion), channel_id=1, source_target_pairs={{0,1},{1,0},{2,3},{3,2},{4,5},{5,4},{6,7},{7,6},{8,9},{9,8},{10,11... | collective-permute-start | bytes 7077896 | tf_op jit(solution)/shard_map/ppermute | solution.py:33
  99.9 59.4 %collective-permute-start.14 = (bf16[4,2,128,1152]{3,2,1,0:T(8,128)(2,1)}, bf16[4,2,128,1152]{3,2,1,0:T(8,128)(2,1)}, u32[]{:S(2)}, u32[]{:S(2)}) collective-permute-start(bf16[4,2,128,1152]{3,2,1,0:T(8,128)(2,1)} %pad_maximum_fusion.1), channel_id=1, source_target_pairs={{0,1},{1,0},{2,3},{3,2},{4,5},{5,4},{6,7},{7,6},{8,9},{9,8},{10,11... | collective-permute-start | bytes 7077896 | tf_op jit(solution)/shard_map/ppermute | solution.py:33
  129.7 18.9 %collective-permute-start.4 = (bf16[2,640,128]{2,1,0:T(8,128)(2,1)S(1)}, bf16[2,640,128]{2,1,0:T(8,128)(2,1)}, u32[]{:S(2)}, u32[]{:S(2)}) collective-permute-start(bf16[2,640,128]{2,1,0:T(8,128)(2,1)S(1)} %pad_maximum_fusion.10.rest_0_), channel_id=1, source_target_pairs={{0,4},{2,6},{4,0},{6,2},{1,5},{3,7},{5,1},{7,3},{8,12},{10,14},{12... | collective-permute-start | bytes 983048 | tf_op jit(solution)/shard_map/ppermute | solution.py:29
  133.3 33.5 %collective-permute-start.68 = (bf16[2,1024,128]{2,1,0:T(8,128)(2,1)S(1)}, bf16[2,1024,128]{2,1,0:T(8,128)(2,1)S(1)}, u32[]{:S(2)}, u32[]{:S(2)}) collective-permute-start(bf16[2,1024,128]{2,1,0:T(8,128)(2,1)S(1)} %copy-done.73), channel_id=1, source_target_pairs={{0,32},{32,64},{64,96},{96,0},{1,97},{33,1},{65,33},{97,65},{2,34}... | collective-permute-start | bytes 1572872 | tf_op jit(solution)/shard_map/ppermute | solution.py:29
  138.8 19.9 %collective-permute-start.10 = (bf16[2,640,128]{2,1,0:T(8,128)(2,1)S(1)}, bf16[2,640,128]{2,1,0:T(8,128)(2,1)}, u32[]{:S(2)}, u32[]{:S(2)}) collective-permute-start(bf16[2,640,128]{2,1,0:T(8,128)(2,1)S(1)} %pad_maximum_fusion.10.rest_0_), channel_id=1, source_target_pairs={{0,8},{16,24},{8,0},{24,16},{1,9},{17,25},{9,1},{25,17},{2,10},{18... | collective-permute-start | bytes 983048 | tf_op jit(solution)/shard_map/ppermute | solution.py:29
  148.6 19.0 %collective-permute-start.54 = (bf16[2,1152,128]{2,1,0:T(8,128)(2,1)}, bf16[2,1152,128]{2,1,0:T(8,128)(2,1)S(1)}, u32[]{:S(2)}, u32[]{:S(2)}) collective-permute-start(bf16[2,1152,128]{2,1,0:T(8,128)(2,1)} %get-tuple-element.376), channel_id=1, source_target_pairs={{0,2},{2,4},{4,6},{6,0},{1,7},{3,1},{5,3},{7,5},{8,10},{10,12},{12... | collective-permute-start | bytes 1769480 | tf_op jit(solution)/shard_map/ppermute | solution.py:29
  148.7 19.0 %collective-permute-start.61 = (bf16[2,1152,128]{2,1,0:T(8,128)(2,1)S(1)}, bf16[2,1152,128]{2,1,0:T(8,128)(2,1)S(1)}, u32[]{:S(2)}, u32[]{:S(2)}) collective-permute-start(bf16[2,1152,128]{2,1,0:T(8,128)(2,1)S(1)} %copy-done.71), channel_id=1, source_target_pairs={{0,16},{16,8},{8,24},{24,0},{1,25},{17,1},{9,17},{25,9},{2,18},{18... | collective-permute-start | bytes 1769480 | tf_op jit(solution)/shard_map/ppermute | solution.py:29
  166.8 15.9 %collective-permute-start.23 = (bf16[2,160,1152]{2,1,0:T(8,128)(2,1)}, bf16[2,160,1152]{2,1,0:T(8,128)(2,1)S(1)}, u32[]{:S(2)}, u32[]{:S(2)}) collective-permute-start(bf16[2,160,1152]{2,1,0:T(8,128)(2,1)} %get-tuple-element.298), channel_id=1, source_target_pairs={{0,32},{32,64},{64,96},{96,0},{1,97},{33,1},{65,33},{97,65},{2,34}... | collective-permute-start | bytes 2211848 | tf_op jit(solution)/shard_map/ppermute | solution.py:29
  167.6 15.1 %collective-permute-start.70 = (bf16[2,1024,128]{2,1,0:T(8,128)(2,1)S(1)}, bf16[2,1024,128]{2,1,0:T(8,128)(2,1)S(1)}, u32[]{:S(2)}, u32[]{:S(2)}) collective-permute-start(bf16[2,1024,128]{2,1,0:T(8,128)(2,1)S(1)} %copy-done.72), channel_id=1, source_target_pairs={{0,64},{32,96},{64,0},{96,32},{1,65},{33,97},{65,1},{97,33},{2,66}... | collective-permute-start | bytes 1572872 | tf_op jit(solution)/shard_map/ppermute | solution.py:29
  167.7 17.1 %collective-permute-start.56 = (bf16[2,1152,128]{2,1,0:T(8,128)(2,1)}, bf16[2,1152,128]{2,1,0:T(8,128)(2,1)S(1)}, u32[]{:S(2)}, u32[]{:S(2)}) collective-permute-start(bf16[2,1152,128]{2,1,0:T(8,128)(2,1)} %get-tuple-element.379), channel_id=1, source_target_pairs={{0,4},{2,6},{4,0},{6,2},{1,5},{3,7},{5,1},{7,3},{8,12},{10,14},{12... | collective-permute-start | bytes 1769480 | tf_op jit(solution)/shard_map/ppermute | solution.py:29
  170.6 25.4 %collective-permute-start.25 = (bf16[2,160,1152]{2,1,0:T(8,128)(2,1)}, bf16[2,160,1152]{2,1,0:T(8,128)(2,1)S(1)}, u32[]{:S(2)}, u32[]{:S(2)}) collective-permute-start(bf16[2,160,1152]{2,1,0:T(8,128)(2,1)} %get-tuple-element.322), channel_id=1, source_target_pairs={{0,24},{16,0},{8,16},{24,8},{1,17},{17,9},{9,25},{25,1},{2,26},{18... | collective-permute-start | bytes 2211848 | tf_op jit(solution)/shard_map/ppermute | solution.py:29
  172.0 24.0 %collective-permute-start.63 = (bf16[2,1152,128]{2,1,0:T(8,128)(2,1)}, bf16[2,1152,128]{2,1,0:T(8,128)(2,1)S(1)}, u32[]{:S(2)}, u32[]{:S(2)}) collective-permute-start(bf16[2,1152,128]{2,1,0:T(8,128)(2,1)} %get-tuple-element.390), channel_id=1, source_target_pairs={{0,8},{16,24},{8,0},{24,16},{1,9},{17,25},{9,1},{25,17},{2,10},{18... | collective-permute-start | bytes 1769480 | tf_op jit(solution)/shard_map/ppermute | solution.py:29
  182.7 16.0 %collective-permute-start.27 = (bf16[2,160,1152]{2,1,0:T(8,128)(2,1)}, bf16[2,160,1152]{2,1,0:T(8,128)(2,1)S(1)}, u32[]{:S(2)}, u32[]{:S(2)}) collective-permute-start(bf16[2,160,1152]{2,1,0:T(8,128)(2,1)} %get-tuple-element.330), channel_id=1, source_target_pairs={{0,96},{32,0},{64,32},{96,64},{1,33},{33,65},{65,97},{97,1},{2,98}... | collective-permute-start | bytes 2211848 | tf_op jit(solution)/shard_map/ppermute | solution.py:29
  182.7 30.4 %collective-permute-start.26 = (bf16[2,160,1152]{2,1,0:T(8,128)(2,1)}, bf16[2,160,1152]{2,1,0:T(8,128)(2,1)S(1)}, u32[]{:S(2)}, u32[]{:S(2)}) collective-permute-start(bf16[2,160,1152]{2,1,0:T(8,128)(2,1)} %get-tuple-element.323), channel_id=1, source_target_pairs={{0,8},{16,24},{8,0},{24,16},{1,9},{17,25},{9,1},{25,17},{2,10},{18... | collective-permute-start | bytes 2211848 | tf_op jit(solution)/shard_map/ppermute | solution.py:29
  184.8 29.7 %collective-permute-start.28 = (bf16[2,160,1152]{2,1,0:T(8,128)(2,1)}, bf16[2,160,1152]{2,1,0:T(8,128)(2,1)S(1)}, u32[]{:S(2)}, u32[]{:S(2)}) collective-permute-start(bf16[2,160,1152]{2,1,0:T(8,128)(2,1)} %get-tuple-element.331), channel_id=1, source_target_pairs={{0,64},{32,96},{64,0},{96,32},{1,65},{33,97},{65,1},{97,33},{2,66}... | collective-permute-start | bytes 2211848 | tf_op jit(solution)/shard_map/ppermute | solution.py:29
  196.0 25.7 %collective-permute-start.29 = (bf16[2,160,1024]{2,1,0:T(8,128)(2,1)}, bf16[2,160,1024]{2,1,0:T(8,128)(2,1)}, u32[]{:S(2)}, u32[]{:S(2)}) collective-permute-start(bf16[2,160,1024]{2,1,0:T(8,128)(2,1)} %get-tuple-element.337), channel_id=1, source_target_pairs={{0,6},{2,0},{4,2},{6,4},{1,3},{3,5},{5,7},{7,1},{8,14},{10,8},{12,... | collective-permute-start | bytes 1966088 | tf_op jit(solution)/shard_map/ppermute | solution.py:29
  196.0 26.1 %collective-permute-start.30 = (bf16[2,160,1024]{2,1,0:T(8,128)(2,1)}, bf16[2,160,1024]{2,1,0:T(8,128)(2,1)}, u32[]{:S(2)}, u32[]{:S(2)}) collective-permute-start(bf16[2,160,1024]{2,1,0:T(8,128)(2,1)} %get-tuple-element.338), channel_id=1, source_target_pairs={{0,4},{2,6},{4,0},{6,2},{1,5},{3,7},{5,1},{7,3},{8,12},{10,14},{12... | collective-permute-start | bytes 1966088 | tf_op jit(solution)/shard_map/ppermute | solution.py:29
  198.7 28.6 %collective-permute-start.69 = (bf16[2,1024,128]{2,1,0:T(8,128)(2,1)}, bf16[2,1024,128]{2,1,0:T(8,128)(2,1)}, u32[]{:S(2)}, u32[]{:S(2)}) collective-permute-start(bf16[2,1024,128]{2,1,0:T(8,128)(2,1)} %get-tuple-element.400), channel_id=1, source_target_pairs={{0,96},{32,0},{64,32},{96,64},{1,33},{33,65},{65,97},{97,1},{2,98}... | collective-permute-start | bytes 1572872 | tf_op jit(solution)/shard_map/ppermute | solution.py:29
  213.2 19.5 %collective-permute-start.55 = (bf16[2,1152,128]{2,1,0:T(8,128)(2,1)}, bf16[2,1152,128]{2,1,0:T(8,128)(2,1)}, u32[]{:S(2)}, u32[]{:S(2)}) collective-permute-start(bf16[2,1152,128]{2,1,0:T(8,128)(2,1)} %get-tuple-element.378), channel_id=1, source_target_pairs={{0,6},{2,0},{4,2},{6,4},{1,3},{3,5},{5,7},{7,1},{8,14},{10,8},{12,... | collective-permute-start | bytes 1769480 | tf_op jit(solution)/shard_map/ppermute | solution.py:29
  214.6 28.9 %collective-permute-start.62 = (bf16[2,1152,128]{2,1,0:T(8,128)(2,1)}, bf16[2,1152,128]{2,1,0:T(8,128)(2,1)S(1)}, u32[]{:S(2)}, u32[]{:S(2)}) collective-permute-start(bf16[2,1152,128]{2,1,0:T(8,128)(2,1)} %get-tuple-element.389), channel_id=1, source_target_pairs={{0,24},{16,0},{8,16},{24,8},{1,17},{17,9},{9,25},{25,1},{2,26},{18... | collective-permute-start | bytes 1769480 | tf_op jit(solution)/shard_map/ppermute | solution.py:29
  221.8 16.9 %collective-permute-start.31 = (bf16[2,40,1152]{2,1,0:T(8,128)(2,1)}, bf16[2,40,1152]{2,1,0:T(8,128)(2,1)}, u32[]{:S(2)}, u32[]{:S(2)}) collective-permute-start(bf16[2,40,1152]{2,1,0:T(8,128)(2,1)} %get-tuple-element.325), channel_id=1, source_target_pairs={{0,32},{32,64},{64,96},{96,0},{1,97},{33,1},{65,33},{97,65},{2,34}... | collective-permute-start | bytes 552968 | tf_op jit(solution)/shard_map/ppermute | solution.py:29
  222.2 16.5 %collective-permute-start.32 = (bf16[2,40,1152]{2,1,0:T(8,128)(2,1)}, bf16[2,40,1152]{2,1,0:T(8,128)(2,1)}, u32[]{:S(2)}, u32[]{:S(2)}) collective-permute-start(bf16[2,40,1152]{2,1,0:T(8,128)(2,1)} %get-tuple-element.332), channel_id=1, source_target_pairs={{0,2},{2,4},{4,6},{6,0},{1,7},{3,1},{5,3},{7,5},{8,10},{10,12},{12... | collective-permute-start | bytes 552968 | tf_op jit(solution)/shard_map/ppermute | solution.py:29
  232.6 58.4 %collective-permute-start.71 = (bf16[4,1024,128]{2,1,0:T(8,128)(2,1)S(1)}, bf16[4,1024,128]{2,1,0:T(8,128)(2,1)S(1)}, u32[]{:S(2)}, u32[]{:S(2)}) collective-permute-start(bf16[4,1024,128]{2,1,0:T(8,128)(2,1)S(1)} %pad_maximum_fusion.5), channel_id=1, source_target_pairs={{0,1},{1,0},{2,3},{3,2},{4,5},{5,4},{6,7},{7,6},{8,9},{9,8},{10,11... | collective-permute-start | bytes 3145736 | tf_op jit(solution)/shard_map/ppermute | solution.py:33
  243.0 49.4 %collective-permute-start.57 = (bf16[4,1152,128]{2,1,0:T(8,128)(2,1)S(1)}, bf16[4,1152,128]{2,1,0:T(8,128)(2,1)S(1)}, u32[]{:S(2)}, u32[]{:S(2)}) collective-permute-start(bf16[4,1152,128]{2,1,0:T(8,128)(2,1)S(1)} %pad_maximum_fusion.3), channel_id=1, source_target_pairs={{0,1},{1,0},{2,3},{3,2},{4,5},{5,4},{6,7},{7,6},{8,9},{9,8},{10,11... | collective-permute-start | bytes 3538952 | tf_op jit(solution)/shard_map/ppermute | solution.py:33
  284.1 36.4 %collective-permute-start.64 = (bf16[4,1152,128]{2,1,0:T(8,128)(2,1)S(1)}, bf16[4,1152,128]{2,1,0:T(8,128)(2,1)}, u32[]{:S(2)}, u32[]{:S(2)}) collective-permute-start(bf16[4,1152,128]{2,1,0:T(8,128)(2,1)S(1)} %pad_maximum_fusion.4), channel_id=1, source_target_pairs={{0,1},{1,0},{2,3},{3,2},{4,5},{5,4},{6,7},{7,6},{8,9},{9,8},{10,11... | collective-permute-start | bytes 3538952 | tf_op jit(solution)/shard_map/ppermute | solution.py:33
  290.5 14.6 %collective-permute-start.66 = (bf16[4,40,1024]{2,1,0:T(8,128)(2,1)S(1)}, bf16[4,40,1024]{2,1,0:T(8,128)(2,1)S(1)}, u32[]{:S(2)}, u32[]{:S(2)}) collective-permute-start(bf16[4,40,1024]{2,1,0:T(8,128)(2,1)S(1)} %pad_maximum_fusion.11.rest_0_), channel_id=1, source_target_pairs={{0,6},{2,0},{4,2},{6,4},{1,3},{3,5},{5,7},{7,1},{8,14},{10,8},{12,... | collective-permute-start | bytes 983048 | tf_op jit(solution)/shard_map/ppermute | solution.py:29
  290.6 15.5 %collective-permute-start.67 = (bf16[4,40,1024]{2,1,0:T(8,128)(2,1)S(1)}, bf16[4,40,1024]{2,1,0:T(8,128)(2,1)S(1)}, u32[]{:S(2)}, u32[]{:S(2)}) collective-permute-start(bf16[4,40,1024]{2,1,0:T(8,128)(2,1)S(1)} %pad_maximum_fusion.11.rest_0_), channel_id=1, source_target_pairs={{0,4},{2,6},{4,0},{6,2},{1,5},{3,7},{5,1},{7,3},{8,12},{10,14},{12... | collective-permute-start | bytes 983048 | tf_op jit(solution)/shard_map/ppermute | solution.py:29
  291.1 22.2 %collective-permute-start.52 = (bf16[4,40,1152]{2,1,0:T(8,128)(2,1)S(1)}, bf16[4,40,1152]{2,1,0:T(8,128)(2,1)}, u32[]{:S(2)}, u32[]{:S(2)}) collective-permute-start(bf16[4,40,1152]{2,1,0:T(8,128)(2,1)S(1)} %pad_maximum_fusion.6.rest_0_), channel_id=1, source_target_pairs={{0,24},{16,0},{8,16},{24,8},{1,17},{17,9},{9,25},{25,1},{2,26},{18... | collective-permute-start | bytes 1105928 | tf_op jit(solution)/shard_map/ppermute | solution.py:29
  292.4 22.3 %collective-permute-start.53 = (bf16[4,40,1152]{2,1,0:T(8,128)(2,1)S(1)}, bf16[4,40,1152]{2,1,0:T(8,128)(2,1)}, u32[]{:S(2)}, u32[]{:S(2)}) collective-permute-start(bf16[4,40,1152]{2,1,0:T(8,128)(2,1)S(1)} %pad_maximum_fusion.6.rest_0_), channel_id=1, source_target_pairs={{0,8},{16,24},{8,0},{24,16},{1,9},{17,25},{9,1},{25,17},{2,10},{18... | collective-permute-start | bytes 1105928 | tf_op jit(solution)/shard_map/ppermute | solution.py:29
  305.1 15.6 %collective-permute-start.59 = (bf16[4,40,1152]{2,1,0:T(8,128)(2,1)S(1)}, bf16[4,40,1152]{2,1,0:T(8,128)(2,1)S(1)}, u32[]{:S(2)}, u32[]{:S(2)}) collective-permute-start(bf16[4,40,1152]{2,1,0:T(8,128)(2,1)S(1)} %pad_maximum_fusion.7.rest_0_), channel_id=1, source_target_pairs={{0,96},{32,0},{64,32},{96,64},{1,33},{33,65},{65,97},{97,1},{2,98}... | collective-permute-start | bytes 1105928 | tf_op jit(solution)/shard_map/ppermute | solution.py:29
  306.1 14.6 %collective-permute-start.60 = (bf16[4,40,1152]{2,1,0:T(8,128)(2,1)S(1)}, bf16[4,40,1152]{2,1,0:T(8,128)(2,1)}, u32[]{:S(2)}, u32[]{:S(2)}) collective-permute-start(bf16[4,40,1152]{2,1,0:T(8,128)(2,1)S(1)} %pad_maximum_fusion.7.rest_0_), channel_id=1, source_target_pairs={{0,64},{32,96},{64,0},{96,32},{1,65},{33,97},{65,1},{97,33},{2,66}... | collective-permute-start | bytes 1105928 | tf_op jit(solution)/shard_map/ppermute | solution.py:29
  353.8 17.5 %collective-permute-start.84 = (bf16[2,640,128]{2,1,0:T(8,128)(2,1)S(1)}, bf16[2,640,128]{2,1,0:T(8,128)(2,1)S(1)}, u32[]{:S(2)}, u32[]{:S(2)}) collective-permute-start(bf16[2,640,128]{2,1,0:T(8,128)(2,1)S(1)} %pad_maximum_fusion.12.rest_0_), channel_id=1, source_target_pairs={{0,6},{2,0},{4,2},{6,4},{1,3},{3,5},{5,7},{7,1},{8,14},{10,8},{12,... | collective-permute-start | bytes 983048 | tf_op jit(solution)/shard_map/ppermute | solution.py:29
  354.3 18.7 %collective-permute-start.85 = (bf16[2,640,128]{2,1,0:T(8,128)(2,1)S(1)}, bf16[2,640,128]{2,1,0:T(8,128)(2,1)S(1)}, u32[]{:S(2)}, u32[]{:S(2)}) collective-permute-start(bf16[2,640,128]{2,1,0:T(8,128)(2,1)S(1)} %pad_maximum_fusion.12.rest_0_), channel_id=1, source_target_pairs={{0,4},{2,6},{4,0},{6,2},{1,5},{3,7},{5,1},{7,3},{8,12},{10,14},{12... | collective-permute-start | bytes 983048 | tf_op jit(solution)/shard_map/ppermute | solution.py:29
  355.1 17.9 %collective-permute-start.86 = (bf16[2,640,128]{2,1,0:T(8,128)(2,1)S(1)}, bf16[2,640,128]{2,1,0:T(8,128)(2,1)S(1)}, u32[]{:S(2)}, u32[]{:S(2)}) collective-permute-start(bf16[2,640,128]{2,1,0:T(8,128)(2,1)S(1)} %pad_maximum_fusion.12.rest_0_), channel_id=1, source_target_pairs={{0,16},{16,8},{8,24},{24,0},{1,25},{17,1},{9,17},{25,9},{2,18},{18... | collective-permute-start | bytes 983048 | tf_op jit(solution)/shard_map/ppermute | solution.py:29
  355.7 26.7 %collective-permute-start.87 = (bf16[2,640,128]{2,1,0:T(8,128)(2,1)S(1)}, bf16[2,640,128]{2,1,0:T(8,128)(2,1)S(1)}, u32[]{:S(2)}, u32[]{:S(2)}) collective-permute-start(bf16[2,640,128]{2,1,0:T(8,128)(2,1)S(1)} %pad_maximum_fusion.12.rest_0_), channel_id=1, source_target_pairs={{0,24},{16,0},{8,16},{24,8},{1,17},{17,9},{9,25},{25,1},{2,26},{18... | collective-permute-start | bytes 983048 | tf_op jit(solution)/shard_map/ppermute | solution.py:29
  361.6 20.8 %collective-permute-start.88 = (bf16[2,640,128]{2,1,0:T(8,128)(2,1)S(1)}, bf16[2,640,128]{2,1,0:T(8,128)(2,1)S(1)}, u32[]{:S(2)}, u32[]{:S(2)}) collective-permute-start(bf16[2,640,128]{2,1,0:T(8,128)(2,1)S(1)} %pad_maximum_fusion.12.rest_0_), channel_id=1, source_target_pairs={{0,8},{16,24},{8,0},{24,16},{1,9},{17,25},{9,1},{25,17},{2,10},{18... | collective-permute-start | bytes 983048 | tf_op jit(solution)/shard_map/ppermute | solution.py:29
  371.4 21.1 %collective-permute-start.89 = (bf16[2,640,128]{2,1,0:T(8,128)(2,1)S(1)}, bf16[2,640,128]{2,1,0:T(8,128)(2,1)S(1)}, u32[]{:S(2)}, u32[]{:S(2)}) collective-permute-start(bf16[2,640,128]{2,1,0:T(8,128)(2,1)S(1)} %pad_maximum_fusion.12.rest_0_), channel_id=1, source_target_pairs={{0,32},{32,64},{64,96},{96,0},{1,97},{33,1},{65,33},{97,65},{2,34}... | collective-permute-start | bytes 983048 | tf_op jit(solution)/shard_map/ppermute | solution.py:29
  373.0 19.4 %collective-permute-start.90 = (bf16[2,640,128]{2,1,0:T(8,128)(2,1)S(1)}, bf16[2,640,128]{2,1,0:T(8,128)(2,1)S(1)}, u32[]{:S(2)}, u32[]{:S(2)}) collective-permute-start(bf16[2,640,128]{2,1,0:T(8,128)(2,1)S(1)} %pad_maximum_fusion.12.rest_0_), channel_id=1, source_target_pairs={{0,96},{32,0},{64,32},{96,64},{1,33},{33,65},{65,97},{97,1},{2,98}... | collective-permute-start | bytes 983048 | tf_op jit(solution)/shard_map/ppermute | solution.py:29
  373.0 19.4 %collective-permute-start.91 = (bf16[2,640,128]{2,1,0:T(8,128)(2,1)S(1)}, bf16[2,640,128]{2,1,0:T(8,128)(2,1)S(1)}, u32[]{:S(2)}, u32[]{:S(2)}) collective-permute-start(bf16[2,640,128]{2,1,0:T(8,128)(2,1)S(1)} %pad_maximum_fusion.12.rest_0_), channel_id=1, source_target_pairs={{0,64},{32,96},{64,0},{96,32},{1,65},{33,97},{65,1},{97,33},{2,66}... | collective-permute-start | bytes 983048 | tf_op jit(solution)/shard_map/ppermute | solution.py:29
  382.3 28.3 %collective-permute-start.92 = (bf16[2,160,1152]{2,1,0:T(8,128)(2,1)}, bf16[2,160,1152]{2,1,0:T(8,128)(2,1)S(1)}, u32[]{:S(2)}, u32[]{:S(2)}) collective-permute-start(bf16[2,160,1152]{2,1,0:T(8,128)(2,1)} %get-tuple-element.426), channel_id=1, source_target_pairs={{0,16},{16,8},{8,24},{24,0},{1,25},{17,1},{9,17},{25,9},{2,18},{18... | collective-permute-start | bytes 2211848 | tf_op jit(solution)/shard_map/ppermute | solution.py:29
  391.3 19.4 %collective-permute-start.93 = (bf16[2,160,1152]{2,1,0:T(8,128)(2,1)}, bf16[2,160,1152]{2,1,0:T(8,128)(2,1)S(1)}, u32[]{:S(2)}, u32[]{:S(2)}) collective-permute-start(bf16[2,160,1152]{2,1,0:T(8,128)(2,1)} %get-tuple-element.429), channel_id=1, source_target_pairs={{0,32},{32,64},{64,96},{96,0},{1,97},{33,1},{65,33},{97,65},{2,34}... | collective-permute-start | bytes 2211848 | tf_op jit(solution)/shard_map/ppermute | solution.py:29
  400.7 15.5 %collective-permute-start.95 = (bf16[2,160,1152]{2,1,0:T(8,128)(2,1)}, bf16[2,160,1152]{2,1,0:T(8,128)(2,1)S(1)}, u32[]{:S(2)}, u32[]{:S(2)}) collective-permute-start(bf16[2,160,1152]{2,1,0:T(8,128)(2,1)} %get-tuple-element.439), channel_id=1, source_target_pairs={{0,24},{16,0},{8,16},{24,8},{1,17},{17,9},{9,25},{25,1},{2,26},{18... | collective-permute-start | bytes 2211848 | tf_op jit(solution)/shard_map/ppermute | solution.py:29
  411.5 16.0 %collective-permute-start.96 = (bf16[2,160,1152]{2,1,0:T(8,128)(2,1)}, bf16[2,160,1152]{2,1,0:T(8,128)(2,1)}, u32[]{:S(2)}, u32[]{:S(2)}) collective-permute-start(bf16[2,160,1152]{2,1,0:T(8,128)(2,1)} %get-tuple-element.440), channel_id=1, source_target_pairs={{0,8},{16,24},{8,0},{24,16},{1,9},{17,25},{9,1},{25,17},{2,10},{18... | collective-permute-start | bytes 2211848 | tf_op jit(solution)/shard_map/ppermute | solution.py:29
  412.7 28.3 %collective-permute-start.97 = (bf16[2,160,1152]{2,1,0:T(8,128)(2,1)}, bf16[2,160,1152]{2,1,0:T(8,128)(2,1)S(1)}, u32[]{:S(2)}, u32[]{:S(2)}) collective-permute-start(bf16[2,160,1152]{2,1,0:T(8,128)(2,1)} %get-tuple-element.447), channel_id=1, source_target_pairs={{0,96},{32,0},{64,32},{96,64},{1,33},{33,65},{65,97},{97,1},{2,98}... | collective-permute-start | bytes 2211848 | tf_op jit(solution)/shard_map/ppermute | solution.py:29
  413.9 27.2 %collective-permute-start.98 = (bf16[2,160,1152]{2,1,0:T(8,128)(2,1)}, bf16[2,160,1152]{2,1,0:T(8,128)(2,1)S(1)}, u32[]{:S(2)}, u32[]{:S(2)}) collective-permute-start(bf16[2,160,1152]{2,1,0:T(8,128)(2,1)} %get-tuple-element.448), channel_id=1, source_target_pairs={{0,64},{32,96},{64,0},{96,32},{1,65},{33,97},{65,1},{97,33},{2,66}... | collective-permute-start | bytes 2211848 | tf_op jit(solution)/shard_map/ppermute | solution.py:29
  414.8 30.8 %collective-permute-start.99 = (bf16[2,160,1024]{2,1,0:T(8,128)(2,1)}, bf16[2,160,1024]{2,1,0:T(8,128)(2,1)}, u32[]{:S(2)}, u32[]{:S(2)}) collective-permute-start(bf16[2,160,1024]{2,1,0:T(8,128)(2,1)} %get-tuple-element.454), channel_id=1, source_target_pairs={{0,6},{2,0},{4,2},{6,4},{1,3},{3,5},{5,7},{7,1},{8,14},{10,8},{12,... | collective-permute-start | bytes 1966088 | tf_op jit(solution)/shard_map/ppermute | solution.py:29
  416.2 29.3 %collective-permute-start.100 = (bf16[2,160,1024]{2,1,0:T(8,128)(2,1)}, bf16[2,160,1024]{2,1,0:T(8,128)(2,1)}, u32[]{:S(2)}, u32[]{:S(2)}) collective-permute-start(bf16[2,160,1024]{2,1,0:T(8,128)(2,1)} %get-tuple-element.455), channel_id=1, source_target_pairs={{0,4},{2,6},{4,0},{6,2},{1,5},{3,7},{5,1},{7,3},{8,12},{10,14},{12... | collective-permute-start | bytes 1966088 | tf_op jit(solution)/shard_map/ppermute | solution.py:29
  430.4 24.2 %collective-permute-start.101 = (bf16[2,40,1152]{2,1,0:T(8,128)(2,1)}, bf16[2,40,1152]{2,1,0:T(8,128)(2,1)S(1)}, u32[]{:S(2)}, u32[]{:S(2)}) collective-permute-start(bf16[2,40,1152]{2,1,0:T(8,128)(2,1)} %get-tuple-element.442), channel_id=1, source_target_pairs={{0,32},{32,64},{64,96},{96,0},{1,97},{33,1},{65,33},{97,65},{2,34}... | collective-permute-start | bytes 552968 | tf_op jit(solution)/shard_map/ppermute | solution.py:29
  492.7 23.4 %collective-permute-start.122 = (bf16[4,40,1152]{2,1,0:T(8,128)(2,1)S(1)}, bf16[4,40,1152]{2,1,0:T(8,128)(2,1)S(1)}, u32[]{:S(2)}, u32[]{:S(2)}) collective-permute-start(bf16[4,40,1152]{2,1,0:T(8,128)(2,1)S(1)} %pad_maximum_fusion.8.rest_0_), channel_id=1, source_target_pairs={{0,24},{16,0},{8,16},{24,8},{1,17},{17,9},{9,25},{25,1},{2,26},{18... | collective-permute-start | bytes 1105928 | tf_op jit(solution)/shard_map/ppermute | solution.py:29
  492.7 23.4 %collective-permute-start.123 = (bf16[4,40,1152]{2,1,0:T(8,128)(2,1)S(1)}, bf16[4,40,1152]{2,1,0:T(8,128)(2,1)}, u32[]{:S(2)}, u32[]{:S(2)}) collective-permute-start(bf16[4,40,1152]{2,1,0:T(8,128)(2,1)S(1)} %pad_maximum_fusion.8.rest_0_), channel_id=1, source_target_pairs={{0,8},{16,24},{8,0},{24,16},{1,9},{17,25},{9,1},{25,17},{2,10},{18... | collective-permute-start | bytes 1105928 | tf_op jit(solution)/shard_map/ppermute | solution.py:29
  494.9 27.9 %collective-permute-start.125 = (bf16[4,40,1152]{2,1,0:T(8,128)(2,1)S(1)}, bf16[4,40,1152]{2,1,0:T(8,128)(2,1)S(1)}, u32[]{:S(2)}, u32[]{:S(2)}) collective-permute-start(bf16[4,40,1152]{2,1,0:T(8,128)(2,1)S(1)} %pad_maximum_fusion.9.rest_0_), channel_id=1, source_target_pairs={{0,96},{32,0},{64,32},{96,64},{1,33},{33,65},{65,97},{97,1},{2,98}... | collective-permute-start | bytes 1105928 | tf_op jit(solution)/shard_map/ppermute | solution.py:29
  495.9 26.9 %collective-permute-start.126 = (bf16[4,40,1152]{2,1,0:T(8,128)(2,1)S(1)}, bf16[4,40,1152]{2,1,0:T(8,128)(2,1)S(1)}, u32[]{:S(2)}, u32[]{:S(2)}) collective-permute-start(bf16[4,40,1152]{2,1,0:T(8,128)(2,1)S(1)} %pad_maximum_fusion.9.rest_0_), channel_id=1, source_target_pairs={{0,64},{32,96},{64,0},{96,32},{1,65},{33,97},{65,1},{97,33},{2,66}... | collective-permute-start | bytes 1105928 | tf_op jit(solution)/shard_map/ppermute | solution.py:29
  507.1 23.5 %collective-permute-start.130 = (bf16[4,640,128]{2,1,0:T(8,128)(2,1)}, bf16[4,640,128]{2,1,0:T(8,128)(2,1)S(1)}, u32[]{:S(2)}, u32[]{:S(2)}) collective-permute-start(bf16[4,640,128]{2,1,0:T(8,128)(2,1)} %get-tuple-element.502), channel_id=1, source_target_pairs={{0,1},{1,0},{2,3},{3,2},{4,5},{5,4},{6,7},{7,6},{8,9},{9,8},{10,11... | collective-permute-start | bytes 1966088 | tf_op jit(solution)/shard_map/ppermute | solution.py:33
  (200 other events, 2107.7 us)

commit v3 on v2

--- a/solution.py
+++ b/solution.py
@@ -288,8 +288,28 @@
     return results
 
 
+def other_halves(received):
+    _, parts, *rest = received[0].shape
+    part, zeros = parts // 2, (0,) * len(rest)
+
+    def body(*refs):
+        for slot in range(4):
+            refs[4][slot] = refs[slot][0]
+
+    return pl.pallas_call(
+        body,
+        grid=(2,),
+        out_shape=jax.ShapeDtypeStruct((4, parts, *rest), received[0].dtype),
+        in_specs=[pl.BlockSpec((1, part, *rest), lambda at: (1, at, *zeros))] * 4,
+        out_specs=pl.BlockSpec((4, part, *rest), lambda at: (0, at, *zeros)),
+        compiler_params=params(),
+        cost_estimate=copy_cost(4 * received[0].size),
+        name="other_halves",
+    )(*received)
+
+
 def share_cores(received):
-    return received, core_swap(jnp.stack([value[1] for value in received]))
+    return received, core_swap(other_halves(received))
 
 
 def block_update(mine, wheres, gate_up, down):

time: 579 us -> 582 us (level)
  waiting for transfers between devices: 176 us -> 213 us
  starting transfers between devices: 208 us -> 181 us
  Pallas kernels: 121 us -> 136 us
  local copies, waits for them, and re-layouts: 28.7 us -> 18.1 us
  other arithmetic: 13 us -> 5.62 us
    ppermute x126, waiting for transfers between devices: 173 us -> 210 us  [ring_permute(): return lax.ppermute(value, RINGS[ring] + ('c',), pairs)]
    ppermute x126, starting transfers between devices: 179 us -> 146 us  [ring_permute(): return lax.ppermute(value, RINGS[ring] + ('c',), pairs)]
    pallas_call x0 -> x6, Pallas kernels: none -> 14.9 us  [other_halves(): pl.pallas_call(body, grid=(2,), out_shape=jax.ShapeDtypeStruct((4, parts,...]
    slice x35 -> x0, local copies, waits for them, and re-layouts: 12.6 us -> none  [share_cores(): return (received, core_swap(jnp.stack([value[1] for value in received])))]
    unnamed x224 -> x192, local copies, waits for them, and re-layouts: 11.1 us -> 14.7 us
  transfers between devices with their start and end apart: 141 -> 141, of which waited for: 44 -> 52; matrix products, arithmetic and copies ran while one was open for 5% -> 1% of each run, Pallas kernels for 20% -> 23%
where the time goes in v3:
time: 582 us; the launch traced here: 573 us
  waiting for transfers between devices  213 us (37%)
  starting transfers between devices  181 us (31%)
  Pallas kernels  136 us (23%)
  local copies, waits for them, and re-layouts  18.1 us (3%)
  blocking collectives  16.3 us (3%)
    ppermute x126, waiting for transfers between devices, ring_permute(): return lax.ppermute(value, RINGS[ring] + ('c',), pairs)  210 us
    ppermute x126, starting transfers between devices, ring_permute(): return lax.ppermute(value, RINGS[ring] + ('c',), pairs)  146 us
    pallas_call x6, Pallas kernels, gate_up_products(): pl.pallas_call(body, grid=(2, width // tile), out_shape=[jax.ShapeDtypeSt...  43.4 us
    pallas_call x6, Pallas kernels, down_products(): pl.pallas_call(body, grid=(1,), out_shape=[jax.ShapeDtypeStruct((rows, ow...  33.3 us
    ppermute x14, starting transfers between devices, core_swap(): return lax.ppermute(value, 'c', [(0, 1), (1, 0)])  27.1 us
    pallas_call x3, Pallas kernels, pack_gate_up(): pl.pallas_call(body, out_shape=[jax.ShapeDtypeStruct((2, 2, rows, width),...  17.2 us
    pallas_call x6, Pallas kernels, first_sums(): pl.pallas_call(body, grid=(2, width // tile), out_shape=[jax.ShapeDtypeSt...  16.7 us
    all_to_all x1, blocking collectives, shards(): both = lax.all_to_all(both, tensor, split_axis=0, concat_axis=0, tiled=True)  16.3 us
  transfers between devices with their start and end apart: 141, of which 52 were waited for; matrix products, arithmetic and copies ran while one was open for 1% of the time, Pallas kernels for 23%

profile of v3, /device:TPU:1, one launch (start us, length us, event | category | flops | bytes accessed | tf_op | source)
XLA Modules:
  0.0 572.9 jit_solution(8384518271816889647)
XLA Ops:
  1.6 5.8 %pack_gate_up.3 = (bf16[2,2,128,1152]{3,2,1,0:T(8,128)(2,1)}, bf16[2,2,128,1152]{3,2,1,0:T(8,128)(2,1)}, bf16[2,2,128,1152]{3,2,1,0:T(8,128)(2,1)}, bf16[2,2,128,1152]{3,2,1,0:T(8,128)(2,1)}) custom-call(s32[21]{0:T(128)} %stack.225.where_ref, bf16[128,26624]{1,0:T(8,128)(2,1)} %rest_3_.10, bf16[128,26624]{1,0:T(8,128)(2,1)} %rest_3_.10, ...), custom_call_target="tpu_custom_call" | custom-call | bytes 9437184 | tf_op jit(solution)/shard_map/pack_gate_up/pallas_call | solution.py:69
  7.4 4.7 collective-permute-start
  12.8 5.8 %pack_gate_up.4 = (bf16[2,2,128,1152]{3,2,1,0:T(8,128)(2,1)}, bf16[2,2,128,1152]{3,2,1,0:T(8,128)(2,1)}, bf16[2,2,128,1152]{3,2,1,0:T(8,128)(2,1)}, bf16[2,2,128,1152]{3,2,1,0:T(8,128)(2,1)}) custom-call(s32[21]{0:T(128)} %stack.231.where_ref, bf16[128,26624]{1,0:T(8,128)(2,1)} %rest_3_.10, bf16[128,26624]{1,0:T(8,128)(2,1)} %rest_3_.10, ...), custom_call_target="tpu_custom_call" | custom-call | bytes 9437184 | tf_op jit(solution)/shard_map/pack_gate_up/pallas_call | solution.py:69
  21.8 5.5 pack_gate_up.5
  31.5 3.2 collective-permute-done.11.refs_1_.rest_5_
  37.1 5.1 collective-permute-done.18.refs_1_.rest_5_
  44.2 2.9 collective-permute-start.20
  47.1 3.6 pack_down.3
  50.7 15.8 %collective-permute-done.6.refs_3_.rest_7_ = bf16[2,2,128,1152]{3,2,1,0:T(8,128)(2,1)} collective-permute-done((bf16[2,2,128,1152]{3,2,1,0:T(8,128)(2,1)}, bf16[2,2,128,1152]{3,2,1,0:T(8,128)(2,1)}, u32[]{:S(2)}, u32[]{:S(2)}) %collective-permute-start.6) | collective-permute-done | bytes 1179680 | tf_op jit(solution)/shard_map/ppermute | solution.py:29
  66.5 2.9 other_halves.6
  69.4 4.2 collective-permute-start.7
  74.4 7.6 %all-to-all-start = ((bf16[16,72,128]{2,1,0:T(8,128)(2,1)}), bf16[16,72,128]{2,1,0:T(8,128)(2,1)S(1)}, u32[]{:S(2)}, u32[]{:S(2)}) async-start(bf16[16,72,128]{2,1,0:T(8,128)(2,1)} %bitcast_bitcast_fusion), calls=%async_computation | async-start | bytes 589824 | tf_op jit(solution)/shard_map/all_to_all | solution.py:381
  82.0 3.6 pack_down.4
  92.1 3.5 pack_down.5
  100.7 4.0 collective-permute-done.2.rest_1_
  106.1 4.5 collective-permute-done.15.rest_1_
  113.2 4.5 collective-permute-done.9.rest_2_
  121.7 3.4 collective-permute-done.4.rest_3_
  126.1 7.6 %gate_up_products.6 = (bf16[2,160,1152]{2,1,0:T(8,128)(2,1)}, bf16[2,160,1152]{2,1,0:T(8,128)(2,1)}, bf16[2,160,1152]{2,1,0:T(8,128)(2,1)}, bf16[2,160,1152]{2,1,0:T(8,128)(2,1)}) custom-call(s32[21]{0:T(128)} %stack.225.where_ref, bf16[2,640,128]{2,1,0:T(8,128)(2,1)} %copy-done.26, bf16[2,640,128]{2,1,0:T(8,128)(2,1)} %copy-done.74, ...), custom_call_target="tpu_custom_call" | custom-call | flops 3019898880 | bytes 8978432 | tf_op jit(solution)/shard_map/gate_up_products/pallas_call | solution.py:148
  134.5 7.5 %gate_up_products.7 = (bf16[2,160,1152]{2,1,0:T(8,128)(2,1)}, bf16[2,160,1152]{2,1,0:T(8,128)(2,1)}, bf16[2,160,1152]{2,1,0:T(8,128)(2,1)}, bf16[2,160,1152]{2,1,0:T(8,128)(2,1)}) custom-call(s32[21]{0:T(128)} %stack.231.where_ref, bf16[2,640,128]{2,1,0:T(8,128)(2,1)} %copy-done.26, bf16[2,640,128]{2,1,0:T(8,128)(2,1)} %copy-done.69, ...), custom_call_target="tpu_custom_call" | custom-call | flops 3019898880 | bytes 8978432 | tf_op jit(solution)/shard_map/gate_up_products/pallas_call | solution.py:148
  145.4 6.7 %gate_up_products.8 = (bf16[2,160,1024]{2,1,0:T(8,128)(2,1)}, bf16[2,160,1024]{2,1,0:T(8,128)(2,1)}, bf16[2,160,1024]{2,1,0:T(8,128)(2,1)}, bf16[2,160,1024]{2,1,0:T(8,128)(2,1)}) custom-call(s32[21]{0:T(128)} %stack.232.where_ref, bf16[2,640,128]{2,1,0:T(8,128)(2,1)} %copy-done.26, bf16[2,640,128]{2,1,0:T(8,128)(2,1)} %copy-done.68, ...), custom_call_target="tpu_custom_call" | custom-call | flops 2684354560 | bytes 8126464 | tf_op jit(solution)/shard_map/gate_up_products/pallas_call | solution.py:148
  152.1 5.0 collective-permute-start.24
  158.5 10.9 %collective-permute-done.24.rest_1_ = bf16[2,160,1024]{2,1,0:T(8,128)(2,1)S(1)} collective-permute-done((bf16[2,160,1024]{2,1,0:T(8,128)(2,1)}, bf16[2,160,1024]{2,1,0:T(8,128)(2,1)S(1)}, u32[]{:S(2)}, u32[]{:S(2)}) %collective-permute-start.24) | collective-permute-done | bytes 655392 | tf_op jit(solution)/shard_map/ppermute | solution.py:29
  171.4 3.1 collective-permute-done.29.rest_2_
  175.5 8.7 %collective-permute-done.26.rest_3_ = bf16[2,160,1152]{2,1,0:T(8,128)(2,1)} collective-permute-done((bf16[2,160,1152]{2,1,0:T(8,128)(2,1)}, bf16[2,160,1152]{2,1,0:T(8,128)(2,1)}, u32[]{:S(2)}, u32[]{:S(2)}) %collective-permute-start.26) | collective-permute-done | bytes 737312 | tf_op jit(solution)/shard_map/ppermute | solution.py:29
  190.9 8.9 %collective-permute-done.27.rest_2_ = bf16[2,160,1152]{2,1,0:T(8,128)(2,1)S(1)} collective-permute-done((bf16[2,160,1152]{2,1,0:T(8,128)(2,1)}, bf16[2,160,1152]{2,1,0:T(8,128)(2,1)S(1)}, u32[]{:S(2)}, u32[]{:S(2)}) %collective-permute-start.27) | collective-permute-done | bytes 737312 | tf_op jit(solution)/shard_map/ppermute | solution.py:29
  199.8 4.7 collective-permute-start.33
  208.1 3.8 collective-permute-start.32
  214.6 14.2 %collective-permute-done.32 = bf16[2,40,1152]{2,1,0:T(8,128)(2,1)S(1)} collective-permute-done((bf16[2,40,1152]{2,1,0:T(8,128)(2,1)}, bf16[2,40,1152]{2,1,0:T(8,128)(2,1)S(1)}, u32[]{:S(2)}, u32[]{:S(2)}) %collective-permute-start.32) | collective-permute-done | bytes 184352 | tf_op jit(solution)/shard_map/ppermute | solution.py:29
  229.8 8.5 %collective-permute-done.69.refs_2_.rest_6_ = bf16[2,1024,128]{2,1,0:T(8,128)(2,1)S(1)} collective-permute-done((bf16[2,1024,128]{2,1,0:T(8,128)(2,1)}, bf16[2,1024,128]{2,1,0:T(8,128)(2,1)S(1)}, u32[]{:S(2)}, u32[]{:S(2)}) %collective-permute-start.69) | collective-permute-done | bytes 524320 | tf_op jit(solution)/shard_map/ppermute | solution.py:29
  246.0 6.2 %collective-permute-done.34 = bf16[2,40,1152]{2,1,0:T(8,128)(2,1)S(1)} collective-permute-done((bf16[2,40,1152]{2,1,0:T(8,128)(2,1)S(1)}, bf16[2,40,1152]{2,1,0:T(8,128)(2,1)S(1)}, u32[]{:S(2)}, u32[]{:S(2)}) %collective-permute-start.34) | collective-permute-done | bytes 184352 | tf_op jit(solution)/shard_map/ppermute | solution.py:29
  252.3 3.9 collective-permute-start.37
  260.1 3.6 collective-permute-start.40
  270.6 3.0 collective-permute-start.71
  274.2 4.0 collective-permute-done.45
  283.1 3.4 collective-permute-start.49
  293.8 3.4 collective-permute-start.53
  297.2 8.9 %collective-permute-done.66.rest_2_ = bf16[4,40,1024]{2,1,0:T(8,128)(2,1)S(1)} collective-permute-done((bf16[4,40,1024]{2,1,0:T(8,128)(2,1)S(1)}, bf16[4,40,1024]{2,1,0:T(8,128)(2,1)S(1)}, u32[]{:S(2)}, u32[]{:S(2)}) %collective-permute-start.66) | collective-permute-done | bytes 327712 | tf_op jit(solution)/shard_map/ppermute | solution.py:29
  309.7 5.2 down_products.8
  318.2 5.7 down_products.6
  325.6 5.7 down_products.7
  333.0 3.4 collective-permute-start.73
  339.5 3.3 collective-permute-done.74
  344.9 5.2 collective-permute-done.81
  358.8 4.2 collective-permute-done.83.rest_1_
  363.6 9.4 %collective-permute-done.84.rest_2_ = bf16[2,640,128]{2,1,0:T(8,128)(2,1)S(1)} collective-permute-done((bf16[2,640,128]{2,1,0:T(8,128)(2,1)S(1)}, bf16[2,640,128]{2,1,0:T(8,128)(2,1)S(1)}, u32[]{:S(2)}, u32[]{:S(2)}) %collective-permute-start.84) | collective-permute-done | bytes 327712 | tf_op jit(solution)/shard_map/ppermute | solution.py:29
  376.3 7.5 %gate_up_products.9 = (bf16[2,160,1152]{2,1,0:T(8,128)(2,1)}, bf16[2,160,1152]{2,1,0:T(8,128)(2,1)}, bf16[2,160,1152]{2,1,0:T(8,128)(2,1)}, bf16[2,160,1152]{2,1,0:T(8,128)(2,1)}) custom-call(s32[21]{0:T(128)} %stack.225.where_ref, bf16[2,640,128]{2,1,0:T(8,128)(2,1)} %copy-done.25, bf16[2,640,128]{2,1,0:T(8,128)(2,1)} %copy-done.79, ...), custom_call_target="tpu_custom_call" | custom-call | flops 3019898880 | bytes 8978432 | tf_op jit(solution)/shard_map/gate_up_products/pallas_call | solution.py:148
  385.8 7.5 %gate_up_products.10 = (bf16[2,160,1152]{2,1,0:T(8,128)(2,1)}, bf16[2,160,1152]{2,1,0:T(8,128)(2,1)}, bf16[2,160,1152]{2,1,0:T(8,128)(2,1)}, bf16[2,160,1152]{2,1,0:T(8,128)(2,1)}) custom-call(s32[21]{0:T(128)} %stack.231.where_ref, bf16[2,640,128]{2,1,0:T(8,128)(2,1)} %copy-done.25, bf16[2,640,128]{2,1,0:T(8,128)(2,1)} %copy-done.73, ...), custom_call_target="tpu_custom_call" | custom-call | flops 3019898880 | bytes 8978432 | tf_op jit(solution)/shard_map/gate_up_products/pallas_call | solution.py:148
  396.9 6.7 %gate_up_products.11 = (bf16[2,160,1024]{2,1,0:T(8,128)(2,1)}, bf16[2,160,1024]{2,1,0:T(8,128)(2,1)}, bf16[2,160,1024]{2,1,0:T(8,128)(2,1)}, bf16[2,160,1024]{2,1,0:T(8,128)(2,1)}) custom-call(s32[21]{0:T(128)} %stack.232.where_ref, bf16[2,640,128]{2,1,0:T(8,128)(2,1)} %copy-done.25, bf16[2,640,128]{2,1,0:T(8,128)(2,1)} %copy-done.70, ...), custom_call_target="tpu_custom_call" | custom-call | flops 2684354560 | bytes 8126464 | tf_op jit(solution)/shard_map/gate_up_products/pallas_call | solution.py:148
  404.9 8.7 %collective-permute-done.94.rest_1_ = bf16[2,160,1024]{2,1,0:T(8,128)(2,1)S(1)} collective-permute-done((bf16[2,160,1024]{2,1,0:T(8,128)(2,1)}, bf16[2,160,1024]{2,1,0:T(8,128)(2,1)S(1)}, u32[]{:S(2)}, u32[]{:S(2)}) %collective-permute-start.94) | collective-permute-done | bytes 655392 | tf_op jit(solution)/shard_map/ppermute | solution.py:29
  420.1 10.1 %collective-permute-done.96.rest_3_ = bf16[2,160,1152]{2,1,0:T(8,128)(2,1)} collective-permute-done((bf16[2,160,1152]{2,1,0:T(8,128)(2,1)}, bf16[2,160,1152]{2,1,0:T(8,128)(2,1)}, u32[]{:S(2)}, u32[]{:S(2)}) %collective-permute-start.96) | collective-permute-done | bytes 737312 | tf_op jit(solution)/shard_map/ppermute | solution.py:29
  433.1 10.9 %collective-permute-done.97.rest_2_ = bf16[2,160,1152]{2,1,0:T(8,128)(2,1)S(1)} collective-permute-done((bf16[2,160,1152]{2,1,0:T(8,128)(2,1)}, bf16[2,160,1152]{2,1,0:T(8,128)(2,1)S(1)}, u32[]{:S(2)}, u32[]{:S(2)}) %collective-permute-start.97) | collective-permute-done | bytes 737312 | tf_op jit(solution)/shard_map/ppermute | solution.py:29
  454.0 3.2 collective-permute-done.103
  478.0 3.1 collective-permute-start.116
  487.5 6.7 %collective-permute-done.121.rest_1_ = bf16[4,40,1024]{2,1,0:T(8,128)(2,1)S(1)} collective-permute-done((bf16[4,40,1024]{2,1,0:T(8,128)(2,1)S(1)}, bf16[4,40,1024]{2,1,0:T(8,128)(2,1)S(1)}, u32[]{:S(2)}, u32[]{:S(2)}) %collective-permute-start.121) | collective-permute-done | bytes 327712 | tf_op jit(solution)/shard_map/ppermute | solution.py:29
  499.2 5.3 collective-permute-done.129.rest_3_
  504.5 5.2 down_products.11
  509.7 10.4 %collective-permute-start.130 = (bf16[4,640,128]{2,1,0:T(8,128)(2,1)}, bf16[4,640,128]{2,1,0:T(8,128)(2,1)S(1)}, u32[]{:S(2)}, u32[]{:S(2)}) collective-permute-start(bf16[4,640,128]{2,1,0:T(8,128)(2,1)} %get-tuple-element.502), channel_id=1, source_target_pairs={{0,1},{1,0},{2,3},{3,2},{4,5},{5,4},{6,7},{7,6},{8,9},{9,8},{10,11... | collective-permute-start | bytes 1966088 | tf_op jit(solution)/shard_map/ppermute | solution.py:33
  520.1 5.7 down_products.9
  529.3 5.7 %down_products.10 = (bf16[640,128]{1,0:T(8,128)(2,1)}, bf16[640,128]{1,0:T(8,128)(2,1)}, bf16[640,128]{1,0:T(8,128)(2,1)}, bf16[640,128]{1,0:T(8,128)(2,1)}, bf16[4,640,128]{2,1,0:T(8,128)(2,1)}) custom-call(s32[21]{0:T(128)} %stack.231.where_ref, bf16[4,40,1152]{2,1,0:T(8,128)(2,1)} %copy-done.22, bf16[4,40,1152]{2,1,0:T(8,128)(2,1)} %copy-done.62, ...), custom_call_target="tpu_custom_call" | custom-call | flops 1509949440 | bytes 5144576 | tf_op jit(solution)/shard_map/down_products/pallas_call | solution.py:230
  539.5 3.3 collective-permute-start.132
  545.0 3.1 collective-permute-start.137
  551.4 2.9 collective-permute-done.135
  554.8 16.3 %all_to_all.10 = bf16[16,72,128]{2,1,0:T(8,128)(2,1)S(1)} all-to-all(bf16[16,72,128]{2,1,0:T(8,128)(2,1)S(1)} %pad_maximum_fusion.8), channel_id=1, replica_groups=mesh['y'=4,'xl'=2,'xh'=2,'z'=4,'c'=2] {'xh','z','c'}, dimensions={0} | all-to-all | bytes 589824 | tf_op jit(solution)/shard_map/all_to_all | solution.py:403
  (490 shorter events, 189.4 us)
Async XLA Ops:
  7.4 22.7 %collective-permute-start = (bf16[2,2,128,1152]{3,2,1,0:T(8,128)(2,1)}, bf16[2,2,128,1152]{3,2,1,0:T(8,128)(2,1)S(1)}, u32[]{:S(2)}, u32[]{:S(2)}) collective-permute-start(bf16[2,2,128,1152]{3,2,1,0:T(8,128)(2,1)} %get-tuple-element.264), channel_id=1, source_target_pairs={{0,2},{2,4},{4,6},{6,0},{1,7},{3,1},{5,3},{7,5},{8,10},{10,12},{12... | collective-permute-start | bytes 3538952 | tf_op jit(solution)/shard_map/ppermute | solution.py:29
  18.6 16.0 %collective-permute-start.11 = (bf16[2,2,128,1152]{3,2,1,0:T(8,128)(2,1)}, bf16[2,2,128,1152]{3,2,1,0:T(8,128)(2,1)S(1)}, u32[]{:S(2)}, u32[]{:S(2)}) collective-permute-start(bf16[2,2,128,1152]{3,2,1,0:T(8,128)(2,1)} %get-tuple-element.290), channel_id=1, source_target_pairs={{0,16},{16,8},{8,24},{24,0},{1,25},{17,1},{9,17},{25,9},{2,18},{18... | collective-permute-start | bytes 3538952 | tf_op jit(solution)/shard_map/ppermute | solution.py:29
  21.2 23.0 %collective-permute-start.5 = (bf16[2,2,128,1152]{3,2,1,0:T(8,128)(2,1)}, bf16[2,2,128,1152]{3,2,1,0:T(8,128)(2,1)}, u32[]{:S(2)}, u32[]{:S(2)}) collective-permute-start(bf16[2,2,128,1152]{3,2,1,0:T(8,128)(2,1)} %get-tuple-element.275), channel_id=1, source_target_pairs={{0,6},{2,0},{4,2},{6,4},{1,3},{3,5},{5,7},{7,1},{8,14},{10,8},{12,... | collective-permute-start | bytes 3538952 | tf_op jit(solution)/shard_map/ppermute | solution.py:29
  27.4 14.9 %collective-permute-start.18 = (bf16[2,2,128,1024]{3,2,1,0:T(8,128)(2,1)}, bf16[2,2,128,1024]{3,2,1,0:T(8,128)(2,1)S(1)}, u32[]{:S(2)}, u32[]{:S(2)}) collective-permute-start(bf16[2,2,128,1024]{3,2,1,0:T(8,128)(2,1)} %get-tuple-element.307), channel_id=1, source_target_pairs={{0,32},{32,64},{64,96},{96,0},{1,97},{33,1},{65,33},{97,65},{2,34}... | collective-permute-start | bytes 3145736 | tf_op jit(solution)/shard_map/ppermute | solution.py:29
  30.2 36.4 %collective-permute-start.6 = (bf16[2,2,128,1152]{3,2,1,0:T(8,128)(2,1)}, bf16[2,2,128,1152]{3,2,1,0:T(8,128)(2,1)}, u32[]{:S(2)}, u32[]{:S(2)}) collective-permute-start(bf16[2,2,128,1152]{3,2,1,0:T(8,128)(2,1)} %get-tuple-element.278), channel_id=1, source_target_pairs={{0,4},{2,6},{4,0},{6,2},{1,5},{3,7},{5,1},{7,3},{8,12},{10,14},{12... | collective-permute-start | bytes 3538952 | tf_op jit(solution)/shard_map/ppermute | solution.py:29
  31.5 54.1 %collective-permute-start.12 = (bf16[2,2,128,1152]{3,2,1,0:T(8,128)(2,1)}, bf16[2,2,128,1152]{3,2,1,0:T(8,128)(2,1)}, u32[]{:S(2)}, u32[]{:S(2)}) collective-permute-start(bf16[2,2,128,1152]{3,2,1,0:T(8,128)(2,1)} %get-tuple-element.293), channel_id=1, source_target_pairs={{0,24},{16,0},{8,16},{24,8},{1,17},{17,9},{9,25},{25,1},{2,26},{18... | collective-permute-start | bytes 3538952 | tf_op jit(solution)/shard_map/ppermute | solution.py:29
  34.6 51.0 %collective-permute-start.13 = (bf16[2,2,128,1152]{3,2,1,0:T(8,128)(2,1)}, bf16[2,2,128,1152]{3,2,1,0:T(8,128)(2,1)}, u32[]{:S(2)}, u32[]{:S(2)}) collective-permute-start(bf16[2,2,128,1152]{3,2,1,0:T(8,128)(2,1)} %get-tuple-element.296), channel_id=1, source_target_pairs={{0,8},{16,24},{8,0},{24,16},{1,9},{17,25},{9,1},{25,17},{2,10},{18... | collective-permute-start | bytes 3538952 | tf_op jit(solution)/shard_map/ppermute | solution.py:29
  42.2 53.4 %collective-permute-start.19 = (bf16[2,2,128,1024]{3,2,1,0:T(8,128)(2,1)}, bf16[2,2,128,1024]{3,2,1,0:T(8,128)(2,1)}, u32[]{:S(2)}, u32[]{:S(2)}) collective-permute-start(bf16[2,2,128,1024]{3,2,1,0:T(8,128)(2,1)} %get-tuple-element.310), channel_id=1, source_target_pairs={{0,96},{32,0},{64,32},{96,64},{1,33},{33,65},{65,97},{97,1},{2,98}... | collective-permute-start | bytes 3145736 | tf_op jit(solution)/shard_map/ppermute | solution.py:29
  44.2 51.5 %collective-permute-start.20 = (bf16[2,2,128,1024]{3,2,1,0:T(8,128)(2,1)}, bf16[2,2,128,1024]{3,2,1,0:T(8,128)(2,1)}, u32[]{:S(2)}, u32[]{:S(2)}) collective-permute-start(bf16[2,2,128,1024]{3,2,1,0:T(8,128)(2,1)} %get-tuple-element.313), channel_id=1, source_target_pairs={{0,64},{32,96},{64,0},{96,32},{1,65},{33,97},{65,1},{97,33},{2,66}... | collective-permute-start | bytes 3145736 | tf_op jit(solution)/shard_map/ppermute | solution.py:29
  69.4 56.7 %collective-permute-start.7 = (bf16[4,2,128,1152]{3,2,1,0:T(8,128)(2,1)}, bf16[4,2,128,1152]{3,2,1,0:T(8,128)(2,1)}, u32[]{:S(2)}, u32[]{:S(2)}) collective-permute-start(bf16[4,2,128,1152]{3,2,1,0:T(8,128)(2,1)} %other_halves.6), channel_id=1, source_target_pairs={{0,1},{1,0},{2,3},{3,2},{4,5},{5,4},{6,7},{7,6},{8,9},{9,8},{10,11... | collective-permute-start | bytes 7077896 | tf_op jit(solution)/shard_map/ppermute | solution.py:33
  74.4 16.4 %all-to-all-start = ((bf16[16,72,128]{2,1,0:T(8,128)(2,1)}), bf16[16,72,128]{2,1,0:T(8,128)(2,1)S(1)}, u32[]{:S(2)}, u32[]{:S(2)}) async-start(bf16[16,72,128]{2,1,0:T(8,128)(2,1)} %bitcast_bitcast_fusion), calls=%async_computation | async-start | bytes 589824 | tf_op jit(solution)/shard_map/all_to_all | solution.py:381
  88.4 45.4 %collective-permute-start.14 = (bf16[4,2,128,1152]{3,2,1,0:T(8,128)(2,1)}, bf16[4,2,128,1152]{3,2,1,0:T(8,128)(2,1)}, u32[]{:S(2)}, u32[]{:S(2)}) collective-permute-start(bf16[4,2,128,1152]{3,2,1,0:T(8,128)(2,1)} %other_halves.7), channel_id=1, source_target_pairs={{0,1},{1,0},{2,3},{3,2},{4,5},{5,4},{6,7},{7,6},{8,9},{9,8},{10,11... | collective-permute-start | bytes 7077896 | tf_op jit(solution)/shard_map/ppermute | solution.py:33
  98.3 46.4 %collective-permute-start.21 = (bf16[4,2,128,1024]{3,2,1,0:T(8,128)(2,1)}, bf16[4,2,128,1024]{3,2,1,0:T(8,128)(2,1)}, u32[]{:S(2)}, u32[]{:S(2)}) collective-permute-start(bf16[4,2,128,1024]{3,2,1,0:T(8,128)(2,1)} %other_halves.8), channel_id=1, source_target_pairs={{0,1},{1,0},{2,3},{3,2},{4,5},{5,4},{6,7},{7,6},{8,9},{9,8},{10,11... | collective-permute-start | bytes 6291464 | tf_op jit(solution)/shard_map/ppermute | solution.py:33
  125.1 19.6 %collective-permute-start.17 = (bf16[2,640,128]{2,1,0:T(8,128)(2,1)S(1)}, bf16[2,640,128]{2,1,0:T(8,128)(2,1)S(1)}, u32[]{:S(2)}, u32[]{:S(2)}) collective-permute-start(bf16[2,640,128]{2,1,0:T(8,128)(2,1)S(1)} %pad_maximum_fusion.4.rest_0_), channel_id=1, source_target_pairs={{0,64},{32,96},{64,0},{96,32},{1,65},{33,97},{65,1},{97,33},{2,66}... | collective-permute-start | bytes 983048 | tf_op jit(solution)/shard_map/ppermute | solution.py:29
  133.7 35.8 %collective-permute-start.22 = (bf16[2,160,1152]{2,1,0:T(8,128)(2,1)}, bf16[2,160,1152]{2,1,0:T(8,128)(2,1)S(1)}, u32[]{:S(2)}, u32[]{:S(2)}) collective-permute-start(bf16[2,160,1152]{2,1,0:T(8,128)(2,1)} %get-tuple-element.281), channel_id=1, source_target_pairs={{0,16},{16,8},{8,24},{24,0},{1,25},{17,1},{9,17},{25,9},{2,18},{18... | collective-permute-start | bytes 2211848 | tf_op jit(solution)/shard_map/ppermute | solution.py:29
  142.0 27.5 %collective-permute-start.23 = (bf16[2,160,1152]{2,1,0:T(8,128)(2,1)}, bf16[2,160,1152]{2,1,0:T(8,128)(2,1)S(1)}, u32[]{:S(2)}, u32[]{:S(2)}) collective-permute-start(bf16[2,160,1152]{2,1,0:T(8,128)(2,1)} %get-tuple-element.298), channel_id=1, source_target_pairs={{0,32},{32,64},{64,96},{96,0},{1,97},{33,1},{65,33},{97,65},{2,34}... | collective-permute-start | bytes 2211848 | tf_op jit(solution)/shard_map/ppermute | solution.py:29
  152.1 17.4 %collective-permute-start.24 = (bf16[2,160,1024]{2,1,0:T(8,128)(2,1)}, bf16[2,160,1024]{2,1,0:T(8,128)(2,1)S(1)}, u32[]{:S(2)}, u32[]{:S(2)}) collective-permute-start(bf16[2,160,1024]{2,1,0:T(8,128)(2,1)} %get-tuple-element.315), channel_id=1, source_target_pairs={{0,2},{2,4},{4,6},{6,0},{1,7},{3,1},{5,3},{7,5},{8,10},{10,12},{12... | collective-permute-start | bytes 1966088 | tf_op jit(solution)/shard_map/ppermute | solution.py:29
  157.1 17.4 %collective-permute-start.29 = (bf16[2,160,1024]{2,1,0:T(8,128)(2,1)}, bf16[2,160,1024]{2,1,0:T(8,128)(2,1)}, u32[]{:S(2)}, u32[]{:S(2)}) collective-permute-start(bf16[2,160,1024]{2,1,0:T(8,128)(2,1)} %get-tuple-element.337), channel_id=1, source_target_pairs={{0,6},{2,0},{4,2},{6,4},{1,3},{3,5},{5,7},{7,1},{8,14},{10,8},{12,... | collective-permute-start | bytes 1966088 | tf_op jit(solution)/shard_map/ppermute | solution.py:29
  157.1 17.4 %collective-permute-start.25 = (bf16[2,160,1152]{2,1,0:T(8,128)(2,1)}, bf16[2,160,1152]{2,1,0:T(8,128)(2,1)}, u32[]{:S(2)}, u32[]{:S(2)}) collective-permute-start(bf16[2,160,1152]{2,1,0:T(8,128)(2,1)} %get-tuple-element.322), channel_id=1, source_target_pairs={{0,24},{16,0},{8,16},{24,8},{1,17},{17,9},{9,25},{25,1},{2,26},{18... | collective-permute-start | bytes 2211848 | tf_op jit(solution)/shard_map/ppermute | solution.py:29
  169.5 14.7 %collective-permute-start.26 = (bf16[2,160,1152]{2,1,0:T(8,128)(2,1)}, bf16[2,160,1152]{2,1,0:T(8,128)(2,1)}, u32[]{:S(2)}, u32[]{:S(2)}) collective-permute-start(bf16[2,160,1152]{2,1,0:T(8,128)(2,1)} %get-tuple-element.323), channel_id=1, source_target_pairs={{0,8},{16,24},{8,0},{24,16},{1,9},{17,25},{9,1},{25,17},{2,10},{18... | collective-permute-start | bytes 2211848 | tf_op jit(solution)/shard_map/ppermute | solution.py:29
  170.4 29.4 %collective-permute-start.27 = (bf16[2,160,1152]{2,1,0:T(8,128)(2,1)}, bf16[2,160,1152]{2,1,0:T(8,128)(2,1)S(1)}, u32[]{:S(2)}, u32[]{:S(2)}) collective-permute-start(bf16[2,160,1152]{2,1,0:T(8,128)(2,1)} %get-tuple-element.330), channel_id=1, source_target_pairs={{0,96},{32,0},{64,32},{96,64},{1,33},{33,65},{65,97},{97,1},{2,98}... | collective-permute-start | bytes 2211848 | tf_op jit(solution)/shard_map/ppermute | solution.py:29
  170.4 34.1 %collective-permute-start.28 = (bf16[2,160,1152]{2,1,0:T(8,128)(2,1)}, bf16[2,160,1152]{2,1,0:T(8,128)(2,1)S(1)}, u32[]{:S(2)}, u32[]{:S(2)}) collective-permute-start(bf16[2,160,1152]{2,1,0:T(8,128)(2,1)} %get-tuple-element.331), channel_id=1, source_target_pairs={{0,64},{32,96},{64,0},{96,32},{1,65},{33,97},{65,1},{97,33},{2,66}... | collective-permute-start | bytes 2211848 | tf_op jit(solution)/shard_map/ppermute | solution.py:29
  174.5 37.3 %collective-permute-start.54 = (bf16[2,1152,128]{2,1,0:T(8,128)(2,1)}, bf16[2,1152,128]{2,1,0:T(8,128)(2,1)}, u32[]{:S(2)}, u32[]{:S(2)}) collective-permute-start(bf16[2,1152,128]{2,1,0:T(8,128)(2,1)} %get-tuple-element.376), channel_id=1, source_target_pairs={{0,2},{2,4},{4,6},{6,0},{1,7},{3,1},{5,3},{7,5},{8,10},{10,12},{12... | collective-permute-start | bytes 1769480 | tf_op jit(solution)/shard_map/ppermute | solution.py:29
  184.2 23.9 %collective-permute-start.68 = (bf16[2,1024,128]{2,1,0:T(8,128)(2,1)}, bf16[2,1024,128]{2,1,0:T(8,128)(2,1)}, u32[]{:S(2)}, u32[]{:S(2)}) collective-permute-start(bf16[2,1024,128]{2,1,0:T(8,128)(2,1)} %get-tuple-element.398), channel_id=1, source_target_pairs={{0,32},{32,64},{64,96},{96,0},{1,97},{33,1},{65,33},{97,65},{2,34}... | collective-permute-start | bytes 1572872 | tf_op jit(solution)/shard_map/ppermute | solution.py:29
  188.2 25.5 %collective-permute-start.31 = (bf16[2,40,1152]{2,1,0:T(8,128)(2,1)}, bf16[2,40,1152]{2,1,0:T(8,128)(2,1)S(1)}, u32[]{:S(2)}, u32[]{:S(2)}) collective-permute-start(bf16[2,40,1152]{2,1,0:T(8,128)(2,1)} %get-tuple-element.325), channel_id=1, source_target_pairs={{0,32},{32,64},{64,96},{96,0},{1,97},{33,1},{65,33},{97,65},{2,34}... | collective-permute-start | bytes 552968 | tf_op jit(solution)/shard_map/ppermute | solution.py:29
  204.4 24.4 %collective-permute-start.61 = (bf16[2,1152,128]{2,1,0:T(8,128)(2,1)}, bf16[2,1152,128]{2,1,0:T(8,128)(2,1)S(1)}, u32[]{:S(2)}, u32[]{:S(2)}) collective-permute-start(bf16[2,1152,128]{2,1,0:T(8,128)(2,1)} %get-tuple-element.387), channel_id=1, source_target_pairs={{0,16},{16,8},{8,24},{24,0},{1,25},{17,1},{9,17},{25,9},{2,18},{18... | collective-permute-start | bytes 1769480 | tf_op jit(solution)/shard_map/ppermute | solution.py:29
  208.1 20.7 %collective-permute-start.32 = (bf16[2,40,1152]{2,1,0:T(8,128)(2,1)}, bf16[2,40,1152]{2,1,0:T(8,128)(2,1)S(1)}, u32[]{:S(2)}, u32[]{:S(2)}) collective-permute-start(bf16[2,40,1152]{2,1,0:T(8,128)(2,1)} %get-tuple-element.332), channel_id=1, source_target_pairs={{0,2},{2,4},{4,6},{6,0},{1,7},{3,1},{5,3},{7,5},{8,10},{10,12},{12... | collective-permute-start | bytes 552968 | tf_op jit(solution)/shard_map/ppermute | solution.py:29
  211.9 17.0 %collective-permute-start.70 = (bf16[2,1024,128]{2,1,0:T(8,128)(2,1)}, bf16[2,1024,128]{2,1,0:T(8,128)(2,1)S(1)}, u32[]{:S(2)}, u32[]{:S(2)}) collective-permute-start(bf16[2,1024,128]{2,1,0:T(8,128)(2,1)} %get-tuple-element.401), channel_id=1, source_target_pairs={{0,64},{32,96},{64,0},{96,32},{1,65},{33,97},{65,1},{97,33},{2,66}... | collective-permute-start | bytes 1572872 | tf_op jit(solution)/shard_map/ppermute | solution.py:29
  213.7 27.5 %collective-permute-start.56 = (bf16[2,1152,128]{2,1,0:T(8,128)(2,1)}, bf16[2,1152,128]{2,1,0:T(8,128)(2,1)S(1)}, u32[]{:S(2)}, u32[]{:S(2)}) collective-permute-start(bf16[2,1152,128]{2,1,0:T(8,128)(2,1)} %get-tuple-element.379), channel_id=1, source_target_pairs={{0,4},{2,6},{4,0},{6,2},{1,5},{3,7},{5,1},{7,3},{8,12},{10,14},{12... | collective-permute-start | bytes 1769480 | tf_op jit(solution)/shard_map/ppermute | solution.py:29
  213.7 27.5 %collective-permute-start.55 = (bf16[2,1152,128]{2,1,0:T(8,128)(2,1)}, bf16[2,1152,128]{2,1,0:T(8,128)(2,1)S(1)}, u32[]{:S(2)}, u32[]{:S(2)}) collective-permute-start(bf16[2,1152,128]{2,1,0:T(8,128)(2,1)} %get-tuple-element.378), channel_id=1, source_target_pairs={{0,6},{2,0},{4,2},{6,4},{1,3},{3,5},{5,7},{7,1},{8,14},{10,8},{12,... | collective-permute-start | bytes 1769480 | tf_op jit(solution)/shard_map/ppermute | solution.py:29
  228.8 15.9 %collective-permute-start.38 = (bf16[2,40,1024]{2,1,0:T(8,128)(2,1)}, bf16[2,40,1024]{2,1,0:T(8,128)(2,1)S(1)}, u32[]{:S(2)}, u32[]{:S(2)}) collective-permute-start(bf16[2,40,1024]{2,1,0:T(8,128)(2,1)} %get-tuple-element.354), channel_id=1, source_target_pairs={{0,24},{16,0},{8,16},{24,8},{1,17},{17,9},{9,25},{25,1},{2,26},{18... | collective-permute-start | bytes 491528 | tf_op jit(solution)/shard_map/ppermute | solution.py:29
  228.9 15.9 %collective-permute-start.39 = (bf16[2,40,1024]{2,1,0:T(8,128)(2,1)}, bf16[2,40,1024]{2,1,0:T(8,128)(2,1)S(1)}, u32[]{:S(2)}, u32[]{:S(2)}) collective-permute-start(bf16[2,40,1024]{2,1,0:T(8,128)(2,1)} %get-tuple-element.355), channel_id=1, source_target_pairs={{0,8},{16,24},{8,0},{24,16},{1,9},{17,25},{9,1},{25,17},{2,10},{18... | collective-permute-start | bytes 491528 | tf_op jit(solution)/shard_map/ppermute | solution.py:29
  239.1 29.8 %collective-permute-start.63 = (bf16[2,1152,128]{2,1,0:T(8,128)(2,1)}, bf16[2,1152,128]{2,1,0:T(8,128)(2,1)S(1)}, u32[]{:S(2)}, u32[]{:S(2)}) collective-permute-start(bf16[2,1152,128]{2,1,0:T(8,128)(2,1)} %get-tuple-element.390), channel_id=1, source_target_pairs={{0,8},{16,24},{8,0},{24,16},{1,9},{17,25},{9,1},{25,17},{2,10},{18... | collective-permute-start | bytes 1769480 | tf_op jit(solution)/shard_map/ppermute | solution.py:29
  244.5 49.3 %collective-permute-start.57 = (bf16[4,1152,128]{2,1,0:T(8,128)(2,1)}, bf16[4,1152,128]{2,1,0:T(8,128)(2,1)}, u32[]{:S(2)}, u32[]{:S(2)}) collective-permute-start(bf16[4,1152,128]{2,1,0:T(8,128)(2,1)} %other_halves.9), channel_id=1, source_target_pairs={{0,1},{1,0},{2,3},{3,2},{4,5},{5,4},{6,7},{7,6},{8,9},{9,8},{10,11... | collective-permute-start | bytes 3538952 | tf_op jit(solution)/shard_map/ppermute | solution.py:33
  268.9 17.7 %collective-permute-start.62 = (bf16[2,1152,128]{2,1,0:T(8,128)(2,1)S(1)}, bf16[2,1152,128]{2,1,0:T(8,128)(2,1)S(1)}, u32[]{:S(2)}, u32[]{:S(2)}) collective-permute-start(bf16[2,1152,128]{2,1,0:T(8,128)(2,1)S(1)} %copy-done.61), channel_id=1, source_target_pairs={{0,24},{16,0},{8,16},{24,8},{1,17},{17,9},{9,25},{25,1},{2,26},{18... | collective-permute-start | bytes 1769480 | tf_op jit(solution)/shard_map/ppermute | solution.py:29
  270.6 23.1 %collective-permute-start.71 = (bf16[4,1024,128]{2,1,0:T(8,128)(2,1)S(1)}, bf16[4,1024,128]{2,1,0:T(8,128)(2,1)}, u32[]{:S(2)}, u32[]{:S(2)}) collective-permute-start(bf16[4,1024,128]{2,1,0:T(8,128)(2,1)S(1)} %copy-done.2), channel_id=1, source_target_pairs={{0,1},{1,0},{2,3},{3,2},{4,5},{5,4},{6,7},{7,6},{8,9},{9,8},{10,11... | collective-permute-start | bytes 3145736 | tf_op jit(solution)/shard_map/ppermute | solution.py:33
  289.7 34.9 %collective-permute-start.64 = (bf16[4,1152,128]{2,1,0:T(8,128)(2,1)}, bf16[4,1152,128]{2,1,0:T(8,128)(2,1)S(1)}, u32[]{:S(2)}, u32[]{:S(2)}) collective-permute-start(bf16[4,1152,128]{2,1,0:T(8,128)(2,1)} %other_halves.10), channel_id=1, source_target_pairs={{0,1},{1,0},{2,3},{3,2},{4,5},{5,4},{6,7},{7,6},{8,9},{9,8},{10,11... | collective-permute-start | bytes 3538952 | tf_op jit(solution)/shard_map/ppermute | solution.py:33
  293.7 21.1 %collective-permute-start.52 = (bf16[4,40,1152]{2,1,0:T(8,128)(2,1)}, bf16[4,40,1152]{2,1,0:T(8,128)(2,1)S(1)}, u32[]{:S(2)}, u32[]{:S(2)}) collective-permute-start(bf16[4,40,1152]{2,1,0:T(8,128)(2,1)} %pad_maximum_fusion.rest_0_), channel_id=1, source_target_pairs={{0,24},{16,0},{8,16},{24,8},{1,17},{17,9},{9,25},{25,1},{2,26},{18... | collective-permute-start | bytes 1105928 | tf_op jit(solution)/shard_map/ppermute | solution.py:29
  293.8 23.6 %collective-permute-start.53 = (bf16[4,40,1152]{2,1,0:T(8,128)(2,1)}, bf16[4,40,1152]{2,1,0:T(8,128)(2,1)S(1)}, u32[]{:S(2)}, u32[]{:S(2)}) collective-permute-start(bf16[4,40,1152]{2,1,0:T(8,128)(2,1)} %pad_maximum_fusion.rest_0_), channel_id=1, source_target_pairs={{0,8},{16,24},{8,0},{24,16},{1,9},{17,25},{9,1},{25,17},{2,10},{18... | collective-permute-start | bytes 1105928 | tf_op jit(solution)/shard_map/ppermute | solution.py:29
  306.0 18.6 %collective-permute-start.59 = (bf16[4,40,1152]{2,1,0:T(8,128)(2,1)S(1)}, bf16[4,40,1152]{2,1,0:T(8,128)(2,1)}, u32[]{:S(2)}, u32[]{:S(2)}) collective-permute-start(bf16[4,40,1152]{2,1,0:T(8,128)(2,1)S(1)} %pad_maximum_fusion.1.rest_0_), channel_id=1, source_target_pairs={{0,96},{32,0},{64,32},{96,64},{1,33},{33,65},{65,97},{97,1},{2,98}... | collective-permute-start | bytes 1105928 | tf_op jit(solution)/shard_map/ppermute | solution.py:29
  308.5 16.1 %collective-permute-start.60 = (bf16[4,40,1152]{2,1,0:T(8,128)(2,1)S(1)}, bf16[4,40,1152]{2,1,0:T(8,128)(2,1)}, u32[]{:S(2)}, u32[]{:S(2)}) collective-permute-start(bf16[4,40,1152]{2,1,0:T(8,128)(2,1)S(1)} %pad_maximum_fusion.1.rest_0_), channel_id=1, source_target_pairs={{0,64},{32,96},{64,0},{96,32},{1,65},{33,97},{65,1},{97,33},{2,66}... | collective-permute-start | bytes 1105928 | tf_op jit(solution)/shard_map/ppermute | solution.py:29
  314.9 16.6 %collective-permute-start.72 = (bf16[4,640,128]{2,1,0:T(8,128)(2,1)}, bf16[4,640,128]{2,1,0:T(8,128)(2,1)S(1)}, u32[]{:S(2)}, u32[]{:S(2)}) collective-permute-start(bf16[4,640,128]{2,1,0:T(8,128)(2,1)} %get-tuple-element.403), channel_id=1, source_target_pairs={{0,1},{1,0},{2,3},{3,2},{4,5},{5,4},{6,7},{7,6},{8,9},{9,8},{10,11... | collective-permute-start | bytes 1966088 | tf_op jit(solution)/shard_map/ppermute | solution.py:33
  355.6 17.4 %collective-permute-start.84 = (bf16[2,640,128]{2,1,0:T(8,128)(2,1)S(1)}, bf16[2,640,128]{2,1,0:T(8,128)(2,1)S(1)}, u32[]{:S(2)}, u32[]{:S(2)}) collective-permute-start(bf16[2,640,128]{2,1,0:T(8,128)(2,1)S(1)} %pad_maximum_fusion.6.rest_0_), channel_id=1, source_target_pairs={{0,6},{2,0},{4,2},{6,4},{1,3},{3,5},{5,7},{7,1},{8,14},{10,8},{12,... | collective-permute-start | bytes 983048 | tf_op jit(solution)/shard_map/ppermute | solution.py:29
  355.6 18.2 %collective-permute-start.85 = (bf16[2,640,128]{2,1,0:T(8,128)(2,1)S(1)}, bf16[2,640,128]{2,1,0:T(8,128)(2,1)S(1)}, u32[]{:S(2)}, u32[]{:S(2)}) collective-permute-start(bf16[2,640,128]{2,1,0:T(8,128)(2,1)S(1)} %pad_maximum_fusion.6.rest_0_), channel_id=1, source_target_pairs={{0,4},{2,6},{4,0},{6,2},{1,5},{3,7},{5,1},{7,3},{8,12},{10,14},{12... | collective-permute-start | bytes 983048 | tf_op jit(solution)/shard_map/ppermute | solution.py:29
  357.2 17.2 %collective-permute-start.86 = (bf16[2,640,128]{2,1,0:T(8,128)(2,1)S(1)}, bf16[2,640,128]{2,1,0:T(8,128)(2,1)S(1)}, u32[]{:S(2)}, u32[]{:S(2)}) collective-permute-start(bf16[2,640,128]{2,1,0:T(8,128)(2,1)S(1)} %pad_maximum_fusion.6.rest_0_), channel_id=1, source_target_pairs={{0,16},{16,8},{8,24},{24,0},{1,25},{17,1},{9,17},{25,9},{2,18},{18... | collective-permute-start | bytes 983048 | tf_op jit(solution)/shard_map/ppermute | solution.py:29
  358.6 25.2 %collective-permute-start.87 = (bf16[2,640,128]{2,1,0:T(8,128)(2,1)S(1)}, bf16[2,640,128]{2,1,0:T(8,128)(2,1)S(1)}, u32[]{:S(2)}, u32[]{:S(2)}) collective-permute-start(bf16[2,640,128]{2,1,0:T(8,128)(2,1)S(1)} %pad_maximum_fusion.6.rest_0_), channel_id=1, source_target_pairs={{0,24},{16,0},{8,16},{24,8},{1,17},{17,9},{9,25},{25,1},{2,26},{18... | collective-permute-start | bytes 983048 | tf_op jit(solution)/shard_map/ppermute | solution.py:29
  363.0 22.0 %collective-permute-start.88 = (bf16[2,640,128]{2,1,0:T(8,128)(2,1)S(1)}, bf16[2,640,128]{2,1,0:T(8,128)(2,1)S(1)}, u32[]{:S(2)}, u32[]{:S(2)}) collective-permute-start(bf16[2,640,128]{2,1,0:T(8,128)(2,1)S(1)} %pad_maximum_fusion.6.rest_0_), channel_id=1, source_target_pairs={{0,8},{16,24},{8,0},{24,16},{1,9},{17,25},{9,1},{25,17},{2,10},{18... | collective-permute-start | bytes 983048 | tf_op jit(solution)/shard_map/ppermute | solution.py:29
  373.0 22.3 %collective-permute-start.89 = (bf16[2,640,128]{2,1,0:T(8,128)(2,1)S(1)}, bf16[2,640,128]{2,1,0:T(8,128)(2,1)S(1)}, u32[]{:S(2)}, u32[]{:S(2)}) collective-permute-start(bf16[2,640,128]{2,1,0:T(8,128)(2,1)S(1)} %pad_maximum_fusion.6.rest_0_), channel_id=1, source_target_pairs={{0,32},{32,64},{64,96},{96,0},{1,97},{33,1},{65,33},{97,65},{2,34}... | collective-permute-start | bytes 983048 | tf_op jit(solution)/shard_map/ppermute | solution.py:29
  373.8 21.5 %collective-permute-start.90 = (bf16[2,640,128]{2,1,0:T(8,128)(2,1)S(1)}, bf16[2,640,128]{2,1,0:T(8,128)(2,1)S(1)}, u32[]{:S(2)}, u32[]{:S(2)}) collective-permute-start(bf16[2,640,128]{2,1,0:T(8,128)(2,1)S(1)} %pad_maximum_fusion.6.rest_0_), channel_id=1, source_target_pairs={{0,96},{32,0},{64,32},{96,64},{1,33},{33,65},{65,97},{97,1},{2,98}... | collective-permute-start | bytes 983048 | tf_op jit(solution)/shard_map/ppermute | solution.py:29
  374.4 20.9 %collective-permute-start.91 = (bf16[2,640,128]{2,1,0:T(8,128)(2,1)S(1)}, bf16[2,640,128]{2,1,0:T(8,128)(2,1)S(1)}, u32[]{:S(2)}, u32[]{:S(2)}) collective-permute-start(bf16[2,640,128]{2,1,0:T(8,128)(2,1)S(1)} %pad_maximum_fusion.6.rest_0_), channel_id=1, source_target_pairs={{0,64},{32,96},{64,0},{96,32},{1,65},{33,97},{65,1},{97,33},{2,66}... | collective-permute-start | bytes 983048 | tf_op jit(solution)/shard_map/ppermute | solution.py:29
  383.8 29.7 %collective-permute-start.92 = (bf16[2,160,1152]{2,1,0:T(8,128)(2,1)}, bf16[2,160,1152]{2,1,0:T(8,128)(2,1)S(1)}, u32[]{:S(2)}, u32[]{:S(2)}) collective-permute-start(bf16[2,160,1152]{2,1,0:T(8,128)(2,1)} %get-tuple-element.426), channel_id=1, source_target_pairs={{0,16},{16,8},{8,24},{24,0},{1,25},{17,1},{9,17},{25,9},{2,18},{18... | collective-permute-start | bytes 2211848 | tf_op jit(solution)/shard_map/ppermute | solution.py:29
  393.3 20.3 %collective-permute-start.93 = (bf16[2,160,1152]{2,1,0:T(8,128)(2,1)}, bf16[2,160,1152]{2,1,0:T(8,128)(2,1)S(1)}, u32[]{:S(2)}, u32[]{:S(2)}) collective-permute-start(bf16[2,160,1152]{2,1,0:T(8,128)(2,1)} %get-tuple-element.429), channel_id=1, source_target_pairs={{0,32},{32,64},{64,96},{96,0},{1,97},{33,1},{65,33},{97,65},{2,34}... | collective-permute-start | bytes 2211848 | tf_op jit(solution)/shard_map/ppermute | solution.py:29
  403.6 14.5 %collective-permute-start.95 = (bf16[2,160,1152]{2,1,0:T(8,128)(2,1)}, bf16[2,160,1152]{2,1,0:T(8,128)(2,1)S(1)}, u32[]{:S(2)}, u32[]{:S(2)}) collective-permute-start(bf16[2,160,1152]{2,1,0:T(8,128)(2,1)} %get-tuple-element.439), channel_id=1, source_target_pairs={{0,24},{16,0},{8,16},{24,8},{1,17},{17,9},{9,25},{25,1},{2,26},{18... | collective-permute-start | bytes 2211848 | tf_op jit(solution)/shard_map/ppermute | solution.py:29
  414.4 15.8 %collective-permute-start.96 = (bf16[2,160,1152]{2,1,0:T(8,128)(2,1)}, bf16[2,160,1152]{2,1,0:T(8,128)(2,1)}, u32[]{:S(2)}, u32[]{:S(2)}) collective-permute-start(bf16[2,160,1152]{2,1,0:T(8,128)(2,1)} %get-tuple-element.440), channel_id=1, source_target_pairs={{0,8},{16,24},{8,0},{24,16},{1,9},{17,25},{9,1},{25,17},{2,10},{18... | collective-permute-start | bytes 2211848 | tf_op jit(solution)/shard_map/ppermute | solution.py:29
  416.1 27.9 %collective-permute-start.97 = (bf16[2,160,1152]{2,1,0:T(8,128)(2,1)}, bf16[2,160,1152]{2,1,0:T(8,128)(2,1)S(1)}, u32[]{:S(2)}, u32[]{:S(2)}) collective-permute-start(bf16[2,160,1152]{2,1,0:T(8,128)(2,1)} %get-tuple-element.447), channel_id=1, source_target_pairs={{0,96},{32,0},{64,32},{96,64},{1,33},{33,65},{65,97},{97,1},{2,98}... | collective-permute-start | bytes 2211848 | tf_op jit(solution)/shard_map/ppermute | solution.py:29
  416.9 27.1 %collective-permute-start.98 = (bf16[2,160,1152]{2,1,0:T(8,128)(2,1)}, bf16[2,160,1152]{2,1,0:T(8,128)(2,1)S(1)}, u32[]{:S(2)}, u32[]{:S(2)}) collective-permute-start(bf16[2,160,1152]{2,1,0:T(8,128)(2,1)} %get-tuple-element.448), channel_id=1, source_target_pairs={{0,64},{32,96},{64,0},{96,32},{1,65},{33,97},{65,1},{97,33},{2,66}... | collective-permute-start | bytes 2211848 | tf_op jit(solution)/shard_map/ppermute | solution.py:29
  417.5 32.1 %collective-permute-start.99 = (bf16[2,160,1024]{2,1,0:T(8,128)(2,1)}, bf16[2,160,1024]{2,1,0:T(8,128)(2,1)}, u32[]{:S(2)}, u32[]{:S(2)}) collective-permute-start(bf16[2,160,1024]{2,1,0:T(8,128)(2,1)} %get-tuple-element.454), channel_id=1, source_target_pairs={{0,6},{2,0},{4,2},{6,4},{1,3},{3,5},{5,7},{7,1},{8,14},{10,8},{12,... | collective-permute-start | bytes 1966088 | tf_op jit(solution)/shard_map/ppermute | solution.py:29
  418.1 31.5 %collective-permute-start.100 = (bf16[2,160,1024]{2,1,0:T(8,128)(2,1)}, bf16[2,160,1024]{2,1,0:T(8,128)(2,1)}, u32[]{:S(2)}, u32[]{:S(2)}) collective-permute-start(bf16[2,160,1024]{2,1,0:T(8,128)(2,1)} %get-tuple-element.455), channel_id=1, source_target_pairs={{0,4},{2,6},{4,0},{6,2},{1,5},{3,7},{5,1},{7,3},{8,12},{10,14},{12... | collective-permute-start | bytes 1966088 | tf_op jit(solution)/shard_map/ppermute | solution.py:29
  433.1 24.1 %collective-permute-start.101 = (bf16[2,40,1152]{2,1,0:T(8,128)(2,1)}, bf16[2,40,1152]{2,1,0:T(8,128)(2,1)S(1)}, u32[]{:S(2)}, u32[]{:S(2)}) collective-permute-start(bf16[2,40,1152]{2,1,0:T(8,128)(2,1)} %get-tuple-element.442), channel_id=1, source_target_pairs={{0,32},{32,64},{64,96},{96,0},{1,97},{33,1},{65,33},{97,65},{2,34}... | collective-permute-start | bytes 552968 | tf_op jit(solution)/shard_map/ppermute | solution.py:29
  494.3 25.7 %collective-permute-start.122 = (bf16[4,40,1152]{2,1,0:T(8,128)(2,1)S(1)}, bf16[4,40,1152]{2,1,0:T(8,128)(2,1)}, u32[]{:S(2)}, u32[]{:S(2)}) collective-permute-start(bf16[4,40,1152]{2,1,0:T(8,128)(2,1)S(1)} %pad_maximum_fusion.2.rest_0_), channel_id=1, source_target_pairs={{0,24},{16,0},{8,16},{24,8},{1,17},{17,9},{9,25},{25,1},{2,26},{18... | collective-permute-start | bytes 1105928 | tf_op jit(solution)/shard_map/ppermute | solution.py:29
  494.4 25.6 %collective-permute-start.123 = (bf16[4,40,1152]{2,1,0:T(8,128)(2,1)S(1)}, bf16[4,40,1152]{2,1,0:T(8,128)(2,1)}, u32[]{:S(2)}, u32[]{:S(2)}) collective-permute-start(bf16[4,40,1152]{2,1,0:T(8,128)(2,1)S(1)} %pad_maximum_fusion.2.rest_0_), channel_id=1, source_target_pairs={{0,8},{16,24},{8,0},{24,16},{1,9},{17,25},{9,1},{25,17},{2,10},{18... | collective-permute-start | bytes 1105928 | tf_op jit(solution)/shard_map/ppermute | solution.py:29
  497.3 30.5 %collective-permute-start.125 = (bf16[4,40,1152]{2,1,0:T(8,128)(2,1)S(1)}, bf16[4,40,1152]{2,1,0:T(8,128)(2,1)S(1)}, u32[]{:S(2)}, u32[]{:S(2)}) collective-permute-start(bf16[4,40,1152]{2,1,0:T(8,128)(2,1)S(1)} %pad_maximum_fusion.3.rest_0_), channel_id=1, source_target_pairs={{0,96},{32,0},{64,32},{96,64},{1,33},{33,65},{65,97},{97,1},{2,98}... | collective-permute-start | bytes 1105928 | tf_op jit(solution)/shard_map/ppermute | solution.py:29
  497.7 30.1 %collective-permute-start.126 = (bf16[4,40,1152]{2,1,0:T(8,128)(2,1)S(1)}, bf16[4,40,1152]{2,1,0:T(8,128)(2,1)S(1)}, u32[]{:S(2)}, u32[]{:S(2)}) collective-permute-start(bf16[4,40,1152]{2,1,0:T(8,128)(2,1)S(1)} %pad_maximum_fusion.3.rest_0_), channel_id=1, source_target_pairs={{0,64},{32,96},{64,0},{96,32},{1,65},{33,97},{65,1},{97,33},{2,66}... | collective-permute-start | bytes 1105928 | tf_op jit(solution)/shard_map/ppermute | solution.py:29
  509.7 25.5 %collective-permute-start.130 = (bf16[4,640,128]{2,1,0:T(8,128)(2,1)}, bf16[4,640,128]{2,1,0:T(8,128)(2,1)S(1)}, u32[]{:S(2)}, u32[]{:S(2)}) collective-permute-start(bf16[4,640,128]{2,1,0:T(8,128)(2,1)} %get-tuple-element.502), channel_id=1, source_target_pairs={{0,1},{1,0},{2,3},{3,2},{4,5},{5,4},{6,7},{7,6},{8,9},{9,8},{10,11... | collective-permute-start | bytes 1966088 | tf_op jit(solution)/shard_map/ppermute | solution.py:33
  (173 other events, 1463.7 us)
